TPU v7x, 512 devices: a whole 4x8x8 slice. The times are simulated.
512 devices in a mesh: gx: 32 (over x_lo, z, core), gy: 8 (over y), gz: 2 (over x_hi).
Axes of the slice: x: 4 (x_hi: 2, x_lo: 2; x = x_hi * 2 + x_lo), y: 8, z: 8, core: 2. Of those that a mesh axis runs over, the one named last changes fastest.
Arguments:
- noisy_volume: float32 [256, 256, 256], P('gx', 'gy', 'gz'), may hold values from -8 to 8
- primal: float32 [256, 256, 256], P('gx', 'gy', 'gz'), may hold values from -6 to 6
- dual_field: float32 [3, 256, 256, 256], P(None, 'gx', 'gy', 'gz'), may hold values from -0.3 to 0.3
Outputs:
- denoised: float32 [256, 256, 256], P('gx', 'gy', 'gz')
- dual_final: float32 [3, 256, 256, 256], P(None, 'gx', 'gy', 'gz')
- residual_norms: float32 [2], replicated
All inputs are finite; a program needn't handle non-finite values.
Results may differ from a plain program's by a relative error of at most 0.0001.
Values sent between devices are 32-bit elements; how exact they have to be, the bound alone decides.
No kernel may reach another device: no remote copies, remote signals or barrier semaphores. Data moves between devices by JAX's collectives and lax.ppermute only.
A program may use at most 64 MiB of HBM per device.

v0:
```python
import jax
import jax.numpy as jnp
from jax import lax
from jax.sharding import PartitionSpec as P

ITERS = 2


step_primal = 0.25
step_dual = 0.3
radius_tv = 0.5


def extended(cells, sides, width):
    for axis, dim in sides:
        count = lax.axis_size(axis)
        ends = count - 1
        head = lax.slice_in_dim(cells, 0, width, axis=dim)
        tail = lax.slice_in_dim(cells, cells.shape[dim] - width, cells.shape[dim], axis=dim)
        cells = jnp.concatenate(
            [
                lax.ppermute(tail, axis, [(i, (i + 1) % count) for i in range(ends)]),
                cells,
                lax.ppermute(head, axis, [((i + 1) % count, i) for i in range(ends)]),
            ],
            axis=dim,
        )
    return cells


def advance(source, current, leading, dual_pad, anchor, extent):
    size_x, size_y, size_z = leading.shape
    centre_vals = leading[:-1, :-1, :-1]
    gradient = jnp.stack(
        [
            leading[1:, :-1, :-1] - centre_vals,
            leading[:-1, 1:, :-1] - centre_vals,
            leading[:-1, :-1, 1:] - centre_vals,
        ]
    )
    index_x = anchor[0] + jnp.arange(size_x - 1, dtype=jnp.int32)
    index_y = anchor[1] + jnp.arange(size_y - 1, dtype=jnp.int32)
    index_z = anchor[2] + jnp.arange(size_z - 1, dtype=jnp.int32)
    inside_x = ((index_x >= 0) & (index_x <= extent[0] - 2))[:, None, None]
    inside_y = ((index_y >= 0) & (index_y <= extent[1] - 2))[None, :, None]
    inside_z = ((index_z >= 0) & (index_z <= extent[2] - 2))[None, None, :]
    shape_out = centre_vals.shape
    inside_mask = jnp.stack(
        [
            jnp.broadcast_to(inside_x, shape_out),
            jnp.broadcast_to(inside_y, shape_out),
            jnp.broadcast_to(inside_z, shape_out),
        ]
    )
    gradient = jnp.where(inside_mask, gradient, 0.0)
    moved = dual_pad[:, :-1, :-1, :-1] + step_dual * gradient
    magnitude = jnp.sqrt(jnp.sum(moved * moved, axis=0))
    shrinkage = jnp.maximum(1.0, magnitude / radius_tv)
    projected = jnp.where(inside_mask, moved / shrinkage, 0.0)
    divergence = (
        projected[0, 1:, 1:, 1:]
        - projected[0, :-1, 1:, 1:]
        + projected[1, 1:, 1:, 1:]
        - projected[1, 1:, :-1, 1:]
        + projected[2, 1:, 1:, 1:]
        - projected[2, 1:, 1:, :-1]
    )
    updated = (current + step_primal * (divergence + source)) / (1.0 + step_primal)
    return (updated, 2.0 * updated - current, projected[:, 1:, 1:, 1:])


def settle(local_sum):
    return lax.psum(local_sum, ("gx", "gy", "gz"))


def on_device(noisy_volume, primal, dual_field):
    cells_x, cells_y, cells_z = noisy_volume.shape
    start_x = lax.axis_index("gx") * cells_x
    start_y = lax.axis_index("gy") * cells_y
    start_z = lax.axis_index("gz") * cells_z
    extent = (
        cells_x * lax.axis_size("gx"),
        cells_y * lax.axis_size("gy"),
        cells_z * lax.axis_size("gz"),
    )
    history = []
    current = primal
    leading = primal
    dual_now = dual_field
    for turn in range(ITERS):
        stacked = jnp.concatenate([leading[None], dual_now], axis=0)
        padded = extended(stacked, (("gx", 1), ("gy", 2), ("gz", 3)), 1)
        lead_pad = padded[0]
        dual_pad = padded[1:]
        updated, leading, dual_new = advance(
            noisy_volume,
            current,
            lead_pad,
            dual_pad,
            (start_x - 1, start_y - 1, start_z - 1),
            extent,
        )
        local_sum = (
            jnp.sum((updated - current) ** 2) / step_primal
            + jnp.sum((dual_new - dual_now) ** 2) / step_dual
        )
        history.append(settle(local_sum))
        current = updated
        dual_now = dual_new
    sums = jnp.stack(history)
    cells = float(extent[0] * extent[1] * extent[2])
    return (current, dual_now, jnp.sqrt(sums / cells))


def solution(mesh):
    placed = (P("gx", "gy", "gz"), P("gx", "gy", "gz"), P(None, "gx", "gy", "gz"))
    return jax.shard_map(
        on_device,
        mesh=mesh,
        in_specs=placed,
        out_specs=(P("gx", "gy", "gz"), P(None, "gx", "gy", "gz"), P()),
        check_vma=False,
    )
```

profile of v0, /device:TPU:1, one launch (start us, length us, event | category | flops | bytes accessed | tf_op | source)
XLA Modules:
  0.0 186.5 jit_solution(3227437164011335665)
XLA Ops:
  0.7 0.9 pad_maximum_fusion.17
  1.6 5.4 %collective-permute-start = (f32[4,1,32,128]{3,2,1,0:T(8,128)S(1)}, f32[4,1,32,128]{3,2,1,0:T(8,128)S(1)}, u32[]{:S(2)}, u32[]{:S(2)}) collective-permute-start(f32[4,1,32,128]{3,2,1,0:T(8,128)S(1)} %get-tuple-element.30), channel_id=1, source_target_pairs={{0,16},{16,32},{32,48},{48,64},{64,80},{80,96},{96,112},{112,128},... | collective-permute-start | bytes 196616 | tf_op jit(solution)/shard_map/ppermute | solution.py:22
  6.9 4.7 %collective-permute-start.1 = (f32[4,1,32,128]{3,2,1,0:T(8,128)S(1)}, f32[4,1,32,128]{3,2,1,0:T(8,128)S(1)}, u32[]{:S(2)}, u32[]{:S(2)}) collective-permute-start(f32[4,1,32,128]{3,2,1,0:T(8,128)S(1)} %get-tuple-element.31), channel_id=1, source_target_pairs={{16,0},{32,16},{48,32},{64,48},{80,64},{96,80},{112,96},{128,112},... | collective-permute-start | bytes 196616 | tf_op jit(solution)/shard_map/ppermute | solution.py:24
  11.7 0.9 collective-permute-done.1
  12.5 1.0 pad_maximum_fusion.25
  13.5 3.2 %collective-permute-start.2 = (f32[4,10,1,128]{3,2,1,0:T(1,128)S(1)}, f32[4,10,1,128]{3,2,1,0:T(1,128)S(1)}, u32[]{:S(2)}, u32[]{:S(2)}) collective-permute-start(f32[4,10,1,128]{3,2,1,0:T(1,128)S(1)} %get-tuple-element.26), channel_id=1, source_target_pairs={{0,2},{2,4},{4,6},{6,8},{8,10},{10,12},{12,14},{1,3},{3,5},{5,7},{... | collective-permute-start | bytes 61448 | tf_op jit(solution)/shard_map/ppermute | solution.py:22
  16.7 1.3 collective-permute-start.3
  18.1 3.2 %collective-permute-done.3 = f32[4,10,1,128]{3,2,1,0:T(1,128)S(1)} collective-permute-done((f32[4,10,1,128]{3,2,1,0:T(1,128)S(1)}, f32[4,10,1,128]{3,2,1,0:T(1,128)S(1)}, u32[]{:S(2)}, u32[]{:S(2)}) %collective-permute-start.3) | collective-permute-done | bytes 20512 | tf_op jit(solution)/shard_map/ppermute | solution.py:24
  22.4 1.3 collective-permute-start.5
  23.7 5.5 %collective-permute-start.4 = (f32[4,10,34,1]{2,0,3,1:T(4,128)S(1)}, f32[4,10,34,1]{2,0,3,1:T(4,128)S(1)}, u32[]{:S(2)}, u32[]{:S(2)}) collective-permute-start(f32[4,10,34,1]{2,0,3,1:T(4,128)S(1)} %copy.23), channel_id=1, source_target_pairs={{0,1},{2,3},{4,5},{6,7},{8,9},{10,11},{12,13},{14,15},{16,17},{18,... | collective-permute-start | bytes 16328 | tf_op jit(solution)/shard_map/ppermute | solution.py:22
  29.2 0.9 collective-permute-done.4
  31.6 0.6 multiply_reduce_fusion.1
  33.2 0.9 subtract_bitcast_fusion
  34.1 4.4 %collective-permute-start.6 = (f32[4,1,32,128]{3,2,1,0:T(8,128)S(1)}, f32[4,1,32,128]{3,2,1,0:T(8,128)S(1)}, u32[]{:S(2)}, u32[]{:S(2)}) collective-permute-start(f32[4,1,32,128]{3,2,1,0:T(8,128)S(1)} %get-tuple-element.28), channel_id=1, source_target_pairs={{0,16},{16,32},{32,48},{48,64},{64,80},{80,96},{96,112},{112,128},... | collective-permute-start | bytes 196616 | tf_op jit(solution)/shard_map/ppermute | solution.py:22
  38.6 1.9 %collective-permute-start.7 = (f32[4,1,32,128]{3,2,1,0:T(8,128)S(1)}, f32[4,1,32,128]{3,2,1,0:T(8,128)S(1)}, u32[]{:S(2)}, u32[]{:S(2)}) collective-permute-start(f32[4,1,32,128]{3,2,1,0:T(8,128)S(1)} %get-tuple-element.29), channel_id=1, source_target_pairs={{16,0},{32,16},{48,32},{64,48},{80,64},{96,80},{112,96},{128,112},... | collective-permute-start | bytes 196616 | tf_op jit(solution)/shard_map/ppermute | solution.py:24
  40.5 3.6 %collective-permute-done.7 = f32[4,1,32,128]{3,2,1,0:T(8,128)S(1)} collective-permute-done((f32[4,1,32,128]{3,2,1,0:T(8,128)S(1)}, f32[4,1,32,128]{3,2,1,0:T(8,128)S(1)}, u32[]{:S(2)}, u32[]{:S(2)}) %collective-permute-start.7) | collective-permute-done | bytes 65568 | tf_op jit(solution)/shard_map/ppermute | solution.py:24
  44.2 3.2 %collective-permute-start.8 = (f32[4,10,1,128]{3,2,1,0:T(1,128)S(1)}, f32[4,10,1,128]{3,2,1,0:T(1,128)S(1)}, u32[]{:S(2)}, u32[]{:S(2)}) collective-permute-start(f32[4,10,1,128]{3,2,1,0:T(1,128)S(1)} %get-tuple-element.24), channel_id=1, source_target_pairs={{0,2},{2,4},{4,6},{6,8},{8,10},{10,12},{12,14},{1,3},{3,5},{5,7},{... | collective-permute-start | bytes 61448 | tf_op jit(solution)/shard_map/ppermute | solution.py:22
  47.4 1.3 collective-permute-start.9
  48.7 3.8 %collective-permute-done.9 = f32[4,10,1,128]{3,2,1,0:T(1,128)S(1)} collective-permute-done((f32[4,10,1,128]{3,2,1,0:T(1,128)S(1)}, f32[4,10,1,128]{3,2,1,0:T(1,128)S(1)}, u32[]{:S(2)}, u32[]{:S(2)}) %collective-permute-start.9) | collective-permute-done | bytes 20512 | tf_op jit(solution)/shard_map/ppermute | solution.py:24
  52.5 0.6 copy-done.4
  53.3 1.2 fusion.40
  54.4 2.3 %copy.30 = f32[4,10,34,1]{2,1,3,0:T(8,128)} copy(f32[4,10,34,1]{3,2,1,0:T(8,128)} %get-tuple-element.21) | data formatting | bytes 10880 | tf_op jit(solution)/shard_map/slice | solution.py:18
  56.7 1.3 collective-permute-start.11
  58.0 1.0 copy.28
  59.0 6.7 %collective-permute-start.10 = (f32[4,10,34,1]{2,0,3,1:T(4,128)}, f32[4,10,34,1]{2,0,3,1:T(4,128)}, u32[]{:S(2)}, u32[]{:S(2)}) collective-permute-start(f32[4,10,34,1]{2,0,3,1:T(4,128)} %copy.28), channel_id=1, source_target_pairs={{0,1},{2,3},{4,5},{6,7},{8,9},{10,11},{12,13},{14,15},{16,17},{18,... | collective-permute-start | bytes 16328 | tf_op jit(solution)/shard_map/ppermute | solution.py:22
  65.7 2.1 %copy.32 = f32[4,10,34,1]{3,2,1,0:T(8,128)} copy(f32[4,10,34,1]{2,1,3,0:T(8,128)} %collective-permute-done.11) | data formatting | bytes 10880 | tf_op jit(solution)/shard_map/ppermute | solution.py:24
  67.7 1.1 copy.29
  68.9 1.2 fusion.11
  71.7 1.7 multiply_reduce_fusion.3
  74.7 1.6 multiply_reduce_fusion.5
  77.6 107.1 %all-reduce = (f32[1]{0:T(128)}, f32[1]{0:T(128)}) all-reduce(f32[1]{0:T(128)} %bitcast.13, f32[1]{0:T(128)} %bitcast.12), channel_id=1, replica_groups=mesh['gx'=32,'gy'=8,'gz'=2] {'gx','gy','gz'}, use_global_device_ids=true, to_apply=%region_7.8 | all-reduce | flops 2 | bytes 16 | tf_op jit(solution)/shard_map/psum | solution.py:73
  184.7 1.8 fusion.35
  (42 shorter events, 5.4 us)
Async XLA Ops:
  0.6 20.6 %copy-start = (f32[3,8,32,128]{3,2,1,0:T(8,128)S(1)}, f32[3,8,32,128]{3,2,1,0:T(8,128)}, u32[]{:S(2)}) copy-start(f32[3,8,32,128]{3,2,1,0:T(8,128)} %param.5) | copy-start | bytes 1179652
  0.6 20.6 %copy-start.1 = (f32[8,32,128]{2,1,0:T(8,128)S(1)}, f32[8,32,128]{2,1,0:T(8,128)}, u32[]{:S(2)}) copy-start(f32[8,32,128]{2,1,0:T(8,128)} %param.4) | copy-start | bytes 393220
  1.6 10.1 %collective-permute-start = (f32[4,1,32,128]{3,2,1,0:T(8,128)S(1)}, f32[4,1,32,128]{3,2,1,0:T(8,128)S(1)}, u32[]{:S(2)}, u32[]{:S(2)}) collective-permute-start(f32[4,1,32,128]{3,2,1,0:T(8,128)S(1)} %get-tuple-element.30), channel_id=1, source_target_pairs={{0,16},{16,32},{32,48},{48,64},{64,80},{80,96},{96,112},{112,128},... | collective-permute-start | bytes 196616 | tf_op jit(solution)/shard_map/ppermute | solution.py:22
  6.9 5.6 %collective-permute-start.1 = (f32[4,1,32,128]{3,2,1,0:T(8,128)S(1)}, f32[4,1,32,128]{3,2,1,0:T(8,128)S(1)}, u32[]{:S(2)}, u32[]{:S(2)}) collective-permute-start(f32[4,1,32,128]{3,2,1,0:T(8,128)S(1)} %get-tuple-element.31), channel_id=1, source_target_pairs={{16,0},{32,16},{48,32},{64,48},{80,64},{96,80},{112,96},{128,112},... | collective-permute-start | bytes 196616 | tf_op jit(solution)/shard_map/ppermute | solution.py:24
  13.5 4.5 %collective-permute-start.2 = (f32[4,10,1,128]{3,2,1,0:T(1,128)S(1)}, f32[4,10,1,128]{3,2,1,0:T(1,128)S(1)}, u32[]{:S(2)}, u32[]{:S(2)}) collective-permute-start(f32[4,10,1,128]{3,2,1,0:T(1,128)S(1)} %get-tuple-element.26), channel_id=1, source_target_pairs={{0,2},{2,4},{4,6},{6,8},{8,10},{10,12},{12,14},{1,3},{3,5},{5,7},{... | collective-permute-start | bytes 61448 | tf_op jit(solution)/shard_map/ppermute | solution.py:22
  16.7 4.5 %collective-permute-start.3 = (f32[4,10,1,128]{3,2,1,0:T(1,128)S(1)}, f32[4,10,1,128]{3,2,1,0:T(1,128)S(1)}, u32[]{:S(2)}, u32[]{:S(2)}) collective-permute-start(f32[4,10,1,128]{3,2,1,0:T(1,128)S(1)} %get-tuple-element.27), channel_id=1, source_target_pairs={{2,0},{4,2},{6,4},{8,6},{10,8},{12,10},{14,12},{3,1},{5,3},{7,5},{... | collective-permute-start | bytes 61448 | tf_op jit(solution)/shard_map/ppermute | solution.py:24
  22.4 8.1 %collective-permute-start.5 = (f32[4,10,34,1]{2,0,3,1:T(4,128)S(1)}, f32[4,10,34,1]{2,0,3,1:T(4,128)S(1)}, u32[]{:S(2)}, u32[]{:S(2)}) collective-permute-start(f32[4,10,34,1]{2,0,3,1:T(4,128)S(1)} %copy.25), channel_id=1, source_target_pairs={{1,0},{3,2},{5,4},{7,6},{9,8},{11,10},{13,12},{15,14},{17,16},{19,... | collective-permute-start | bytes 16328 | tf_op jit(solution)/shard_map/ppermute | solution.py:24
  23.7 6.4 %collective-permute-start.4 = (f32[4,10,34,1]{2,0,3,1:T(4,128)S(1)}, f32[4,10,34,1]{2,0,3,1:T(4,128)S(1)}, u32[]{:S(2)}, u32[]{:S(2)}) collective-permute-start(f32[4,10,34,1]{2,0,3,1:T(4,128)S(1)} %copy.23), channel_id=1, source_target_pairs={{0,1},{2,3},{4,5},{6,7},{8,9},{10,11},{12,13},{14,15},{16,17},{18,... | collective-permute-start | bytes 16328 | tf_op jit(solution)/shard_map/ppermute | solution.py:22
  32.3 0.9 copy-start.2
  34.1 6.4 %collective-permute-start.6 = (f32[4,1,32,128]{3,2,1,0:T(8,128)S(1)}, f32[4,1,32,128]{3,2,1,0:T(8,128)S(1)}, u32[]{:S(2)}, u32[]{:S(2)}) collective-permute-start(f32[4,1,32,128]{3,2,1,0:T(8,128)S(1)} %get-tuple-element.28), channel_id=1, source_target_pairs={{0,16},{16,32},{32,48},{48,64},{64,80},{80,96},{96,112},{112,128},... | collective-permute-start | bytes 196616 | tf_op jit(solution)/shard_map/ppermute | solution.py:22
  38.6 5.6 %collective-permute-start.7 = (f32[4,1,32,128]{3,2,1,0:T(8,128)S(1)}, f32[4,1,32,128]{3,2,1,0:T(8,128)S(1)}, u32[]{:S(2)}, u32[]{:S(2)}) collective-permute-start(f32[4,1,32,128]{3,2,1,0:T(8,128)S(1)} %get-tuple-element.29), channel_id=1, source_target_pairs={{16,0},{32,16},{48,32},{64,48},{80,64},{96,80},{112,96},{128,112},... | collective-permute-start | bytes 196616 | tf_op jit(solution)/shard_map/ppermute | solution.py:24
  44.2 4.5 %collective-permute-start.8 = (f32[4,10,1,128]{3,2,1,0:T(1,128)S(1)}, f32[4,10,1,128]{3,2,1,0:T(1,128)S(1)}, u32[]{:S(2)}, u32[]{:S(2)}) collective-permute-start(f32[4,10,1,128]{3,2,1,0:T(1,128)S(1)} %get-tuple-element.24), channel_id=1, source_target_pairs={{0,2},{2,4},{4,6},{6,8},{8,10},{10,12},{12,14},{1,3},{3,5},{5,7},{... | collective-permute-start | bytes 61448 | tf_op jit(solution)/shard_map/ppermute | solution.py:22
  47.4 5.1 %collective-permute-start.9 = (f32[4,10,1,128]{3,2,1,0:T(1,128)S(1)}, f32[4,10,1,128]{3,2,1,0:T(1,128)S(1)}, u32[]{:S(2)}, u32[]{:S(2)}) collective-permute-start(f32[4,10,1,128]{3,2,1,0:T(1,128)S(1)} %get-tuple-element.25), channel_id=1, source_target_pairs={{2,0},{4,2},{6,4},{8,6},{10,8},{12,10},{14,12},{3,1},{5,3},{7,5},{... | collective-permute-start | bytes 61448 | tf_op jit(solution)/shard_map/ppermute | solution.py:24
  52.5 0.6 copy-start.4
  56.7 9.0 %collective-permute-start.11 = (f32[4,10,34,1]{2,1,3,0:T(8,128)}, f32[4,10,34,1]{2,1,3,0:T(8,128)}, u32[]{:S(2)}, u32[]{:S(2)}) collective-permute-start(f32[4,10,34,1]{2,1,3,0:T(8,128)} %copy.30), channel_id=1, source_target_pairs={{1,0},{3,2},{5,4},{7,6},{9,8},{11,10},{13,12},{15,14},{17,16},{19,... | collective-permute-start | bytes 16328 | tf_op jit(solution)/shard_map/ppermute | solution.py:24
  59.0 8.8 %collective-permute-start.10 = (f32[4,10,34,1]{2,0,3,1:T(4,128)}, f32[4,10,34,1]{2,0,3,1:T(4,128)}, u32[]{:S(2)}, u32[]{:S(2)}) collective-permute-start(f32[4,10,34,1]{2,0,3,1:T(4,128)} %copy.28), channel_id=1, source_target_pairs={{0,1},{2,3},{4,5},{6,7},{8,9},{10,11},{12,13},{14,15},{16,17},{18,... | collective-permute-start | bytes 16328 | tf_op jit(solution)/shard_map/ppermute | solution.py:22
  70.1 0.7 copy-start.5
  71.7 3.0 %copy-start.3 = (f32[8,32,128]{2,1,0:T(8,128)S(1)}, f32[8,32,128]{2,1,0:T(8,128)}, u32[]{:S(2)}) copy-start(f32[8,32,128]{2,1,0:T(8,128)} %get-tuple-element.17) | copy-start | bytes 393220
where the time goes:
time: 187 us; the launch traced here: 186 us
  blocking collectives  107 us (57%)
  starting transfers between devices  40.2 us (21%)
  waiting for transfers between devices  12.4 us (7%)
  other arithmetic  11.8 us (6%)
  local copies, waits for them, and re-layouts  11.5 us (6%)
  between operations  3.5 us (2%)
    psum x1, blocking collectives, settle(): return lax.psum(local_sum, ('gx', 'gy', 'gz'))  107 us
    ppermute x6, starting transfers between devices, extended(): lax.ppermute(tail, axis, [(i, (i + 1) % count) for i in range(ends)])  28.4 us
    ppermute x6, starting transfers between devices, extended(): lax.ppermute(head, axis, [((i + 1) % count, i) for i in range(ends)])  11.8 us
    ppermute x6, waiting for transfers between devices, extended(): lax.ppermute(head, axis, [((i + 1) % count, i) for i in range(ends)])  11.5 us
  transfers between devices with their start and end apart: 12, of which 5 were waited for; matrix products, arithmetic and copies ran while one was open for 2% of the time, Pallas kernels for 0%

commit v1 on v0

--- a/solution.py
+++ b/solution.py
@@ -1,9 +1,12 @@
 import jax
 import jax.numpy as jnp
 from jax import lax
-from jax.sharding import PartitionSpec as P
+from jax.sharding import Mesh, PartitionSpec as P
 
 ITERS = 2
+GX = ("xl", "z", "core")
+GY = "y"
+GZ = "xh"
 
 
 step_primal = 0.25
@@ -69,19 +72,23 @@
     return (updated, 2.0 * updated - current, projected[:, 1:, 1:, 1:])
 
 
-def settle(local_sum):
-    return lax.psum(local_sum, ("gx", "gy", "gz"))
+def settle(values):
+    for axes in (("xl", "core", "xh"), ("z", "y")):
+        count = lax.axis_size(axes)
+        spread = jnp.broadcast_to(values[None], (count,) + values.shape)
+        values = jnp.sum(lax.all_to_all(spread, axes, 0, 0), axis=0)
+    return values
 
 
 def on_device(noisy_volume, primal, dual_field):
     cells_x, cells_y, cells_z = noisy_volume.shape
-    start_x = lax.axis_index("gx") * cells_x
-    start_y = lax.axis_index("gy") * cells_y
-    start_z = lax.axis_index("gz") * cells_z
+    start_x = lax.axis_index(GX) * cells_x
+    start_y = lax.axis_index(GY) * cells_y
+    start_z = lax.axis_index(GZ) * cells_z
     extent = (
-        cells_x * lax.axis_size("gx"),
-        cells_y * lax.axis_size("gy"),
-        cells_z * lax.axis_size("gz"),
+        cells_x * lax.axis_size(GX),
+        cells_y * lax.axis_size(GY),
+        cells_z * lax.axis_size(GZ),
     )
     history = []
     current = primal
@@ -89,7 +96,7 @@
     dual_now = dual_field
     for turn in range(ITERS):
         stacked = jnp.concatenate([leading[None], dual_now], axis=0)
-        padded = extended(stacked, (("gx", 1), ("gy", 2), ("gz", 3)), 1)
+        padded = extended(stacked, ((GX, 1), (GY, 2), (GZ, 3)), 1)
         lead_pad = padded[0]
         dual_pad = padded[1:]
         updated, leading, dual_new = advance(
@@ -104,20 +111,21 @@
             jnp.sum((updated - current) ** 2) / step_primal
             + jnp.sum((dual_new - dual_now) ** 2) / step_dual
         )
-        history.append(settle(local_sum))
+        history.append(local_sum)
         current = updated
         dual_now = dual_new
-    sums = jnp.stack(history)
+    sums = settle(jnp.stack(history))
     cells = float(extent[0] * extent[1] * extent[2])
     return (current, dual_now, jnp.sqrt(sums / cells))
 
 
 def solution(mesh):
-    placed = (P("gx", "gy", "gz"), P("gx", "gy", "gz"), P(None, "gx", "gy", "gz"))
+    mesh = Mesh(mesh.devices.reshape(2, 8, 2, 8, 2), ("xl", "z", "core", "y", "xh"))
+    placed = (P(GX, GY, GZ), P(GX, GY, GZ), P(None, GX, GY, GZ))
     return jax.shard_map(
         on_device,
         mesh=mesh,
         in_specs=placed,
-        out_specs=(P("gx", "gy", "gz"), P(None, "gx", "gy", "gz"), P()),
+        out_specs=(P(GX, GY, GZ), P(None, GX, GY, GZ), P()),
         check_vma=False,
     )

time: 187 us -> 117 us (0.63)
  blocking collectives: 107 us -> 37.7 us
    psum x1 -> x0, blocking collectives: 107 us -> none  [settle(): return lax.psum(local_sum, ('gx', 'gy', 'gz'))]
    all_to_all x0 -> x2, blocking collectives: none -> 37.7 us  [settle(): values = jnp.sum(lax.all_to_all(spread, axes, 0, 0), axis=0)]
  transfers between devices with their start and end apart: 12 -> 12, of which waited for: 5 -> 5; matrix products, arithmetic and copies ran while one was open for 2% -> 3% of each run, Pallas kernels for 0% -> 0%
where the time goes in v1:
time: 117 us; the launch traced here: 116 us
  starting transfers between devices  40.2 us (34%)
  blocking collectives  37.7 us (32%)
  waiting for transfers between devices  12.4 us (11%)
  local copies, waits for them, and re-layouts  11.5 us (10%)
  other arithmetic  10.6 us (9%)
  between operations  3.39 us (3%)
    all_to_all x2, blocking collectives, settle(): values = jnp.sum(lax.all_to_all(spread, axes, 0, 0), axis=0)  37.7 us
    ppermute x6, starting transfers between devices, extended(): lax.ppermute(tail, axis, [(i, (i + 1) % count) for i in range(ends)])  28.4 us
    ppermute x6, starting transfers between devices, extended(): lax.ppermute(head, axis, [((i + 1) % count, i) for i in range(ends)])  11.8 us
    ppermute x6, waiting for transfers between devices, extended(): lax.ppermute(head, axis, [((i + 1) % count, i) for i in range(ends)])  11.5 us
    slice x4, local copies, waits for them, and re-layouts, extended(): lax.slice_in_dim(cells, cells.shape[dim] - width, cells.shape[dim], axis=...  2.76 us
    slice x2, local copies, waits for them, and re-layouts, extended(): head = lax.slice_in_dim(cells, 0, width, axis=dim)  2.66 us
    ppermute x2, local copies, waits for them, and re-layouts, extended(): lax.ppermute(head, axis, [((i + 1) % count, i) for i in range(ends)])  2.45 us
  transfers between devices with their start and end apart: 12, of which 5 were waited for; matrix products, arithmetic and copies ran while one was open for 3% of the time, Pallas kernels for 0%

profile of v1, /device:TPU:1, one launch (start us, length us, event | category | flops | bytes accessed | tf_op | source)
XLA Modules:
  0.0 115.8 jit_solution(5847528507702066027)
XLA Ops:
  0.7 0.9 pad_maximum_fusion.17
  1.6 5.4 %collective-permute-start = (f32[4,1,32,128]{3,2,1,0:T(8,128)S(1)}, f32[4,1,32,128]{3,2,1,0:T(8,128)S(1)}, u32[]{:S(2)}, u32[]{:S(2)}) collective-permute-start(f32[4,1,32,128]{3,2,1,0:T(8,128)S(1)} %get-tuple-element.28), channel_id=1, source_target_pairs={{0,16},{16,32},{32,48},{48,64},{64,80},{80,96},{96,112},{112,128},... | collective-permute-start | bytes 196616 | tf_op jit(solution)/shard_map/ppermute | solution.py:25
  6.9 4.7 %collective-permute-start.1 = (f32[4,1,32,128]{3,2,1,0:T(8,128)S(1)}, f32[4,1,32,128]{3,2,1,0:T(8,128)S(1)}, u32[]{:S(2)}, u32[]{:S(2)}) collective-permute-start(f32[4,1,32,128]{3,2,1,0:T(8,128)S(1)} %get-tuple-element.29), channel_id=1, source_target_pairs={{16,0},{32,16},{48,32},{64,48},{80,64},{96,80},{112,96},{128,112},... | collective-permute-start | bytes 196616 | tf_op jit(solution)/shard_map/ppermute | solution.py:27
  11.7 0.8 collective-permute-done.1
  12.5 1.0 pad_maximum_fusion.25
  13.5 3.2 %collective-permute-start.2 = (f32[4,10,1,128]{3,2,1,0:T(1,128)S(1)}, f32[4,10,1,128]{3,2,1,0:T(1,128)S(1)}, u32[]{:S(2)}, u32[]{:S(2)}) collective-permute-start(f32[4,10,1,128]{3,2,1,0:T(1,128)S(1)} %get-tuple-element.24), channel_id=1, source_target_pairs={{0,2},{2,4},{4,6},{6,8},{8,10},{10,12},{12,14},{1,3},{3,5},{5,7},{... | collective-permute-start | bytes 61448 | tf_op jit(solution)/shard_map/ppermute | solution.py:25
  16.7 1.3 %collective-permute-start.3 = (f32[4,10,1,128]{3,2,1,0:T(1,128)S(1)}, f32[4,10,1,128]{3,2,1,0:T(1,128)S(1)}, u32[]{:S(2)}, u32[]{:S(2)}) collective-permute-start(f32[4,10,1,128]{3,2,1,0:T(1,128)S(1)} %get-tuple-element.25), channel_id=1, source_target_pairs={{2,0},{4,2},{6,4},{8,6},{10,8},{12,10},{14,12},{3,1},{5,3},{7,5},{... | collective-permute-start | bytes 61448 | tf_op jit(solution)/shard_map/ppermute | solution.py:27
  18.1 3.2 %collective-permute-done.3 = f32[4,10,1,128]{3,2,1,0:T(1,128)S(1)} collective-permute-done((f32[4,10,1,128]{3,2,1,0:T(1,128)S(1)}, f32[4,10,1,128]{3,2,1,0:T(1,128)S(1)}, u32[]{:S(2)}, u32[]{:S(2)}) %collective-permute-start.3) | collective-permute-done | bytes 20512 | tf_op jit(solution)/shard_map/ppermute | solution.py:27
  22.4 1.3 %collective-permute-start.5 = (f32[4,10,34,1]{2,0,3,1:T(4,128)S(1)}, f32[4,10,34,1]{2,0,3,1:T(4,128)S(1)}, u32[]{:S(2)}, u32[]{:S(2)}) collective-permute-start(f32[4,10,34,1]{2,0,3,1:T(4,128)S(1)} %copy.45), channel_id=1, source_target_pairs={{1,0},{3,2},{5,4},{7,6},{9,8},{11,10},{13,12},{15,14},{17,16},{19,... | collective-permute-start | bytes 16328 | tf_op jit(solution)/shard_map/ppermute | solution.py:27
  23.7 5.5 %collective-permute-start.4 = (f32[4,10,34,1]{2,0,3,1:T(4,128)S(1)}, f32[4,10,34,1]{2,0,3,1:T(4,128)S(1)}, u32[]{:S(2)}, u32[]{:S(2)}) collective-permute-start(f32[4,10,34,1]{2,0,3,1:T(4,128)S(1)} %copy.43), channel_id=1, source_target_pairs={{0,1},{2,3},{4,5},{6,7},{8,9},{10,11},{12,13},{14,15},{16,17},{18,... | collective-permute-start | bytes 16328 | tf_op jit(solution)/shard_map/ppermute | solution.py:25
  29.2 0.9 collective-permute-done.4
  31.6 0.6 multiply_reduce_fusion.1
  33.2 0.9 subtract_bitcast_fusion
  34.1 4.4 %collective-permute-start.6 = (f32[4,1,32,128]{3,2,1,0:T(8,128)S(1)}, f32[4,1,32,128]{3,2,1,0:T(8,128)S(1)}, u32[]{:S(2)}, u32[]{:S(2)}) collective-permute-start(f32[4,1,32,128]{3,2,1,0:T(8,128)S(1)} %get-tuple-element.26), channel_id=1, source_target_pairs={{0,16},{16,32},{32,48},{48,64},{64,80},{80,96},{96,112},{112,128},... | collective-permute-start | bytes 196616 | tf_op jit(solution)/shard_map/ppermute | solution.py:25
  38.6 1.9 %collective-permute-start.7 = (f32[4,1,32,128]{3,2,1,0:T(8,128)S(1)}, f32[4,1,32,128]{3,2,1,0:T(8,128)S(1)}, u32[]{:S(2)}, u32[]{:S(2)}) collective-permute-start(f32[4,1,32,128]{3,2,1,0:T(8,128)S(1)} %get-tuple-element.27), channel_id=1, source_target_pairs={{16,0},{32,16},{48,32},{64,48},{80,64},{96,80},{112,96},{128,112},... | collective-permute-start | bytes 196616 | tf_op jit(solution)/shard_map/ppermute | solution.py:27
  40.5 3.6 %collective-permute-done.7 = f32[4,1,32,128]{3,2,1,0:T(8,128)S(1)} collective-permute-done((f32[4,1,32,128]{3,2,1,0:T(8,128)S(1)}, f32[4,1,32,128]{3,2,1,0:T(8,128)S(1)}, u32[]{:S(2)}, u32[]{:S(2)}) %collective-permute-start.7) | collective-permute-done | bytes 65568 | tf_op jit(solution)/shard_map/ppermute | solution.py:27
  44.2 3.2 %collective-permute-start.8 = (f32[4,10,1,128]{3,2,1,0:T(1,128)S(1)}, f32[4,10,1,128]{3,2,1,0:T(1,128)S(1)}, u32[]{:S(2)}, u32[]{:S(2)}) collective-permute-start(f32[4,10,1,128]{3,2,1,0:T(1,128)S(1)} %get-tuple-element.22), channel_id=1, source_target_pairs={{0,2},{2,4},{4,6},{6,8},{8,10},{10,12},{12,14},{1,3},{3,5},{5,7},{... | collective-permute-start | bytes 61448 | tf_op jit(solution)/shard_map/ppermute | solution.py:25
  47.4 1.3 %collective-permute-start.9 = (f32[4,10,1,128]{3,2,1,0:T(1,128)S(1)}, f32[4,10,1,128]{3,2,1,0:T(1,128)S(1)}, u32[]{:S(2)}, u32[]{:S(2)}) collective-permute-start(f32[4,10,1,128]{3,2,1,0:T(1,128)S(1)} %get-tuple-element.23), channel_id=1, source_target_pairs={{2,0},{4,2},{6,4},{8,6},{10,8},{12,10},{14,12},{3,1},{5,3},{7,5},{... | collective-permute-start | bytes 61448 | tf_op jit(solution)/shard_map/ppermute | solution.py:27
  48.7 3.8 %collective-permute-done.9 = f32[4,10,1,128]{3,2,1,0:T(1,128)S(1)} collective-permute-done((f32[4,10,1,128]{3,2,1,0:T(1,128)S(1)}, f32[4,10,1,128]{3,2,1,0:T(1,128)S(1)}, u32[]{:S(2)}, u32[]{:S(2)}) %collective-permute-start.9) | collective-permute-done | bytes 20512 | tf_op jit(solution)/shard_map/ppermute | solution.py:27
  52.5 0.6 copy-done.4
  53.3 1.1 fusion.39
  54.4 2.3 %copy.50 = f32[4,10,34,1]{2,1,3,0:T(8,128)} copy(f32[4,10,34,1]{3,2,1,0:T(8,128)} %get-tuple-element.19) | data formatting | bytes 10880 | tf_op jit(solution)/shard_map/slice | solution.py:21
  56.7 1.3 %collective-permute-start.11 = (f32[4,10,34,1]{2,1,3,0:T(8,128)}, f32[4,10,34,1]{2,1,3,0:T(8,128)}, u32[]{:S(2)}, u32[]{:S(2)}) collective-permute-start(f32[4,10,34,1]{2,1,3,0:T(8,128)} %copy.50), channel_id=1, source_target_pairs={{1,0},{3,2},{5,4},{7,6},{9,8},{11,10},{13,12},{15,14},{17,16},{19,... | collective-permute-start | bytes 16328 | tf_op jit(solution)/shard_map/ppermute | solution.py:27
  58.0 1.0 copy.48
  59.0 6.7 %collective-permute-start.10 = (f32[4,10,34,1]{2,0,3,1:T(4,128)}, f32[4,10,34,1]{2,0,3,1:T(4,128)}, u32[]{:S(2)}, u32[]{:S(2)}) collective-permute-start(f32[4,10,34,1]{2,0,3,1:T(4,128)} %copy.48), channel_id=1, source_target_pairs={{0,1},{2,3},{4,5},{6,7},{8,9},{10,11},{12,13},{14,15},{16,17},{18,... | collective-permute-start | bytes 16328 | tf_op jit(solution)/shard_map/ppermute | solution.py:25
  65.7 2.0 %copy.52 = f32[4,10,34,1]{3,2,1,0:T(8,128)} copy(f32[4,10,34,1]{2,1,3,0:T(8,128)} %collective-permute-done.11) | data formatting | bytes 10880 | tf_op jit(solution)/shard_map/ppermute | solution.py:27
  67.7 1.1 copy.49
  68.8 1.2 %fusion.11 = f32[10,34,130]{2,1,0:T(8,128)S(1)} fusion(f32[1,8,32,128]{3,2,1,0:T(8,128)S(1)} %get-tuple-element.14, f32[3,8,32,128]{3,2,1,0:T(8,128)S(1)} %slice.172, f32[4,10,34,1]{3,2,1,0:T(8,128)} %copy.52, f32[4,10,34,1]{3,2,1,0:T(8,128)S(1)} %copy.49, f32[4,10,1,128]{3,2,1,0:T(1,128)} %copy-done.4, f32[4,10,1,128]{3,2,1,0:T(1,128)S(1)} %collective-permute-done.8, ...), kind=kLoop, calls=%fused_computation.36 | loop fusion | flops 309400 | bytes 884000 | tf_op jit(solution)/shard_map/squeeze | solution.py:100
  71.7 1.7 %multiply_reduce_fusion.3 = (f32[]{:T(128)}, f32[]{:T(128)}, f32[3,8,32,128]{3,2,1,0:T(8,128)}) fusion(f32[3,8,32,128]{3,2,1,0:T(8,128)S(1)} %copy-done, f32[3,9,33,129]{3,2,1,0:T(8,128)S(1)} %divide_select_fusion.1, f32[3,9,33,129]{3,2,1,0:T(8,128)S(1)} %divide_select_fusion), kind=kLoop, calls=%fused_computation.46 | loop fusion | flops 589822 | bytes 1572872 | tf_op jit(solution)/shard_map/reduce_sum | solution.py:112
  74.6 1.5 %multiply_reduce_fusion.5 = (f32[]{:T(128)}, f32[]{:T(128)}, f32[8,32,128]{2,1,0:T(8,128)}) fusion(f32[8,32,128]{2,1,0:T(8,128)S(1)} %copy-done.1, f32[8,32,128]{2,1,0:T(8,128)S(1)} %copy-done.3, f32[8,32,128]{2,1,0:T(8,128)S(1)} %copy-done.2, f32[3,9,33,129]{3,2,1,0:T(8,128)S(1)} %divide_select_fusion), kind=kLoop, calls=%fused_computation.81 | loop fusion | flops 524286 | bytes 1310728 | tf_op jit(solution)/shard_map/reduce_sum | solution.py:111
  77.4 17.7 %all_to_all.12 = f32[8,1,2]{2,1,0:T(1,128)S(1)} all-to-all(f32[8,1,2]{2,1,0:T(1,128)S(1)} %broadcast_in_dim.18), channel_id=1, replica_groups=mesh['xl'=2,'z'=8,'core'=2,'y'=8,'xh'=2] {'xl','core','xh'}, dimensions={0} | all-to-all | bytes 128 | tf_op jit(solution)/shard_map/all_to_all | solution.py:79
  95.1 20.0 %all_to_all.13 = f32[64,1,2]{2,1,0:T(1,128)S(1)} all-to-all(f32[64,1,2]{2,1,0:T(1,128)S(1)} %broadcast_in_dim.19), channel_id=1, replica_groups=mesh['xl'=2,'z'=8,'core'=2,'y'=8,'xh'=2] {'z','y'}, dimensions={0} | all-to-all | bytes 1024 | tf_op jit(solution)/shard_map/all_to_all | solution.py:79
  (48 shorter events, 6.2 us)
Async XLA Ops:
  0.6 20.6 %copy-start = (f32[3,8,32,128]{3,2,1,0:T(8,128)S(1)}, f32[3,8,32,128]{3,2,1,0:T(8,128)}, u32[]{:S(2)}) copy-start(f32[3,8,32,128]{3,2,1,0:T(8,128)} %param.5) | copy-start | bytes 1179652
  0.6 20.6 %copy-start.1 = (f32[8,32,128]{2,1,0:T(8,128)S(1)}, f32[8,32,128]{2,1,0:T(8,128)}, u32[]{:S(2)}) copy-start(f32[8,32,128]{2,1,0:T(8,128)} %param.4) | copy-start | bytes 393220
  1.6 10.1 %collective-permute-start = (f32[4,1,32,128]{3,2,1,0:T(8,128)S(1)}, f32[4,1,32,128]{3,2,1,0:T(8,128)S(1)}, u32[]{:S(2)}, u32[]{:S(2)}) collective-permute-start(f32[4,1,32,128]{3,2,1,0:T(8,128)S(1)} %get-tuple-element.28), channel_id=1, source_target_pairs={{0,16},{16,32},{32,48},{48,64},{64,80},{80,96},{96,112},{112,128},... | collective-permute-start | bytes 196616 | tf_op jit(solution)/shard_map/ppermute | solution.py:25
  6.9 5.6 %collective-permute-start.1 = (f32[4,1,32,128]{3,2,1,0:T(8,128)S(1)}, f32[4,1,32,128]{3,2,1,0:T(8,128)S(1)}, u32[]{:S(2)}, u32[]{:S(2)}) collective-permute-start(f32[4,1,32,128]{3,2,1,0:T(8,128)S(1)} %get-tuple-element.29), channel_id=1, source_target_pairs={{16,0},{32,16},{48,32},{64,48},{80,64},{96,80},{112,96},{128,112},... | collective-permute-start | bytes 196616 | tf_op jit(solution)/shard_map/ppermute | solution.py:27
  13.5 4.5 %collective-permute-start.2 = (f32[4,10,1,128]{3,2,1,0:T(1,128)S(1)}, f32[4,10,1,128]{3,2,1,0:T(1,128)S(1)}, u32[]{:S(2)}, u32[]{:S(2)}) collective-permute-start(f32[4,10,1,128]{3,2,1,0:T(1,128)S(1)} %get-tuple-element.24), channel_id=1, source_target_pairs={{0,2},{2,4},{4,6},{6,8},{8,10},{10,12},{12,14},{1,3},{3,5},{5,7},{... | collective-permute-start | bytes 61448 | tf_op jit(solution)/shard_map/ppermute | solution.py:25
  16.7 4.5 %collective-permute-start.3 = (f32[4,10,1,128]{3,2,1,0:T(1,128)S(1)}, f32[4,10,1,128]{3,2,1,0:T(1,128)S(1)}, u32[]{:S(2)}, u32[]{:S(2)}) collective-permute-start(f32[4,10,1,128]{3,2,1,0:T(1,128)S(1)} %get-tuple-element.25), channel_id=1, source_target_pairs={{2,0},{4,2},{6,4},{8,6},{10,8},{12,10},{14,12},{3,1},{5,3},{7,5},{... | collective-permute-start | bytes 61448 | tf_op jit(solution)/shard_map/ppermute | solution.py:27
  22.4 8.1 %collective-permute-start.5 = (f32[4,10,34,1]{2,0,3,1:T(4,128)S(1)}, f32[4,10,34,1]{2,0,3,1:T(4,128)S(1)}, u32[]{:S(2)}, u32[]{:S(2)}) collective-permute-start(f32[4,10,34,1]{2,0,3,1:T(4,128)S(1)} %copy.45), channel_id=1, source_target_pairs={{1,0},{3,2},{5,4},{7,6},{9,8},{11,10},{13,12},{15,14},{17,16},{19,... | collective-permute-start | bytes 16328 | tf_op jit(solution)/shard_map/ppermute | solution.py:27
  23.7 6.4 %collective-permute-start.4 = (f32[4,10,34,1]{2,0,3,1:T(4,128)S(1)}, f32[4,10,34,1]{2,0,3,1:T(4,128)S(1)}, u32[]{:S(2)}, u32[]{:S(2)}) collective-permute-start(f32[4,10,34,1]{2,0,3,1:T(4,128)S(1)} %copy.43), channel_id=1, source_target_pairs={{0,1},{2,3},{4,5},{6,7},{8,9},{10,11},{12,13},{14,15},{16,17},{18,... | collective-permute-start | bytes 16328 | tf_op jit(solution)/shard_map/ppermute | solution.py:25
  32.3 0.9 copy-start.2
  34.1 6.4 %collective-permute-start.6 = (f32[4,1,32,128]{3,2,1,0:T(8,128)S(1)}, f32[4,1,32,128]{3,2,1,0:T(8,128)S(1)}, u32[]{:S(2)}, u32[]{:S(2)}) collective-permute-start(f32[4,1,32,128]{3,2,1,0:T(8,128)S(1)} %get-tuple-element.26), channel_id=1, source_target_pairs={{0,16},{16,32},{32,48},{48,64},{64,80},{80,96},{96,112},{112,128},... | collective-permute-start | bytes 196616 | tf_op jit(solution)/shard_map/ppermute | solution.py:25
  38.6 5.6 %collective-permute-start.7 = (f32[4,1,32,128]{3,2,1,0:T(8,128)S(1)}, f32[4,1,32,128]{3,2,1,0:T(8,128)S(1)}, u32[]{:S(2)}, u32[]{:S(2)}) collective-permute-start(f32[4,1,32,128]{3,2,1,0:T(8,128)S(1)} %get-tuple-element.27), channel_id=1, source_target_pairs={{16,0},{32,16},{48,32},{64,48},{80,64},{96,80},{112,96},{128,112},... | collective-permute-start | bytes 196616 | tf_op jit(solution)/shard_map/ppermute | solution.py:27
  44.2 4.5 %collective-permute-start.8 = (f32[4,10,1,128]{3,2,1,0:T(1,128)S(1)}, f32[4,10,1,128]{3,2,1,0:T(1,128)S(1)}, u32[]{:S(2)}, u32[]{:S(2)}) collective-permute-start(f32[4,10,1,128]{3,2,1,0:T(1,128)S(1)} %get-tuple-element.22), channel_id=1, source_target_pairs={{0,2},{2,4},{4,6},{6,8},{8,10},{10,12},{12,14},{1,3},{3,5},{5,7},{... | collective-permute-start | bytes 61448 | tf_op jit(solution)/shard_map/ppermute | solution.py:25
  47.4 5.1 %collective-permute-start.9 = (f32[4,10,1,128]{3,2,1,0:T(1,128)S(1)}, f32[4,10,1,128]{3,2,1,0:T(1,128)S(1)}, u32[]{:S(2)}, u32[]{:S(2)}) collective-permute-start(f32[4,10,1,128]{3,2,1,0:T(1,128)S(1)} %get-tuple-element.23), channel_id=1, source_target_pairs={{2,0},{4,2},{6,4},{8,6},{10,8},{12,10},{14,12},{3,1},{5,3},{7,5},{... | collective-permute-start | bytes 61448 | tf_op jit(solution)/shard_map/ppermute | solution.py:27
  52.5 0.6 copy-start.4
  56.7 9.0 %collective-permute-start.11 = (f32[4,10,34,1]{2,1,3,0:T(8,128)}, f32[4,10,34,1]{2,1,3,0:T(8,128)}, u32[]{:S(2)}, u32[]{:S(2)}) collective-permute-start(f32[4,10,34,1]{2,1,3,0:T(8,128)} %copy.50), channel_id=1, source_target_pairs={{1,0},{3,2},{5,4},{7,6},{9,8},{11,10},{13,12},{15,14},{17,16},{19,... | collective-permute-start | bytes 16328 | tf_op jit(solution)/shard_map/ppermute | solution.py:27
  59.0 8.7 %collective-permute-start.10 = (f32[4,10,34,1]{2,0,3,1:T(4,128)}, f32[4,10,34,1]{2,0,3,1:T(4,128)}, u32[]{:S(2)}, u32[]{:S(2)}) collective-permute-start(f32[4,10,34,1]{2,0,3,1:T(4,128)} %copy.48), channel_id=1, source_target_pairs={{0,1},{2,3},{4,5},{6,7},{8,9},{10,11},{12,13},{14,15},{16,17},{18,... | collective-permute-start | bytes 16328 | tf_op jit(solution)/shard_map/ppermute | solution.py:25
  70.0 0.7 copy-start.5
  71.7 2.9 %copy-start.3 = (f32[8,32,128]{2,1,0:T(8,128)S(1)}, f32[8,32,128]{2,1,0:T(8,128)}, u32[]{:S(2)}) copy-start(f32[8,32,128]{2,1,0:T(8,128)} %get-tuple-element.15) | copy-start | bytes 393220

commit v2 on v1

v2 whole, which is shorter than its diff:
```python
import jax
import jax.numpy as jnp
from jax import lax
from jax.experimental import pallas as pl
from jax.experimental.pallas import tpu as pltpu
from jax.sharding import Mesh, PartitionSpec as P


GX = ("xl", "z", "core")
GY = "y"
GZ = "xh"
SIZES = (2, 8, 2, 8, 2)

STEP_PRIMAL = 0.25
STEP_DUAL = 0.3
RADIUS = 0.5
OWN = 8
ROWS = 32
ALL_ROWS = 40
LANES = 128
GROUP = 24

VMEM = pl.BlockSpec(memory_space=pltpu.VMEM)


def lanes_of(rows):
    return lax.broadcasted_iota(jnp.int32, (rows, LANES), 1)


def rows_of(rows):
    return lax.broadcasted_iota(jnp.int32, (rows, LANES), 0)


def fields(u_ref, p_ref, f_ref):
    return (u_ref, p_ref.at[0], p_ref.at[1], p_ref.at[2], f_ref)


def z_faces(u_ref, f_ref, p_ref, out_ref):
    first = 1 - lax.axis_index(GZ)
    pair = lanes_of(ROWS) >> 1
    columns = jnp.zeros((ROWS, LANES), jnp.float32)
    for g, field in enumerate(fields(u_ref, p_ref, f_ref)):
        for x in range(OWN):
            lane = g * GROUP + 2 * (x + 2)
            moved = pltpu.roll(field[x], lane + 2 * first, 1)
            columns = jnp.where(pair == lane // 2, moved, columns)
    out_ref[...] = columns


def y_faces(u_ref, f_ref, p_ref, columns_ref, up_ref, down_ref):
    up_ref[0] = u_ref[:, ROWS - 2, :]
    up_ref[1] = u_ref[:, ROWS - 1, :]
    down_ref[0] = u_ref[:, 0, :]
    down_ref[1] = u_ref[:, 1, :]
    for d in range(3):
        up_ref[2 + d] = p_ref[d, :, ROWS - 2, :]
        up_ref[5 + d] = p_ref[d, :, ROWS - 1, :]
        down_ref[2 + d] = p_ref[d, :, 0, :]
    up_ref[8] = f_ref[:, ROWS - 1, :]
    down_ref[5] = f_ref[:, 0, :]
    up_ref[9] = columns_ref[ROWS - 8 :, :]
    down_ref[6] = columns_ref[:8, :]


U_ROWS = ((0, False, 0), (1, False, 1), (6, True, 0), (7, True, 1))
P_ROWS = tuple(((0, False, 2 + d), (6, True, 2 + d), (7, True, 5 + d)) for d in range(3))
F_ROWS = ((0, False, 5), (7, True, 8))
HALO_ROWS = (U_ROWS, *P_ROWS, F_ROWS)


def store_halo_tile(out_ref, field, x, below_ref, above_ref):
    out_ref[...] = jnp.zeros((8, LANES), jnp.float32)
    for row, from_below, tile in HALO_ROWS[field]:
        source = below_ref if from_below else above_ref
        out_ref[row : row + 1, :] = source[tile, x : x + 1, :]


def columns_halo(below_ref, above_ref):
    row = rows_of(8)
    return jnp.where(row >= 6, below_ref[9], jnp.where(row < 2, above_ref[6], 0.0))


def x_faces(u_ref, f_ref, p_ref, columns_ref, below_ref, above_ref, up_ref, down_ref):
    named = fields(u_ref, p_ref, f_ref)
    up = ((0, 6), (0, 7), (1, 6), (2, 6), (3, 6), (1, 7), (2, 7), (3, 7), (4, 7))
    down = ((0, 0), (0, 1), (1, 0), (2, 0), (3, 0), (4, 0))
    for out_ref, planes in ((up_ref, up), (down_ref, down)):
        for k, (field, x) in enumerate(planes):
            out_ref[k, :ROWS, :] = named[field][x]
            store_halo_tile(out_ref.at[k, ROWS:, :], field, x, below_ref, above_ref)
    halo = columns_halo(below_ref, above_ref)
    for out_ref, k in ((up_ref, 9), (down_ref, 6)):
        out_ref[k, :ROWS, :] = columns_ref[...]
        out_ref[k, ROWS:, :] = halo


def y_halo(below_ref, above_ref, out_ref):
    for field in range(5):
        for x in range(OWN):
            store_halo_tile(out_ref.at[field, x], field, x, below_ref, above_ref)


def iterate(
    u_ref, f_ref, p_ref, halo_ref, columns_ref, below_y_ref, above_y_ref, below_ref, above_ref,
    u_out, p_out, sums_out, bar_s, dual_s, primal_s,
):
    size_x = OWN * lax.axis_size(GX)
    size_y = ROWS * lax.axis_size(GY)
    start_x = lax.axis_index(GX) * OWN
    start_y = lax.axis_index(GY) * ROWS
    second = lax.axis_index(GZ)
    later = second.astype(jnp.float32)
    lane = lanes_of(ALL_ROWS)
    row = rows_of(ALL_ROWS)
    odd = (lane & 1) == 1
    last_lane = lane == LANES - 1
    first_lane = lane == 0

    def as_float(mask):
        return jnp.where(mask, 1.0, 0.0)

    place_y = start_y + jnp.where(row < ROWS + 4, row, row - ALL_ROWS)
    inside_y = as_float((place_y >= 0) & (place_y <= size_y - 2))
    inside_z = 1.0 - later * as_float(last_lane)
    place_x = start_x + ((lane % GROUP) >> 1) - 2
    inside_h = as_float((place_x >= 0) & (place_x <= size_x - 2))

    def inside_x(x):
        place = start_x + x
        return jnp.where((place >= 0) & (place <= size_x - 2), 1.0, 0.0)

    def next_row(v):
        return pltpu.roll(v, ALL_ROWS - 1, 0)

    def previous_row(v):
        return pltpu.roll(v, 1, 0)

    def turn(v, by):
        return pltpu.roll(v, by % LANES, 1)

    own_columns = jnp.concatenate([columns_ref[...], columns_halo(below_y_ref, above_y_ref)], axis=0)
    in_group = lane % GROUP
    columns = jnp.where(
        in_group < 4,
        turn(below_ref[9], -16),
        jnp.where(in_group >= 20, turn(above_ref[6], 16), own_columns),
    )
    columns_u, columns_p0, columns_p1, columns_p2, columns_f = [
        turn(columns, -GROUP * g) for g in range(5)
    ]
    columns_p = (columns_p0, columns_p1, columns_p2)

    def plane(field, x):
        if 0 <= x < OWN:
            source = fields(u_ref, p_ref, f_ref)[field]
            return jnp.concatenate([source[x], halo_ref[field, x]], axis=0)
        if x < 0:
            at = {(0, -2): 0, (0, -1): 1, (4, -1): 8}
            at |= {(1 + d, -2): 2 + d for d in range(3)} | {(1 + d, -1): 5 + d for d in range(3)}
            return below_ref[at[field, x]]
        at = {(0, 8): 0, (0, 9): 1, (4, 8): 5} | {(1 + d, 8): 2 + d for d in range(3)}
        return above_ref[at[field, x]]

    def from_columns(v, x):
        return turn(v, LANES - 1 - 2 * (x + 2))

    def into_columns(into, v, x):
        return jnp.where((lane >> 1) == x + 2, turn(v, 2 * (x + 2) + 1), into)

    def project(dual, gradient, inside):
        moved = [p + (STEP_DUAL * i) * g for p, g, i in zip(dual, gradient, inside)]
        square = moved[0] * moved[0] + moved[1] * moved[1] + moved[2] * moved[2]
        scale = RADIUS * lax.rsqrt(jnp.maximum(square, RADIUS * RADIUS))
        return [q * (scale * i) for q, i in zip(moved, inside)]

    def update(u, f, divergence):
        return (u + STEP_PRIMAL * (divergence + f)) * (1.0 / (1.0 + STEP_PRIMAL))

    def fold(v):
        return v[0:8] + v[8:16] + v[16:24] + v[24:32]

    one = jnp.ones((ALL_ROWS, LANES), jnp.float32)
    totals = []
    for turn_k in range(2):
        low, high = ((-2, 9), (-1, 8))[turn_k]

        def bar(x):
            return plane(0, x) if turn_k == 0 else bar_s[x + 2]

        def dual(x):
            if turn_k == 0:
                return [plane(1 + d, x) for d in range(3)]
            return [dual_s[d, x + 2] for d in range(3)]

        def current(x):
            return plane(0, x) if turn_k == 0 else primal_s[x + 2]

        if turn_k == 0:
            columns_bar = columns_u
        gathered = jnp.zeros((ALL_ROWS, LANES), jnp.float32)
        for x in range(low, high):
            gathered = into_columns(gathered, bar(x), x)
        columns_gradient = (
            turn(columns_bar, -2) - columns_bar,
            next_row(columns_bar) - columns_bar,
            jnp.where(odd, gathered, turn(columns_bar, -1)) - columns_bar,
        )
        columns_new = project(columns_p, columns_gradient, (inside_h, inside_y, one))

        total = jnp.zeros((8, LANES), jnp.float32)
        gathered = jnp.zeros((ALL_ROWS, LANES), jnp.float32)
        previous = None
        for x in range(low, high):
            here = bar(x)
            old = dual(x)
            following = jnp.where(last_lane, from_columns(columns_bar, x), turn(here, -1))
            gradient = (bar(x + 1) - here, next_row(here) - here, following - here)
            new = project(old, gradient, (inside_x(x), inside_y, inside_z))
            if 0 <= x < OWN:
                change = sum((n - o) * (n - o) for n, o in zip(new, old))
                total += fold(change) * (1.0 / STEP_DUAL)
            gathered = into_columns(gathered, new[2], x)

            if x > low:
                before = jnp.where(
                    first_lane, later * from_columns(columns_new[2], x), turn(new[2], 1)
                )
                divergence = (
                    new[0] - previous + new[1] - previous_row(new[1]) + new[2] - before
                )
                now = current(x)
                updated = update(now, plane(4, x), divergence)
                if 0 <= x < OWN:
                    change = updated - now
                    total += fold(change * change) * (1.0 / STEP_PRIMAL)
                if turn_k == 0:
                    bar_s[x + 2] = 2.0 * updated - now
                    primal_s[x + 2] = updated
                    for d in range(3):
                        dual_s[d, x + 2] = new[d]
                else:
                    u_out[x] = updated[:ROWS]
                    for d in range(3):
                        p_out[d, x] = new[d][:ROWS]
            previous = new[0]
        totals.append(jnp.sum(total))

        if turn_k == 0:
            divergence = (
                columns_new[0] - turn(columns_new[0], 2)
                + columns_new[1] - previous_row(columns_new[1])
                + columns_new[2] - jnp.where(odd, turn(columns_new[2], 1), gathered)
            )
            updated = update(columns_u, columns_f, divergence)
            columns_bar = 2.0 * updated - columns_u
            columns_p = columns_new
    out_lane = lanes_of(8)
    sums_out[...] = jnp.where(out_lane == 0, totals[0], jnp.where(out_lane == 1, totals[1], 0.0))


def shape(*dims):
    return jax.ShapeDtypeStruct(dims, jnp.float32)


def call(kernel, count, outs, scratch=(), flops=0, size=0):
    return pl.pallas_call(
        kernel,
        out_shape=outs,
        in_specs=[VMEM] * count,
        out_specs=jax.tree.map(lambda _: VMEM, outs),
        scratch_shapes=list(scratch),
        cost_estimate=pl.CostEstimate(flops=flops, bytes_accessed=size, transcendentals=0),
    )


def shifted(axes, by):
    count = lax.axis_size(axes)
    return [(i, (i + by) % count) for i in range(count)]


def settle(values):
    for axes in (("xl", "core", "xh"), ("z", "y")):
        count = lax.axis_size(axes)
        spread = jnp.broadcast_to(values[:1, :2], (count, 2))
        values = jnp.sum(lax.all_to_all(spread, axes, 0, 0, tiled=True), axis=0, keepdims=True)
    return values[0, :2]


def on_device(f, u, p):
    columns = call(z_faces, 3, shape(ROWS, LANES))(u, f, p)
    columns = lax.ppermute(columns, GZ, shifted(GZ, 1))

    up, down = call(y_faces, 4, (shape(10, 8, LANES), shape(7, 8, LANES)))(u, f, p, columns)
    below_y = lax.ppermute(up, GY, shifted(GY, 1))
    above_y = lax.ppermute(down, GY, shifted(GY, -1))

    faces = (shape(10, ALL_ROWS, LANES), shape(7, ALL_ROWS, LANES))
    up, down = call(x_faces, 6, faces)(u, f, p, columns, below_y, above_y)
    below = lax.ppermute(up, GX, shifted(GX, 1))
    above = lax.ppermute(down, GX, shifted(GX, -1))

    halo = call(y_halo, 2, shape(5, OWN, 8, LANES))(below_y, above_y)
    denoised, dual, sums = call(
        iterate,
        9,
        (shape(OWN, ROWS, LANES), shape(3, OWN, ROWS, LANES), shape(8, LANES)),
        (
            pltpu.VMEM((12, ALL_ROWS, LANES), jnp.float32),
            pltpu.VMEM((3, 12, ALL_ROWS, LANES), jnp.float32),
            pltpu.VMEM((12, ALL_ROWS, LANES), jnp.float32),
        ),
    )(u, f, p, halo, columns, below_y, above_y, below, above)
    cells = OWN * lax.axis_size(GX) * ROWS * lax.axis_size(GY) * LANES * lax.axis_size(GZ)
    return denoised, dual, jnp.sqrt(settle(sums) / float(cells))


def solution(mesh):
    mesh = Mesh(mesh.devices.reshape(SIZES), ("xl", "z", "core", "y", "xh"))
    placed = (P(GX, GY, GZ), P(GX, GY, GZ), P(None, GX, GY, GZ))
    return jax.shard_map(
        on_device,
        mesh=mesh,
        in_specs=placed,
        out_specs=(P(GX, GY, GZ), P(None, GX, GY, GZ), P()),
        check_vma=False,
    )
```

time: 117 us -> 79 us (0.68)
  starting transfers between devices: 40.2 us -> 24.3 us
  Pallas kernels: 0 us -> 10.8 us
  other arithmetic: 10.6 us -> 0.63 us
  waiting for transfers between devices: 12.4 us -> 2.97 us
  local copies, waits for them, and re-layouts: 11.5 us -> 3.82 us
  between operations: 3.39 us -> 0.69 us
  blocking collectives: 37.7 us -> 35.3 us
    ppermute x12 -> x5, starting transfers between devices: 40.2 us -> 24.3 us  [the longest x1 6.96 us: on_device(): below = lax.ppermute(up, GX, shifted(GX, 1))]
    pallas_call x0 -> x5, Pallas kernels: none -> 10.8 us  [the longest x1 3.61 us: on_device(): call(iterate, 9, (shape(OWN, ROWS, LANES), shape(3, OWN, ROWS, LANES), sh...]
    ppermute x12 -> x5, waiting for transfers between devices: 12.4 us -> 2.97 us  [the longest x1 1.32 us: on_device(): columns = lax.ppermute(columns, GZ, shifted(GZ, 1))]
    slice x7 -> x1, local copies, waits for them, and re-layouts: 5.59 us -> 0.66 us  [settle(): spread = jnp.broadcast_to(values[:1, :2], (count, 2))]
    reduce_sum x6 -> x2, other arithmetic: 4.46 us -> 0.11 us  [settle(): jnp.sum(lax.all_to_all(spread, axes, 0, 0, tiled=True), axis=0, keepdims=...]
    ppermute x4 -> x0, local copies, waits for them, and re-layouts: 3.98 us -> none  [the longest x2 2.45 us: extended(): lax.ppermute(head, axis, [((i + 1) % count, i) for i in range(ends)])]
    all_to_all x2, blocking collectives: 37.7 us -> 35.3 us  [settle(): lax.all_to_all(spread, axes, 0, 0, tiled=True)]
    slice x4 -> x0, other arithmetic: 1.91 us -> none  [extended(): lax.slice_in_dim(cells, cells.shape[dim] - width, cells.shape[dim], axis=...]
  transfers between devices with their start and end apart: 12 -> 5, of which waited for: 5 -> 3; matrix products, arithmetic and copies ran while one was open for 3% -> 0% of each run, Pallas kernels for 0% -> 2%
where the time goes in v2:
time: 79 us; the launch traced here: 78.5 us
  blocking collectives  35.3 us (45%)
  starting transfers between devices  24.3 us (31%)
  Pallas kernels  10.8 us (14%)
  local copies, waits for them, and re-layouts  3.82 us (5%)
  waiting for transfers between devices  2.97 us (4%)
    all_to_all x2, blocking collectives, settle(): lax.all_to_all(spread, axes, 0, 0, tiled=True)  35.3 us
    ppermute x1, starting transfers between devices, on_device(): below = lax.ppermute(up, GX, shifted(GX, 1))  6.96 us
    ppermute x1, starting transfers between devices, on_device(): columns = lax.ppermute(columns, GZ, shifted(GZ, 1))  5.47 us
    ppermute x1, starting transfers between devices, on_device(): above = lax.ppermute(down, GX, shifted(GX, -1))  4.67 us
    ppermute x1, starting transfers between devices, on_device(): above_y = lax.ppermute(down, GY, shifted(GY, -1))  3.81 us
    pallas_call x1, Pallas kernels, on_device(): call(iterate, 9, (shape(OWN, ROWS, LANES), shape(3, OWN, ROWS, LANES), sh...  3.61 us
    ppermute x1, starting transfers between devices, on_device(): below_y = lax.ppermute(up, GY, shifted(GY, 1))  3.41 us
    unnamed x10, local copies, waits for them, and re-layouts  3.13 us
  transfers between devices with their start and end apart: 5, of which 3 were waited for; matrix products, arithmetic and copies ran while one was open for 0% of the time, Pallas kernels for 2%

profile of v2, /device:TPU:1, one launch (start us, length us, event | category | flops | bytes accessed | tf_op | source)
XLA Modules:
  0.0 78.5 jit_solution(4728453511513265023)
XLA Ops:
  0.6 2.0 %shard_map.58 = f32[32,128]{1,0:T(8,128)} custom-call(f32[8,32,128]{2,1,0:T(8,128)} %u_ref.7, f32[8,32,128]{2,1,0:T(8,128)} %f_ref.7, f32[3,8,32,128]{3,2,1,0:T(8,128)} %p_ref.7), custom_call_target="tpu_custom_call" | custom-call | tf_op jit(solution)/shard_map/pallas_call | solution.py:290
  2.6 5.5 %collective-permute-start = (f32[32,128]{1,0:T(8,128)}, f32[32,128]{1,0:T(8,128)S(1)}, u32[]{:S(2)}, u32[]{:S(2)}) collective-permute-start(f32[32,128]{1,0:T(8,128)} %shard_map.58), channel_id=1, source_target_pairs={{0,1},{1,0},{2,3},{3,2},{4,5},{5,4},{6,7},{7,6},{8,9},{9,8},{10,11... | collective-permute-start | bytes 49160 | tf_op jit(solution)/shard_map/ppermute | solution.py:291
  8.1 1.3 %collective-permute-done.columns_ref = f32[32,128]{1,0:T(8,128)S(1)} collective-permute-done((f32[32,128]{1,0:T(8,128)}, f32[32,128]{1,0:T(8,128)S(1)}, u32[]{:S(2)}, u32[]{:S(2)}) %collective-permute-start) | collective-permute-done | bytes 16416 | tf_op jit(solution)/shard_map/ppermute | solution.py:291
  9.4 0.0 copy-start.3
  9.4 0.6 copy-done.3
  10.0 1.8 %shard_map.59 = (f32[10,8,128]{2,1,0:T(8,128)}, f32[7,8,128]{2,1,0:T(8,128)}) custom-call(f32[8,32,128]{2,1,0:T(8,128)} %u_ref.7, f32[8,32,128]{2,1,0:T(8,128)} %f_ref.7, f32[3,8,32,128]{3,2,1,0:T(8,128)} %p_ref.7, f32[32,128]{1,0:T(8,128)} %copy-done.3), custom_call_target="tpu_custom_call" | custom-call | tf_op jit(solution)/shard_map/pallas_call | solution.py:293
  11.8 3.4 %collective-permute-start.1 = (f32[10,8,128]{2,1,0:T(8,128)}, f32[10,8,128]{2,1,0:T(8,128)S(1)}, u32[]{:S(2)}, u32[]{:S(2)}) collective-permute-start(f32[10,8,128]{2,1,0:T(8,128)} %get-tuple-element.10), channel_id=1, source_target_pairs={{0,2},{2,4},{4,6},{6,8},{8,10},{10,12},{12,14},{14,0},{1,3},{3,5},... | collective-permute-start | bytes 122888 | tf_op jit(solution)/shard_map/ppermute | solution.py:294
  15.2 3.8 %collective-permute-start.2 = (f32[7,8,128]{2,1,0:T(8,128)}, f32[7,8,128]{2,1,0:T(8,128)S(1)}, u32[]{:S(2)}, u32[]{:S(2)}) collective-permute-start(f32[7,8,128]{2,1,0:T(8,128)} %get-tuple-element.11), channel_id=1, source_target_pairs={{0,14},{2,0},{4,2},{6,4},{8,6},{10,8},{12,10},{14,12},{1,15},{3,1}... | collective-permute-start | bytes 86024 | tf_op jit(solution)/shard_map/ppermute | solution.py:295
  19.0 1.2 %collective-permute-done.2.above_ref.above_y_ref = f32[7,8,128]{2,1,0:T(8,128)S(1)} collective-permute-done((f32[7,8,128]{2,1,0:T(8,128)}, f32[7,8,128]{2,1,0:T(8,128)S(1)}, u32[]{:S(2)}, u32[]{:S(2)}) %collective-permute-start.2) | collective-permute-done | bytes 28704 | tf_op jit(solution)/shard_map/ppermute | solution.py:295
  20.2 0.0 copy-start.1
  20.2 0.0 collective-permute-done.1.below_ref.below_y_ref
  20.2 0.6 copy-done.1
  20.8 0.0 copy-start
  20.8 0.6 copy-done
  21.4 1.9 %shard_map.61 = (f32[10,40,128]{2,1,0:T(8,128)}, f32[7,40,128]{2,1,0:T(8,128)}) custom-call(f32[8,32,128]{2,1,0:T(8,128)} %u_ref.7, f32[8,32,128]{2,1,0:T(8,128)} %f_ref.7, f32[3,8,32,128]{3,2,1,0:T(8,128)} %p_ref.7, f32[32,128]{1,0:T(8,128)} %copy-done.3, f32[10,8,128]{2,1,0:T(8,128)} %copy-done, f32[7,8,128]{2,1,0:T(8,128)} %copy-done.1), custom_call_target="tpu_custom_call" | custom-call | tf_op jit(solution)/shard_map/pallas_call | solution.py:298
  23.3 7.0 %collective-permute-start.3 = (f32[10,40,128]{2,1,0:T(8,128)}, f32[10,40,128]{2,1,0:T(8,128)S(1)}, u32[]{:S(2)}, u32[]{:S(2)}) collective-permute-start(f32[10,40,128]{2,1,0:T(8,128)} %get-tuple-element.12), channel_id=1, source_target_pairs={{0,16},{16,32},{32,48},{48,64},{64,80},{80,96},{96,112},{112,128},... | collective-permute-start | bytes 614408 | tf_op jit(solution)/shard_map/ppermute | solution.py:299
  30.3 4.7 %collective-permute-start.4 = (f32[7,40,128]{2,1,0:T(8,128)}, f32[7,40,128]{2,1,0:T(8,128)S(1)}, u32[]{:S(2)}, u32[]{:S(2)}) collective-permute-start(f32[7,40,128]{2,1,0:T(8,128)} %get-tuple-element.13), channel_id=1, source_target_pairs={{0,496},{16,0},{32,16},{48,32},{64,48},{80,64},{96,80},{112,96},{1... | collective-permute-start | bytes 430088 | tf_op jit(solution)/shard_map/ppermute | solution.py:300
  35.0 1.5 %shard_map.60.halo_ref = f32[5,8,8,128]{3,2,1,0:T(8,128)} custom-call(f32[10,8,128]{2,1,0:T(8,128)} %copy-done, f32[7,8,128]{2,1,0:T(8,128)} %copy-done.1), custom_call_target="tpu_custom_call" | custom-call | tf_op jit(solution)/shard_map/pallas_call | solution.py:302
  36.5 0.5 collective-permute-done.4.above_ref
  36.9 0.0 copy-start.4
  36.9 0.0 collective-permute-done.3.below_ref
  36.9 0.6 copy-done.4
  37.6 0.0 copy-start.2
  37.6 0.7 copy-done.2
  38.3 3.6 %shard_map.62 = (f32[8,32,128]{2,1,0:T(8,128)}, f32[3,8,32,128]{3,2,1,0:T(8,128)}, f32[8,128]{1,0:T(8,128)}) custom-call(f32[8,32,128]{2,1,0:T(8,128)} %u_ref.7, f32[8,32,128]{2,1,0:T(8,128)} %f_ref.7, f32[3,8,32,128]{3,2,1,0:T(8,128)} %p_ref.7, f32[5,8,8,128]{3,2,1,0:T(8,128)} %shard_map.60.halo_ref, f32[32,128]{1,0:T(8,128)} %copy-done.3, ...), custom_call_target="tpu_custom_call" | custom-call | tf_op jit(solution)/shard_map/pallas_call | solution.py:303
  41.9 0.7 slice_bitcast_fusion
  42.5 11.7 %all_to_all.12 = f32[8,1,2]{2,1,0:T(1,128)S(1)} all-to-all(f32[8,1,2]{2,1,0:T(1,128)S(1)} %broadcast_in_dim.4), channel_id=1, replica_groups=mesh['xl'=2,'z'=8,'core'=2,'y'=8,'xh'=2] {'xl','core','xh'}, dimensions={0} | all-to-all | bytes 128 | tf_op jit(solution)/shard_map/all_to_all | solution.py:285
  54.3 23.6 %all_to_all.13 = f32[64,1,2]{2,1,0:T(1,128)S(1)} all-to-all(f32[64,1,2]{2,1,0:T(1,128)S(1)} %broadcast_in_dim.5), channel_id=1, replica_groups=mesh['xl'=2,'z'=8,'core'=2,'y'=8,'xh'=2] {'z','y'}, dimensions={0} | all-to-all | bytes 1024 | tf_op jit(solution)/shard_map/all_to_all | solution.py:285
  77.9 0.1 reduce_sum.19
  78.0 0.5 multiply_sqrt_fusion
  (3 shorter events, 0.1 us)
Async XLA Ops:
  2.6 6.8 %collective-permute-start = (f32[32,128]{1,0:T(8,128)}, f32[32,128]{1,0:T(8,128)S(1)}, u32[]{:S(2)}, u32[]{:S(2)}) collective-permute-start(f32[32,128]{1,0:T(8,128)} %shard_map.58), channel_id=1, source_target_pairs={{0,1},{1,0},{2,3},{3,2},{4,5},{5,4},{6,7},{7,6},{8,9},{9,8},{10,11... | collective-permute-start | bytes 49160 | tf_op jit(solution)/shard_map/ppermute | solution.py:291
  9.4 0.6 copy-start.3
  11.8 8.4 %collective-permute-start.1 = (f32[10,8,128]{2,1,0:T(8,128)}, f32[10,8,128]{2,1,0:T(8,128)S(1)}, u32[]{:S(2)}, u32[]{:S(2)}) collective-permute-start(f32[10,8,128]{2,1,0:T(8,128)} %get-tuple-element.10), channel_id=1, source_target_pairs={{0,2},{2,4},{4,6},{6,8},{8,10},{10,12},{12,14},{14,0},{1,3},{3,5},... | collective-permute-start | bytes 122888 | tf_op jit(solution)/shard_map/ppermute | solution.py:294
  15.2 5.0 %collective-permute-start.2 = (f32[7,8,128]{2,1,0:T(8,128)}, f32[7,8,128]{2,1,0:T(8,128)S(1)}, u32[]{:S(2)}, u32[]{:S(2)}) collective-permute-start(f32[7,8,128]{2,1,0:T(8,128)} %get-tuple-element.11), channel_id=1, source_target_pairs={{0,14},{2,0},{4,2},{6,4},{8,6},{10,8},{12,10},{14,12},{1,15},{3,1}... | collective-permute-start | bytes 86024 | tf_op jit(solution)/shard_map/ppermute | solution.py:295
  20.2 0.6 copy-start.1
  20.8 0.6 copy-start
  23.3 13.6 %collective-permute-start.3 = (f32[10,40,128]{2,1,0:T(8,128)}, f32[10,40,128]{2,1,0:T(8,128)S(1)}, u32[]{:S(2)}, u32[]{:S(2)}) collective-permute-start(f32[10,40,128]{2,1,0:T(8,128)} %get-tuple-element.12), channel_id=1, source_target_pairs={{0,16},{16,32},{32,48},{48,64},{64,80},{80,96},{96,112},{112,128},... | collective-permute-start | bytes 614408 | tf_op jit(solution)/shard_map/ppermute | solution.py:299
  30.3 6.6 %collective-permute-start.4 = (f32[7,40,128]{2,1,0:T(8,128)}, f32[7,40,128]{2,1,0:T(8,128)S(1)}, u32[]{:S(2)}, u32[]{:S(2)}) collective-permute-start(f32[7,40,128]{2,1,0:T(8,128)} %get-tuple-element.13), channel_id=1, source_target_pairs={{0,496},{16,0},{32,16},{48,32},{64,48},{80,64},{96,80},{112,96},{1... | collective-permute-start | bytes 430088 | tf_op jit(solution)/shard_map/ppermute | solution.py:300
  36.9 0.7 copy-start.4
  37.6 0.7 copy-start.2

commit v3 on v2

--- a/solution.py
+++ b/solution.py
@@ -262,14 +262,14 @@
     return jax.ShapeDtypeStruct(dims, jnp.float32)
 
 
-def call(kernel, count, outs, scratch=(), flops=0, size=0):
+def call(kernel, count, outs, scratch=(), limit=4):
     return pl.pallas_call(
         kernel,
         out_shape=outs,
         in_specs=[VMEM] * count,
         out_specs=jax.tree.map(lambda _: VMEM, outs),
         scratch_shapes=list(scratch),
-        cost_estimate=pl.CostEstimate(flops=flops, bytes_accessed=size, transcendentals=0),
+        compiler_params=pltpu.CompilerParams(vmem_limit_bytes=limit * 2**20),
     )
 
 

time: 79 us -> 70.8 us (0.90)
  Pallas kernels: 10.8 us -> 2.63 us
  local copies, waits for them, and re-layouts: 3.82 us -> 2.84 us
  waiting for transfers between devices: 2.97 us -> 3.77 us
    pallas_call x1, Pallas kernels: 1.91 us -> 0.04 us  [on_device(): up, down = call(x_faces, 6, faces)(u, f, p, columns, below_y, above_y)]
    pallas_call x1, Pallas kernels: 1.79 us -> 0.04 us  [on_device(): call(y_faces, 4, (shape(10, 8, LANES), shape(7, 8, LANES)))]
    pallas_call x1, Pallas kernels: 1.98 us -> 0.24 us  [on_device(): columns = call(z_faces, 3, shape(ROWS, LANES))(u, f, p)]
    pallas_call x1, Pallas kernels: 1.49 us -> 0.05 us  [on_device(): halo = call(y_halo, 2, shape(5, OWN, 8, LANES))(below_y, above_y)]
    pallas_call x1, Pallas kernels: 3.61 us -> 2.27 us  [on_device(): call(iterate, 9, (shape(OWN, ROWS, LANES), shape(3, OWN, ROWS, LANES), sh...]
    ppermute x1, waiting for transfers between devices: 0.47 us -> 1.69 us  [on_device(): above = lax.ppermute(down, GX, shifted(GX, -1))]
  transfers between devices with their start and end apart: 5 -> 5, of which waited for: 3 -> 3; matrix products, arithmetic and copies ran while one was open for 0% -> 0% of each run, Pallas kernels for 2% -> 0%
where the time goes in v3:
time: 70.8 us; the launch traced here: 70.4 us
  blocking collectives  35.3 us (50%)
  starting transfers between devices  24.5 us (35%)
  waiting for transfers between devices  3.77 us (5%)
  local copies, waits for them, and re-layouts  2.84 us (4%)
  Pallas kernels  2.63 us (4%)
  between operations  0.72 us (1%)
    all_to_all x2, blocking collectives, settle(): lax.all_to_all(spread, axes, 0, 0, tiled=True)  35.3 us
    ppermute x1, starting transfers between devices, on_device(): below = lax.ppermute(up, GX, shifted(GX, 1))  7.1 us
    ppermute x1, starting transfers between devices, on_device(): columns = lax.ppermute(columns, GZ, shifted(GZ, 1))  5.48 us
    ppermute x1, starting transfers between devices, on_device(): above = lax.ppermute(down, GX, shifted(GX, -1))  4.67 us
    ppermute x1, starting transfers between devices, on_device(): above_y = lax.ppermute(down, GY, shifted(GY, -1))  3.81 us
    ppermute x1, starting transfers between devices, on_device(): below_y = lax.ppermute(up, GY, shifted(GY, 1))  3.42 us
    unnamed x10, local copies, waits for them, and re-layouts  2.81 us
    pallas_call x1, Pallas kernels, on_device(): call(iterate, 9, (shape(OWN, ROWS, LANES), shape(3, OWN, ROWS, LANES), sh...  2.27 us
  transfers between devices with their start and end apart: 5, of which 3 were waited for; matrix products, arithmetic and copies ran while one was open for 0% of the time, Pallas kernels for 0%

profile of v3, /device:TPU:1, one launch (start us, length us, event | category | flops | bytes accessed | tf_op | source)
XLA Modules:
  0.0 70.4 jit_solution(9276779743793625912)
XLA Ops:
  0.6 0.0 copy-start
  0.6 1.0 %copy-done = f32[3,8,32,128]{3,2,1,0:T(8,128)S(1)} copy-done((f32[3,8,32,128]{3,2,1,0:T(8,128)S(1)}, f32[3,8,32,128]{3,2,1,0:T(8,128)}, u32[]{:S(2)}) %copy-start) | copy-done | bytes 393240
  1.6 0.0 copy-start.1
  1.6 0.9 %copy-done.1 = f32[8,32,128]{2,1,0:T(8,128)S(1)} copy-done((f32[8,32,128]{2,1,0:T(8,128)S(1)}, f32[8,32,128]{2,1,0:T(8,128)}, u32[]{:S(2)}) %copy-start.1) | copy-done | bytes 131096
  2.5 0.0 copy-start.3
  2.5 0.9 %copy-done.3 = f32[8,32,128]{2,1,0:T(8,128)S(1)} copy-done((f32[8,32,128]{2,1,0:T(8,128)S(1)}, f32[8,32,128]{2,1,0:T(8,128)}, u32[]{:S(2)}) %copy-start.3) | copy-done | bytes 131096
  3.4 0.2 shard_map.58
  3.7 5.5 %collective-permute-start = (f32[32,128]{1,0:T(8,128)S(1)}, f32[32,128]{1,0:T(8,128)S(1)}, u32[]{:S(2)}, u32[]{:S(2)}) collective-permute-start(f32[32,128]{1,0:T(8,128)S(1)} %shard_map.58), channel_id=1, source_target_pairs={{0,1},{1,0},{2,3},{3,2},{4,5},{5,4},{6,7},{7,6},{8,9},{9,8},{10,11... | collective-permute-start | bytes 49160 | tf_op jit(solution)/shard_map/ppermute | solution.py:291
  9.2 1.1 %collective-permute-done.columns_ref = f32[32,128]{1,0:T(8,128)S(1)} collective-permute-done((f32[32,128]{1,0:T(8,128)S(1)}, f32[32,128]{1,0:T(8,128)S(1)}, u32[]{:S(2)}, u32[]{:S(2)}) %collective-permute-start) | collective-permute-done | bytes 16416 | tf_op jit(solution)/shard_map/ppermute | solution.py:291
  10.3 3.4 %collective-permute-start.1 = (f32[10,8,128]{2,1,0:T(8,128)S(1)}, f32[10,8,128]{2,1,0:T(8,128)S(1)}, u32[]{:S(2)}, u32[]{:S(2)}) collective-permute-start(f32[10,8,128]{2,1,0:T(8,128)S(1)} %get-tuple-element.10), channel_id=1, source_target_pairs={{0,2},{2,4},{4,6},{6,8},{8,10},{10,12},{12,14},{14,0},{1,3},{3,5},... | collective-permute-start | bytes 122888 | tf_op jit(solution)/shard_map/ppermute | solution.py:294
  13.7 3.8 %collective-permute-start.2 = (f32[7,8,128]{2,1,0:T(8,128)S(1)}, f32[7,8,128]{2,1,0:T(8,128)S(1)}, u32[]{:S(2)}, u32[]{:S(2)}) collective-permute-start(f32[7,8,128]{2,1,0:T(8,128)S(1)} %get-tuple-element.11), channel_id=1, source_target_pairs={{0,14},{2,0},{4,2},{6,4},{8,6},{10,8},{12,10},{14,12},{1,15},{3,1}... | collective-permute-start | bytes 86024 | tf_op jit(solution)/shard_map/ppermute | solution.py:295
  17.6 1.0 %collective-permute-done.2.above_ref.above_y_ref = f32[7,8,128]{2,1,0:T(8,128)S(1)} collective-permute-done((f32[7,8,128]{2,1,0:T(8,128)S(1)}, f32[7,8,128]{2,1,0:T(8,128)S(1)}, u32[]{:S(2)}, u32[]{:S(2)}) %collective-permute-start.2) | collective-permute-done | bytes 28704 | tf_op jit(solution)/shard_map/ppermute | solution.py:295
  18.5 0.0 collective-permute-done.1.below_ref.below_y_ref
  18.5 0.0 copy-start.4
  18.6 0.0 copy-start.2
  18.6 7.1 %collective-permute-start.3 = (f32[10,40,128]{2,1,0:T(8,128)S(1)}, f32[10,40,128]{2,1,0:T(8,128)S(1)}, u32[]{:S(2)}, u32[]{:S(2)}) collective-permute-start(f32[10,40,128]{2,1,0:T(8,128)S(1)} %get-tuple-element.12), channel_id=1, source_target_pairs={{0,16},{16,32},{32,48},{48,64},{64,80},{80,96},{96,112},{112,128},... | collective-permute-start | bytes 614408 | tf_op jit(solution)/shard_map/ppermute | solution.py:299
  25.7 4.7 %collective-permute-start.4 = (f32[7,40,128]{2,1,0:T(8,128)S(1)}, f32[7,40,128]{2,1,0:T(8,128)S(1)}, u32[]{:S(2)}, u32[]{:S(2)}) collective-permute-start(f32[7,40,128]{2,1,0:T(8,128)S(1)} %get-tuple-element.13), channel_id=1, source_target_pairs={{0,496},{16,0},{32,16},{48,32},{64,48},{80,64},{96,80},{112,96},{1... | collective-permute-start | bytes 430088 | tf_op jit(solution)/shard_map/ppermute | solution.py:300
  30.4 1.7 %collective-permute-done.4.above_ref = f32[7,40,128]{2,1,0:T(8,128)S(1)} collective-permute-done((f32[7,40,128]{2,1,0:T(8,128)S(1)}, f32[7,40,128]{2,1,0:T(8,128)S(1)}, u32[]{:S(2)}, u32[]{:S(2)}) %collective-permute-start.4) | collective-permute-done | bytes 143392 | tf_op jit(solution)/shard_map/ppermute | solution.py:300
  32.1 0.0 collective-permute-done.3.below_ref
  32.1 0.0 copy-done.4
  32.1 0.0 copy-done.2
  32.1 2.3 %shard_map.62 = (f32[8,32,128]{2,1,0:T(8,128)}, f32[3,8,32,128]{3,2,1,0:T(8,128)}, f32[8,128]{1,0:T(8,128)S(1)}) custom-call(f32[8,32,128]{2,1,0:T(8,128)S(1)} %copy-done.2, f32[8,32,128]{2,1,0:T(8,128)S(1)} %copy-done.4, f32[3,8,32,128]{3,2,1,0:T(8,128)S(1)} %copy-done, f32[5,8,8,128]{3,2,1,0:T(8,128)S(1)} %shard_map.60.halo_ref, ...), custom_call_target="tpu_custom_call" | custom-call | tf_op jit(solution)/shard_map/pallas_call | solution.py:303
  34.4 11.6 %all_to_all.12 = f32[8,1,2]{2,1,0:T(1,128)S(1)} all-to-all(f32[8,1,2]{2,1,0:T(1,128)S(1)} %broadcast_in_dim.4), channel_id=1, replica_groups=mesh['xl'=2,'z'=8,'core'=2,'y'=8,'xh'=2] {'xl','core','xh'}, dimensions={0} | all-to-all | bytes 128 | tf_op jit(solution)/shard_map/all_to_all | solution.py:285
  46.1 23.7 %all_to_all.13 = f32[64,1,2]{2,1,0:T(1,128)S(1)} all-to-all(f32[64,1,2]{2,1,0:T(1,128)S(1)} %broadcast_in_dim.5), channel_id=1, replica_groups=mesh['xl'=2,'z'=8,'core'=2,'y'=8,'xh'=2] {'z','y'}, dimensions={0} | all-to-all | bytes 1024 | tf_op jit(solution)/shard_map/all_to_all | solution.py:285
  69.8 0.1 reduce_sum.19
  69.8 0.5 multiply_sqrt_fusion
  (7 shorter events, 0.2 us)
Async XLA Ops:
  0.6 1.0 %copy-start = (f32[3,8,32,128]{3,2,1,0:T(8,128)S(1)}, f32[3,8,32,128]{3,2,1,0:T(8,128)}, u32[]{:S(2)}) copy-start(f32[3,8,32,128]{3,2,1,0:T(8,128)} %p_ref.7) | copy-start | bytes 1179652
  1.6 0.9 %copy-start.1 = (f32[8,32,128]{2,1,0:T(8,128)S(1)}, f32[8,32,128]{2,1,0:T(8,128)}, u32[]{:S(2)}) copy-start(f32[8,32,128]{2,1,0:T(8,128)} %u_ref.7) | copy-start | bytes 393220
  2.5 0.9 %copy-start.3 = (f32[8,32,128]{2,1,0:T(8,128)S(1)}, f32[8,32,128]{2,1,0:T(8,128)}, u32[]{:S(2)}) copy-start(f32[8,32,128]{2,1,0:T(8,128)} %f_ref.7) | copy-start | bytes 393220
  3.7 6.6 %collective-permute-start = (f32[32,128]{1,0:T(8,128)S(1)}, f32[32,128]{1,0:T(8,128)S(1)}, u32[]{:S(2)}, u32[]{:S(2)}) collective-permute-start(f32[32,128]{1,0:T(8,128)S(1)} %shard_map.58), channel_id=1, source_target_pairs={{0,1},{1,0},{2,3},{3,2},{4,5},{5,4},{6,7},{7,6},{8,9},{9,8},{10,11... | collective-permute-start | bytes 49160 | tf_op jit(solution)/shard_map/ppermute | solution.py:291
  10.3 8.2 %collective-permute-start.1 = (f32[10,8,128]{2,1,0:T(8,128)S(1)}, f32[10,8,128]{2,1,0:T(8,128)S(1)}, u32[]{:S(2)}, u32[]{:S(2)}) collective-permute-start(f32[10,8,128]{2,1,0:T(8,128)S(1)} %get-tuple-element.10), channel_id=1, source_target_pairs={{0,2},{2,4},{4,6},{6,8},{8,10},{10,12},{12,14},{14,0},{1,3},{3,5},... | collective-permute-start | bytes 122888 | tf_op jit(solution)/shard_map/ppermute | solution.py:294
  13.7 4.8 %collective-permute-start.2 = (f32[7,8,128]{2,1,0:T(8,128)S(1)}, f32[7,8,128]{2,1,0:T(8,128)S(1)}, u32[]{:S(2)}, u32[]{:S(2)}) collective-permute-start(f32[7,8,128]{2,1,0:T(8,128)S(1)} %get-tuple-element.11), channel_id=1, source_target_pairs={{0,14},{2,0},{4,2},{6,4},{8,6},{10,8},{12,10},{14,12},{1,15},{3,1}... | collective-permute-start | bytes 86024 | tf_op jit(solution)/shard_map/ppermute | solution.py:295
  18.5 13.6 %copy-start.4 = (f32[8,32,128]{2,1,0:T(8,128)S(1)}, f32[8,32,128]{2,1,0:T(8,128)}, u32[]{:S(2)}) copy-start(f32[8,32,128]{2,1,0:T(8,128)} %f_ref.7) | copy-start | bytes 393220
  18.6 13.5 %copy-start.2 = (f32[8,32,128]{2,1,0:T(8,128)S(1)}, f32[8,32,128]{2,1,0:T(8,128)}, u32[]{:S(2)}) copy-start(f32[8,32,128]{2,1,0:T(8,128)} %u_ref.7) | copy-start | bytes 393220
  18.6 13.5 %collective-permute-start.3 = (f32[10,40,128]{2,1,0:T(8,128)S(1)}, f32[10,40,128]{2,1,0:T(8,128)S(1)}, u32[]{:S(2)}, u32[]{:S(2)}) collective-permute-start(f32[10,40,128]{2,1,0:T(8,128)S(1)} %get-tuple-element.12), channel_id=1, source_target_pairs={{0,16},{16,32},{32,48},{48,64},{64,80},{80,96},{96,112},{112,128},... | collective-permute-start | bytes 614408 | tf_op jit(solution)/shard_map/ppermute | solution.py:299
  25.7 6.4 %collective-permute-start.4 = (f32[7,40,128]{2,1,0:T(8,128)S(1)}, f32[7,40,128]{2,1,0:T(8,128)S(1)}, u32[]{:S(2)}, u32[]{:S(2)}) collective-permute-start(f32[7,40,128]{2,1,0:T(8,128)S(1)} %get-tuple-element.13), channel_id=1, source_target_pairs={{0,496},{16,0},{32,16},{48,32},{64,48},{80,64},{96,80},{112,96},{1... | collective-permute-start | bytes 430088 | tf_op jit(solution)/shard_map/ppermute | solution.py:300

commit v4 on v3

--- a/solution.py
+++ b/solution.py
@@ -33,6 +33,20 @@
 
 def fields(u_ref, p_ref, f_ref):
     return (u_ref, p_ref.at[0], p_ref.at[1], p_ref.at[2], f_ref)
+
+
+def load(u_ref, f_ref, p_ref, out_ref, u_vmem, f_vmem, p_vmem, sem):
+    copies = [
+        pltpu.make_async_copy(source, target, sem.at[k])
+        for k, (source, target) in enumerate(
+            ((u_ref, u_vmem), (f_ref, f_vmem), (p_ref, p_vmem))
+        )
+    ]
+    for copy in copies:
+        copy.start()
+    for copy in copies:
+        copy.wait()
+    z_faces(u_vmem, f_vmem, p_vmem, out_ref)
 
 
 def z_faces(u_ref, f_ref, p_ref, out_ref):
@@ -287,7 +301,14 @@
 
 
 def on_device(f, u, p):
-    columns = call(z_faces, 3, shape(ROWS, LANES))(u, f, p)
+    columns, u, f, p = pl.pallas_call(
+        load,
+        out_shape=(shape(ROWS, LANES), shape(*u.shape), shape(*f.shape), shape(*p.shape)),
+        in_specs=[pl.BlockSpec(memory_space=pltpu.HBM)] * 3,
+        out_specs=(VMEM,) * 4,
+        scratch_shapes=[pltpu.SemaphoreType.DMA((3,))],
+        compiler_params=pltpu.CompilerParams(vmem_limit_bytes=4 * 2**20),
+    )(*[pltpu.with_memory_space_constraint(v, pltpu.HBM) for v in (u, f, p)])
     columns = lax.ppermute(columns, GZ, shifted(GZ, 1))
 
     up, down = call(y_faces, 4, (shape(10, 8, LANES), shape(7, 8, LANES)))(u, f, p, columns)

time: 70.8 us -> 68.9 us (0.973)
  local copies, waits for them, and re-layouts: 2.84 us -> 0.03 us
  Pallas kernels: 2.63 us -> 3.79 us
    unnamed x10 -> x0, local copies, waits for them, and re-layouts: 2.81 us -> none
    pallas_call x1, Pallas kernels: 0.24 us -> 1.4 us  [on_device(): pl.pallas_call(load, out_shape=(shape(ROWS, LANES), shape(*u.shape), shap...]
where the time goes in v4:
time: 68.9 us; the launch traced here: 68.6 us
  blocking collectives  35.3 us (51%)
  starting transfers between devices  24.4 us (35%)
  Pallas kernels  3.79 us (6%)
  waiting for transfers between devices  3.77 us (5%)
  between operations  0.7 us (1%)
    all_to_all x2, blocking collectives, settle(): lax.all_to_all(spread, axes, 0, 0, tiled=True)  35.3 us
    ppermute x1, starting transfers between devices, on_device(): below = lax.ppermute(up, GX, shifted(GX, 1))  6.97 us
    ppermute x1, starting transfers between devices, on_device(): columns = lax.ppermute(columns, GZ, shifted(GZ, 1))  5.48 us
    ppermute x1, starting transfers between devices, on_device(): above = lax.ppermute(down, GX, shifted(GX, -1))  4.67 us
    ppermute x1, starting transfers between devices, on_device(): above_y = lax.ppermute(down, GY, shifted(GY, -1))  3.81 us
    ppermute x1, starting transfers between devices, on_device(): below_y = lax.ppermute(up, GY, shifted(GY, 1))  3.42 us
    pallas_call x1, Pallas kernels, on_device(): call(iterate, 9, (shape(OWN, ROWS, LANES), shape(3, OWN, ROWS, LANES), sh...  2.27 us
    ppermute x1, waiting for transfers between devices, on_device(): above = lax.ppermute(down, GX, shifted(GX, -1))  1.69 us
  transfers between devices with their start and end apart: 5, of which 3 were waited for; matrix products, arithmetic and copies ran while one was open for 0% of the time, Pallas kernels for 0%

profile of v4, /device:TPU:1, one launch (start us, length us, event | category | flops | bytes accessed | tf_op | source)
XLA Modules:
  0.0 68.6 jit_solution(5274397689721727133)
XLA Ops:
  0.6 1.4 %shard_map.58 = (f32[32,128]{1,0:T(8,128)S(1)}, f32[8,32,128]{2,1,0:T(8,128)S(1)}, f32[8,32,128]{2,1,0:T(8,128)S(1)}, f32[3,8,32,128]{3,2,1,0:T(8,128)S(1)}) custom-call(f32[8,32,128]{2,1,0:T(8,128)} %u_ref.1, f32[8,32,128]{2,1,0:T(8,128)} %f_ref.1, f32[3,8,32,128]{3,2,1,0:T(8,128)} %p_ref.1), custom_call_target="tpu_custom_call" | custom-call | tf_op jit(solution)/shard_map/pallas_call | solution.py:304
  2.0 5.5 %collective-permute-start = (f32[32,128]{1,0:T(8,128)S(1)}, f32[32,128]{1,0:T(8,128)S(1)}, u32[]{:S(2)}, u32[]{:S(2)}) collective-permute-start(f32[32,128]{1,0:T(8,128)S(1)} %get-tuple-element.17), channel_id=1, source_target_pairs={{0,1},{1,0},{2,3},{3,2},{4,5},{5,4},{6,7},{7,6},{8,9},{9,8},{10,11... | collective-permute-start | bytes 49160 | tf_op jit(solution)/shard_map/ppermute | solution.py:312
  7.5 1.1 %collective-permute-done.columns_ref = f32[32,128]{1,0:T(8,128)S(1)} collective-permute-done((f32[32,128]{1,0:T(8,128)S(1)}, f32[32,128]{1,0:T(8,128)S(1)}, u32[]{:S(2)}, u32[]{:S(2)}) %collective-permute-start) | collective-permute-done | bytes 16416 | tf_op jit(solution)/shard_map/ppermute | solution.py:312
  8.7 3.4 %collective-permute-start.1 = (f32[10,8,128]{2,1,0:T(8,128)S(1)}, f32[10,8,128]{2,1,0:T(8,128)S(1)}, u32[]{:S(2)}, u32[]{:S(2)}) collective-permute-start(f32[10,8,128]{2,1,0:T(8,128)S(1)} %get-tuple-element.18), channel_id=1, source_target_pairs={{0,2},{2,4},{4,6},{6,8},{8,10},{10,12},{12,14},{14,0},{1,3},{3,5},... | collective-permute-start | bytes 122888 | tf_op jit(solution)/shard_map/ppermute | solution.py:315
  12.1 3.8 %collective-permute-start.2 = (f32[7,8,128]{2,1,0:T(8,128)S(1)}, f32[7,8,128]{2,1,0:T(8,128)S(1)}, u32[]{:S(2)}, u32[]{:S(2)}) collective-permute-start(f32[7,8,128]{2,1,0:T(8,128)S(1)} %get-tuple-element.19), channel_id=1, source_target_pairs={{0,14},{2,0},{4,2},{6,4},{8,6},{10,8},{12,10},{14,12},{1,15},{3,1}... | collective-permute-start | bytes 86024 | tf_op jit(solution)/shard_map/ppermute | solution.py:316
  15.9 1.0 %collective-permute-done.2.above_ref.above_y_ref = f32[7,8,128]{2,1,0:T(8,128)S(1)} collective-permute-done((f32[7,8,128]{2,1,0:T(8,128)S(1)}, f32[7,8,128]{2,1,0:T(8,128)S(1)}, u32[]{:S(2)}, u32[]{:S(2)}) %collective-permute-start.2) | collective-permute-done | bytes 28704 | tf_op jit(solution)/shard_map/ppermute | solution.py:316
  16.9 0.0 collective-permute-done.1.below_ref.below_y_ref
  16.9 7.0 %collective-permute-start.3 = (f32[10,40,128]{2,1,0:T(8,128)S(1)}, f32[10,40,128]{2,1,0:T(8,128)S(1)}, u32[]{:S(2)}, u32[]{:S(2)}) collective-permute-start(f32[10,40,128]{2,1,0:T(8,128)S(1)} %get-tuple-element.20), channel_id=1, source_target_pairs={{0,16},{16,32},{32,48},{48,64},{64,80},{80,96},{96,112},{112,128},... | collective-permute-start | bytes 614408 | tf_op jit(solution)/shard_map/ppermute | solution.py:320
  23.9 4.7 %collective-permute-start.4 = (f32[7,40,128]{2,1,0:T(8,128)S(1)}, f32[7,40,128]{2,1,0:T(8,128)S(1)}, u32[]{:S(2)}, u32[]{:S(2)}) collective-permute-start(f32[7,40,128]{2,1,0:T(8,128)S(1)} %get-tuple-element.21), channel_id=1, source_target_pairs={{0,496},{16,0},{32,16},{48,32},{64,48},{80,64},{96,80},{112,96},{1... | collective-permute-start | bytes 430088 | tf_op jit(solution)/shard_map/ppermute | solution.py:321
  28.7 1.7 %collective-permute-done.4.above_ref = f32[7,40,128]{2,1,0:T(8,128)S(1)} collective-permute-done((f32[7,40,128]{2,1,0:T(8,128)S(1)}, f32[7,40,128]{2,1,0:T(8,128)S(1)}, u32[]{:S(2)}, u32[]{:S(2)}) %collective-permute-start.4) | collective-permute-done | bytes 143392 | tf_op jit(solution)/shard_map/ppermute | solution.py:321
  30.3 0.0 collective-permute-done.3.below_ref
  30.3 2.3 %shard_map.62 = (f32[8,32,128]{2,1,0:T(8,128)}, f32[3,8,32,128]{3,2,1,0:T(8,128)}, f32[8,128]{1,0:T(8,128)S(1)}) custom-call(f32[8,32,128]{2,1,0:T(8,128)S(1)} %get-tuple-element.14.u_ref, f32[8,32,128]{2,1,0:T(8,128)S(1)} %get-tuple-element.15.f_ref, f32[3,8,32,128]{3,2,1,0:T(8,128)S(1)} %get-tuple-element.16.p_ref, ...), custom_call_target="tpu_custom_call" | custom-call | tf_op jit(solution)/shard_map/pallas_call | solution.py:324
  32.6 11.6 %all_to_all.12 = f32[8,1,2]{2,1,0:T(1,128)S(1)} all-to-all(f32[8,1,2]{2,1,0:T(1,128)S(1)} %broadcast_in_dim.4), channel_id=1, replica_groups=mesh['xl'=2,'z'=8,'core'=2,'y'=8,'xh'=2] {'xl','core','xh'}, dimensions={0} | all-to-all | bytes 128 | tf_op jit(solution)/shard_map/all_to_all | solution.py:299
  44.3 23.7 %all_to_all.13 = f32[64,1,2]{2,1,0:T(1,128)S(1)} all-to-all(f32[64,1,2]{2,1,0:T(1,128)S(1)} %broadcast_in_dim.5), channel_id=1, replica_groups=mesh['xl'=2,'z'=8,'core'=2,'y'=8,'xh'=2] {'z','y'}, dimensions={0} | all-to-all | bytes 1024 | tf_op jit(solution)/shard_map/all_to_all | solution.py:299
  68.0 0.1 reduce_sum.19
  68.0 0.5 multiply_sqrt_fusion
  (7 shorter events, 0.2 us)
Async XLA Ops:
  2.0 6.6 %collective-permute-start = (f32[32,128]{1,0:T(8,128)S(1)}, f32[32,128]{1,0:T(8,128)S(1)}, u32[]{:S(2)}, u32[]{:S(2)}) collective-permute-start(f32[32,128]{1,0:T(8,128)S(1)} %get-tuple-element.17), channel_id=1, source_target_pairs={{0,1},{1,0},{2,3},{3,2},{4,5},{5,4},{6,7},{7,6},{8,9},{9,8},{10,11... | collective-permute-start | bytes 49160 | tf_op jit(solution)/shard_map/ppermute | solution.py:312
  8.7 8.2 %collective-permute-start.1 = (f32[10,8,128]{2,1,0:T(8,128)S(1)}, f32[10,8,128]{2,1,0:T(8,128)S(1)}, u32[]{:S(2)}, u32[]{:S(2)}) collective-permute-start(f32[10,8,128]{2,1,0:T(8,128)S(1)} %get-tuple-element.18), channel_id=1, source_target_pairs={{0,2},{2,4},{4,6},{6,8},{8,10},{10,12},{12,14},{14,0},{1,3},{3,5},... | collective-permute-start | bytes 122888 | tf_op jit(solution)/shard_map/ppermute | solution.py:315
  12.1 4.8 %collective-permute-start.2 = (f32[7,8,128]{2,1,0:T(8,128)S(1)}, f32[7,8,128]{2,1,0:T(8,128)S(1)}, u32[]{:S(2)}, u32[]{:S(2)}) collective-permute-start(f32[7,8,128]{2,1,0:T(8,128)S(1)} %get-tuple-element.19), channel_id=1, source_target_pairs={{0,14},{2,0},{4,2},{6,4},{8,6},{10,8},{12,10},{14,12},{1,15},{3,1}... | collective-permute-start | bytes 86024 | tf_op jit(solution)/shard_map/ppermute | solution.py:316
  16.9 13.4 %collective-permute-start.3 = (f32[10,40,128]{2,1,0:T(8,128)S(1)}, f32[10,40,128]{2,1,0:T(8,128)S(1)}, u32[]{:S(2)}, u32[]{:S(2)}) collective-permute-start(f32[10,40,128]{2,1,0:T(8,128)S(1)} %get-tuple-element.20), channel_id=1, source_target_pairs={{0,16},{16,32},{32,48},{48,64},{64,80},{80,96},{96,112},{112,128},... | collective-permute-start | bytes 614408 | tf_op jit(solution)/shard_map/ppermute | solution.py:320
  23.9 6.4 %collective-permute-start.4 = (f32[7,40,128]{2,1,0:T(8,128)S(1)}, f32[7,40,128]{2,1,0:T(8,128)S(1)}, u32[]{:S(2)}, u32[]{:S(2)}) collective-permute-start(f32[7,40,128]{2,1,0:T(8,128)S(1)} %get-tuple-element.21), channel_id=1, source_target_pairs={{0,496},{16,0},{32,16},{48,32},{64,48},{80,64},{96,80},{112,96},{1... | collective-permute-start | bytes 430088 | tf_op jit(solution)/shard_map/ppermute | solution.py:321

commit v5 on v1

v5 whole, which is shorter than its diff:
```python
import jax
import jax.numpy as jnp
from jax import lax
from jax.experimental import pallas as pl
from jax.experimental.pallas import tpu as pltpu
from jax.sharding import Mesh, PartitionSpec as P


GX = ("xl", "z", "core")
GY = "y"
GZ = "xh"
SIZES = (2, 8, 2, 8, 2)

STEP_PRIMAL = 0.25
STEP_DUAL = 0.3
RADIUS = 0.5
OWN = 8
ROWS = 32
ALL_ROWS = 40
LANES = 128
GROUP = 24

VMEM = pl.BlockSpec(memory_space=pltpu.VMEM)


def lanes_of(rows):
    return lax.broadcasted_iota(jnp.int32, (rows, LANES), 1)


def rows_of(rows):
    return lax.broadcasted_iota(jnp.int32, (rows, LANES), 0)


def fields(u_ref, p_ref, f_ref):
    return (u_ref, p_ref.at[0], p_ref.at[1], p_ref.at[2], f_ref)


def next_row(v):
    return pltpu.roll(v, v.shape[0] - 1, 0)


def previous_row(v):
    return pltpu.roll(v, 1, 0)


def turn(v, by):
    return pltpu.roll(v, by % LANES, 1)


def lane_of(x):
    return 2 * (x + 2)


def from_columns(v, x):
    return turn(v, LANES - 1 - lane_of(x))


def into_columns(into, v, x):
    return jnp.where((lanes_of(ALL_ROWS) >> 1) == x + 2, turn(v, lane_of(x) + 1), into)


def load(u_ref, f_ref, p_ref, out_ref, u_vmem, f_vmem, p_vmem, sem):
    copies = [
        pltpu.make_async_copy(source, target, sem.at[k])
        for k, (source, target) in enumerate(
            ((u_ref, u_vmem), (f_ref, f_vmem), (p_ref, p_vmem))
        )
    ]
    for copy in copies:
        copy.start()
    for copy in copies:
        copy.wait()
    first = 1 - lax.axis_index(GZ)
    pair = lanes_of(ROWS) >> 1
    columns = jnp.zeros((ROWS, LANES), jnp.float32)
    for g, field in enumerate(fields(u_vmem, p_vmem, f_vmem)):
        for x in range(OWN):
            lane = g * GROUP + lane_of(x)
            moved = pltpu.roll(field[x], lane + 2 * first, 1)
            columns = jnp.where(pair == lane // 2, moved, columns)
    out_ref[...] = columns


def is_even(axes):
    return lax.rem(lax.axis_index(axes), 2) == 0


def sort_out(even, up, down):
    return jnp.where(even, up, down), jnp.where(even, down, up)


def y_faces(u_ref, f_ref, p_ref, columns_ref, first_ref, second_ref):
    up = [u_ref[:, ROWS - 2, :], u_ref[:, ROWS - 1, :]]
    up += [p_ref[d, :, ROWS - 2, :] for d in range(3)]
    up += [p_ref[d, :, ROWS - 1, :] for d in range(3)]
    up += [f_ref[:, ROWS - 1, :], columns_ref[ROWS - 8 :, :]]
    down = {0: u_ref[:, 0, :], 1: u_ref[:, 1, :], 8: f_ref[:, 0, :], 9: columns_ref[:8, :]}
    down |= {2 + d: p_ref[d, :, 0, :] for d in range(3)}
    even = is_even(GY)
    for k, tile in enumerate(up):
        first_ref[k], second_ref[k] = sort_out(even, tile, down.get(k, tile))


U_ROWS = ((0, False, 0), (1, False, 1), (6, True, 0), (7, True, 1))
P_ROWS = tuple(((0, False, 2 + d), (6, True, 2 + d), (7, True, 5 + d)) for d in range(3))
F_ROWS = ((0, False, 8), (7, True, 8))
HALO_ROWS = (U_ROWS, *P_ROWS, F_ROWS)


class Local:
    def __init__(self):
        self.size_x = OWN * lax.axis_size(GX)
        size_y = ROWS * lax.axis_size(GY)
        self.start_x = lax.axis_index(GX) * OWN
        start_y = lax.axis_index(GY) * ROWS
        self.later = lax.axis_index(GZ).astype(jnp.float32)
        lane = lanes_of(ALL_ROWS)
        row = rows_of(ALL_ROWS)
        self.lane = lane
        self.odd = (lane & 1) == 1
        self.last_lane = lane == LANES - 1
        self.first_lane = lane == 0
        place_y = start_y + jnp.where(row < ROWS + 4, row, row - ALL_ROWS)
        self.inside_y = jnp.where((place_y >= 0) & (place_y <= size_y - 2), 1.0, 0.0)
        self.inside_z = 1.0 - self.later * jnp.where(self.last_lane, 1.0, 0.0)
        place_x = self.start_x + ((lane % GROUP) >> 1) - 2
        self.inside_h = jnp.where((place_x >= 0) & (place_x <= self.size_x - 2), 1.0, 0.0)
        self.columns_inside = (self.inside_h, self.inside_y, 1.0)

    def inside(self, x):
        place = self.start_x + x
        at_x = jnp.where((place >= 0) & (place <= self.size_x - 2), 1.0, 0.0)
        return (at_x, self.inside_y, self.inside_z)

    def columns_at(self, x):
        return (self.lane >> 1) == x + 2

    def following(self, v, columns, x):
        return jnp.where(self.last_lane, from_columns(columns, x), turn(v, -1))

    def preceding(self, v, columns, x):
        return jnp.where(self.first_lane, self.later * from_columns(columns, x), turn(v, 1))

    def columns_following(self, v, gathered):
        return jnp.where(self.odd, gathered, turn(v, -1))

    def columns_preceding(self, v, gathered):
        return jnp.where(self.odd, turn(v, 1), gathered)

    def move(self, dual, bar, nexts, inside):
        return [p + (STEP_DUAL * i) * (n - bar) for p, n, i in zip(dual, nexts, inside)]

    def project(self, moved, inside):
        square = moved[0] * moved[0] + moved[1] * moved[1] + moved[2] * moved[2]
        scale = RADIUS * lax.rsqrt(jnp.maximum(square, RADIUS * RADIUS))
        return [q * (scale * i) for q, i in zip(moved, inside)]

    def dual_plane(self, dual, bar, above, columns_bar, x):
        nexts = (above, next_row(bar), self.following(bar, columns_bar, x))
        inside = self.inside(x)
        return self.project(self.move(dual, bar, nexts, inside), inside)

    def dual_columns(self, dual, bar, gathered):
        moved = self.move(
            dual,
            bar,
            (turn(bar, -2), next_row(bar), self.columns_following(bar, gathered)),
            self.columns_inside,
        )
        return moved, self.project(moved, self.columns_inside)

    def across(self, dual, columns_z, x):
        return dual[1] - previous_row(dual[1]) + dual[2] - self.preceding(dual[2], columns_z, x)

    def columns_across(self, dual, gathered):
        return (
            dual[1] - previous_row(dual[1]) + dual[2] - self.columns_preceding(dual[2], gathered)
        )


UPDATE = 1.0 / (1.0 + STEP_PRIMAL)
BAR_U = 2.0 * UPDATE - 1.0
BAR_F = 2.0 * UPDATE * STEP_PRIMAL


def updated(u, f, divergence):
    return (u + STEP_PRIMAL * (divergence + f)) * UPDATE


def early_bar(u, f):
    return BAR_U * u + BAR_F * f


def fold(v):
    return v[0:8] + v[8:16] + v[16:24] + v[24:32]


def change_of(new, old):
    return sum(fold((n - o) * (n - o)) for n, o in zip(new, old))


def plane_of(u_ref, f_ref, p_ref, halo_ref):
    sources = fields(u_ref, p_ref, f_ref)

    def plane(field, x):
        return jnp.concatenate([sources[field][x], halo_ref[field, x]], axis=0)

    def dual(x):
        return [plane(1 + d, x) for d in range(3)]

    return plane, dual


def split(columns):
    u, p0, p1, p2, f = [turn(columns, -GROUP * g) for g in range(5)]
    return u, [p0, p1, p2], f


def zeros():
    return jnp.zeros((ALL_ROWS, LANES), jnp.float32)


def gather(v, planes):
    into = zeros()
    for x in planes:
        into = into_columns(into, v(x), x)
    return into


def x_faces(
    u_ref, f_ref, p_ref, columns_ref, first_y_ref, second_y_ref,
    halo_ref, columns_out, first_ref, second_ref, below_s, above_s,
):
    even = is_even(GY)
    for k in range(10):
        above_s[k], below_s[k] = sort_out(even, first_y_ref[k], second_y_ref[k])
    for field in range(5):
        for x in range(OWN):
            halo_ref[field, x] = jnp.zeros((8, LANES), jnp.float32)
            for row, from_below, tile in HALO_ROWS[field]:
                source = below_s if from_below else above_s
                halo_ref[field, x, row : row + 1, :] = source[tile, x : x + 1, :]
    row = rows_of(8)
    columns_out[:ROWS, :] = columns_ref[...]
    columns_out[ROWS:, :] = jnp.where(row >= 6, below_s[9], jnp.where(row < 2, above_s[9], 0.0))

    here = Local()
    plane, dual = plane_of(u_ref, f_ref, p_ref, halo_ref)
    c_u, c_p, c_f = split(columns_out[...])
    c_moved, c_dual = here.dual_columns(c_p, c_u, gather(lambda x: plane(0, x), range(OWN)))

    top = OWN - 1
    u, p = plane(0, top), dual(top)
    nexts = (0.0, next_row(u), here.following(u, c_u, top))
    moved = here.move(p, u, nexts, (1.0, here.inside_y, here.inside_z))
    last = here.dual_plane(dual(top - 1), plane(0, top - 1), u, c_u, top - 1)
    up = [*moved, early_bar(u, plane(4, top)) - BAR_F * last[0]]
    c_up = [
        c_p[0] - STEP_DUAL * c_u, c_moved[1], c_moved[2],
        early_bar(c_u, c_f) - BAR_F * turn(c_dual[0], 2),
    ]

    u = plane(0, 0)
    new = here.dual_plane(dual(0), u, plane(0, 1), c_u, 0)
    bar = early_bar(u, plane(4, 0)) + BAR_F * (new[0] + here.across(new, c_dual[2], 0))
    down = [u, bar]
    gathered = into_columns(zeros(), new[2], 0)
    c_bar = early_bar(c_u, c_f) + BAR_F * (c_dual[0] + here.columns_across(c_dual, gathered))
    c_down = [c_u, c_bar]

    def packed(parts):
        group = here.lane // GROUP
        whole = parts[0]
        for k, part in enumerate(parts[1:], 1):
            whole = jnp.where(group == k, turn(part, GROUP * k), whole)
        return whole

    up.append(packed(c_up))
    down = [*down, up[2], up[3], packed(c_down)]
    even = is_even(GX)
    for k in range(5):
        first_ref[k], second_ref[k] = sort_out(even, up[k], down[k])


def early(
    u_ref, f_ref, p_ref, halo_ref, columns_ref,
    dual_out, bar_out, primal_out, dual_end, primal_end, gathered_out, sums_out,
):
    here = Local()
    plane, dual = plane_of(u_ref, f_ref, p_ref, halo_ref)
    c_u, c_p, c_f = split(columns_ref[...])
    sums = [jnp.zeros((8, LANES), jnp.float32) for _ in range(2)]

    gathered_u = gather(lambda x: plane(0, x), range(OWN))
    _, c_dual = here.dual_columns(c_p, c_u, gathered_u)
    gathered_dual = zeros()
    gathered_bar = zeros()
    for x in range(7):
        old = dual(x)
        u = plane(0, x)
        new = here.dual_plane(old, u, plane(0, x + 1), c_u, x)
        sums[0] += change_of(new, old) * (1.0 / STEP_DUAL)
        gathered_dual = into_columns(gathered_dual, new[2], x)
        for d in range(3):
            dual_out[d, x] = new[d]
        if x > 0:
            divergence = new[0] - previous + here.across(new, c_dual[2], x)
            now = updated(u, plane(4, x), divergence)
            bar = 2.0 * now - u
            sums[0] += change_of([now], [u]) * (1.0 / STEP_PRIMAL)
            gathered_bar = into_columns(gathered_bar, bar, x)
            primal_out[x] = now
            bar_out[x] = bar
        previous = new[0]
    divergence = c_dual[0] - turn(c_dual[0], 2) + here.columns_across(c_dual, gathered_dual)
    c_bar = early_bar(c_u, c_f) + BAR_F * divergence

    _, c_end = here.dual_columns(c_dual, c_bar, gathered_bar)
    for x in range(1, 6):
        old = [dual_out[d, x] for d in range(3)]
        new = here.dual_plane(old, bar_out[x], bar_out[x + 1], c_bar, x)
        sums[1] += change_of(new, old) * (1.0 / STEP_DUAL)
        for d in range(3):
            dual_end[d, x] = new[d]
        if x > 1:
            u = primal_out[x]
            divergence = new[0] - previous + here.across(new, c_end[2], x)
            now = updated(u, plane(4, x), divergence)
            sums[1] += change_of([now], [u]) * (1.0 / STEP_PRIMAL)
            primal_end[x] = now[:ROWS]
        previous = new[0]
    for k, v in enumerate((gathered_u, gathered_dual, gathered_bar)):
        gathered_out[k] = v
    for k in range(2):
        sums_out[k] = sums[k]


def late(
    u_ref, f_ref, p_ref, halo_ref, columns_ref, first_x_ref, second_x_ref,
    dual_ref, bar_ref, primal_ref, dual_end, primal_end, gathered_ref, early_sums,
    u_out, p_out, sums_out,
):
    here = Local()
    plane, dual = plane_of(u_ref, f_ref, p_ref, halo_ref)
    even = is_even(GX)
    above, below = zip(*[sort_out(even, first_x_ref[k], second_x_ref[k]) for k in range(5)])
    sums = [early_sums[0], early_sums[1]]

    c_u, c_p, c_f = split(columns_ref[...])
    lowest, highest = here.columns_at(-1), here.columns_at(OWN)

    def from_below(k):
        return turn(below[4], -GROUP * k - 16)

    def from_above(k):
        return turn(above[4], -GROUP * k + 16)

    c_u = jnp.where(highest, from_above(0), c_u)
    c_moved, _ = here.dual_columns(c_p, c_u, gathered_ref[0])
    sent = (from_below(0) + STEP_DUAL * turn(c_u, -2), from_below(1), from_below(2))
    c_moved = [jnp.where(lowest, s, m) for s, m in zip(sent, c_moved)]
    c_dual = here.project(c_moved, here.columns_inside)

    duals = {x: [dual_ref[d, x] for d in range(3)] for x in range(7)}
    bars = {x: bar_ref[x] for x in range(1, 7)}
    primals = {x: primal_ref[x] for x in range(1, 7)}
    top = OWN - 1
    moved = (below[0] + STEP_DUAL * plane(0, 0), below[1], below[2])
    duals[-1] = here.project(moved, here.inside(-1))
    old = dual(top)
    duals[top] = here.dual_plane(old, plane(0, top), above[0], c_u, top)
    sums[0] += change_of(duals[top], old) * (1.0 / STEP_DUAL)
    for x in (0, top):
        u = plane(0, x)
        divergence = duals[x][0] - duals[x - 1][0] + here.across(duals[x], c_dual[2], x)
        primals[x] = updated(u, plane(4, x), divergence)
        bars[x] = 2.0 * primals[x] - u
        sums[0] += change_of([primals[x]], [u]) * (1.0 / STEP_PRIMAL)
    bars[-1] = below[3] + BAR_F * (duals[-1][0] + here.across(duals[-1], c_dual[2], -1))
    bars[OWN] = above[1] - BAR_F * duals[top][0]

    gathered = gathered_ref[1]
    for x in (-1, top):
        gathered = into_columns(gathered, duals[x][2], x)
    known = jnp.where(
        lowest, from_below(3), jnp.where(highest, from_above(1), early_bar(c_u, c_f))
    )
    own_part = jnp.where(highest, 0.0, c_dual[0] + here.columns_across(c_dual, gathered))
    previous = jnp.where(lowest, 0.0, turn(c_dual[0], 2))
    c_bar = known + BAR_F * (own_part - previous)

    gathered = gathered_ref[2]
    for x in (0, top):
        gathered = into_columns(gathered, bars[x], x)
    _, c_end = here.dual_columns(c_dual, c_bar, gathered)
    ends = {x: [dual_end[d, x] for d in range(3)] for x in range(1, 6)}
    for x in (-1, 0, 6, 7):
        ends[x] = here.dual_plane(duals[x], bars[x], bars[x + 1], c_bar, x)
        if x >= 0:
            sums[1] += change_of(ends[x], duals[x]) * (1.0 / STEP_DUAL)
    for x in range(OWN):
        if 2 <= x <= 5:
            u_out[x] = primal_end[x]
        else:
            divergence = ends[x][0] - ends[x - 1][0] + here.across(ends[x], c_end[2], x)
            now = updated(primals[x], plane(4, x), divergence)
            sums[1] += change_of([now], [primals[x]]) * (1.0 / STEP_PRIMAL)
            u_out[x] = now[:ROWS]
        for d in range(3):
            p_out[d, x] = ends[x][d][:ROWS]
    out_lane = lanes_of(8)
    sums_out[...] = jnp.where(
        out_lane == 0, jnp.sum(sums[0]), jnp.where(out_lane == 1, jnp.sum(sums[1]), 0.0)
    )


def shape(*dims):
    return jax.ShapeDtypeStruct(dims, jnp.float32)


def call(kernel, count, outs, scratch=(), specs=None, work=0):
    return pl.pallas_call(
        kernel,
        out_shape=outs,
        in_specs=specs or [VMEM] * count,
        out_specs=jax.tree.map(lambda _: VMEM, outs),
        scratch_shapes=list(scratch),
        compiler_params=pltpu.CompilerParams(vmem_limit_bytes=4 * 2**20),
        cost_estimate=pl.CostEstimate(flops=work, bytes_accessed=work, transcendentals=0),
    )


def trade(first, second, axes):
    count = lax.axis_size(axes)
    outer = [(i, (i + 1 if i % 2 else i - 1) % count) for i in range(count)]
    second = lax.ppermute(second, axes, outer)
    first = lax.ppermute(first, axes, [(i, i ^ 1) for i in range(count)])
    return first, second


def settle(values):
    for axes in (("xl", "core", "xh"), ("z", "y")):
        count = lax.axis_size(axes)
        spread = jnp.broadcast_to(values[:1, :2], (count, 2))
        values = jnp.sum(lax.all_to_all(spread, axes, 0, 0, tiled=True), axis=0, keepdims=True)
    return values[0, :2]


def on_device(f, u, p):
    inputs = [pltpu.with_memory_space_constraint(v, pltpu.HBM) for v in (u, f, p)]
    columns, u, f, p = call(
        load,
        3,
        (shape(ROWS, LANES), shape(*u.shape), shape(*f.shape), shape(*p.shape)),
        [pltpu.SemaphoreType.DMA((3,))],
        [pl.BlockSpec(memory_space=pltpu.HBM)] * 3,
    )(*inputs)
    columns = lax.ppermute(columns, GZ, [(0, 1), (1, 0)])

    message = shape(10, 8, LANES)
    first_y, second_y = trade(*call(y_faces, 4, (message, message))(u, f, p, columns), GY)

    message = shape(5, ALL_ROWS, LANES)
    halo, columns, first, second = call(
        x_faces,
        6,
        (shape(5, OWN, 8, LANES), shape(ALL_ROWS, LANES), message, message),
        [pltpu.VMEM((10, 8, LANES), jnp.float32)] * 2,
    )(u, f, p, columns, first_y, second_y)
    first, second = trade(first, second, GX)

    planes = shape(OWN, ALL_ROWS, LANES)
    triple = shape(3, OWN, ALL_ROWS, LANES)
    done = call(
        early,
        5,
        (
            triple, planes, planes, triple, shape(OWN, ROWS, LANES),
            shape(3, ALL_ROWS, LANES), shape(2, 8, LANES),
        ),
        work=10**6,
    )(u, f, p, halo, columns)
    denoised, dual, sums = call(
        late,
        14,
        (shape(OWN, ROWS, LANES), shape(3, OWN, ROWS, LANES), shape(8, LANES)),
    )(u, f, p, halo, columns, first, second, *done)
    cells = OWN * lax.axis_size(GX) * ROWS * lax.axis_size(GY) * LANES * lax.axis_size(GZ)
    return denoised, dual, jnp.sqrt(settle(sums) / float(cells))


def solution(mesh):
    mesh = Mesh(mesh.devices.reshape(SIZES), ("xl", "z", "core", "y", "xh"))
    placed = (P(GX, GY, GZ), P(GX, GY, GZ), P(None, GX, GY, GZ))
    return jax.shard_map(
        on_device,
        mesh=mesh,
        in_specs=placed,
        out_specs=(P(GX, GY, GZ), P(None, GX, GY, GZ), P()),
        check_vma=False,
    )
```

time: 117 us -> 68.8 us (0.59)
  starting transfers between devices: 40.2 us -> 24.4 us
  local copies, waits for them, and re-layouts: 11.5 us -> 0.03 us
  other arithmetic: 10.6 us -> 0.63 us
  waiting for transfers between devices: 12.4 us -> 5.39 us
  blocking collectives: 37.7 us -> 33.1 us
  Pallas kernels: 0 us -> 4.24 us
  between operations: 3.39 us -> 0.72 us
    ppermute x12 -> x5, starting transfers between devices: 40.2 us -> 24.4 us  [the longest x2 12.1 us: trade(): first = lax.ppermute(first, axes, [(i, i ^ 1) for i in range(count)])]
    ppermute x12 -> x5, waiting for transfers between devices: 12.4 us -> 5.39 us  [the longest x2 4.27 us: trade(): second = lax.ppermute(second, axes, outer)]
    slice x7 -> x1, local copies, waits for them, and re-layouts: 5.59 us -> 0.01 us  [settle(): spread = jnp.broadcast_to(values[:1, :2], (count, 2))]
    all_to_all x2, blocking collectives: 37.7 us -> 33.1 us  [settle(): lax.all_to_all(spread, axes, 0, 0, tiled=True)]
    reduce_sum x6 -> x2, other arithmetic: 4.46 us -> 0.11 us  [settle(): jnp.sum(lax.all_to_all(spread, axes, 0, 0, tiled=True), axis=0, keepdims=...]
    pallas_call x0 -> x5, Pallas kernels: none -> 4.24 us  [the longest x1 1.4 us: on_device(): call(load, 3, (shape(ROWS, LANES), shape(*u.shape), shape(*f.shape), shap...]
    ppermute x4 -> x0, local copies, waits for them, and re-layouts: 3.98 us -> none  [the longest x2 2.45 us: extended(): lax.ppermute(head, axis, [((i + 1) % count, i) for i in range(ends)])]
    slice x4 -> x0, other arithmetic: 1.91 us -> none  [extended(): lax.slice_in_dim(cells, cells.shape[dim] - width, cells.shape[dim], axis=...]
  transfers between devices with their start and end apart: 12 -> 5, of which waited for: 5 -> 3; matrix products, arithmetic and copies ran while one was open for 3% -> 0% of each run, Pallas kernels for 0% -> 2%
where the time goes in v5:
time: 68.8 us; the launch traced here: 68.5 us
  blocking collectives  33.1 us (48%)
  starting transfers between devices  24.4 us (35%)
  waiting for transfers between devices  5.39 us (8%)
  Pallas kernels  4.24 us (6%)
  between operations  0.72 us (1%)
    all_to_all x2, blocking collectives, settle(): lax.all_to_all(spread, axes, 0, 0, tiled=True)  33.1 us
    ppermute x2, starting transfers between devices, trade(): first = lax.ppermute(first, axes, [(i, i ^ 1) for i in range(count)])  12.1 us
    ppermute x2, starting transfers between devices, trade(): second = lax.ppermute(second, axes, outer)  6.79 us
    ppermute x1, starting transfers between devices, on_device(): columns = lax.ppermute(columns, GZ, [(0, 1), (1, 0)])  5.48 us
    ppermute x2, waiting for transfers between devices, trade(): second = lax.ppermute(second, axes, outer)  4.27 us
    pallas_call x1, Pallas kernels, on_device(): call(load, 3, (shape(ROWS, LANES), shape(*u.shape), shape(*f.shape), shap...  1.4 us
  transfers between devices with their start and end apart: 5, of which 3 were waited for; matrix products, arithmetic and copies ran while one was open for 0% of the time, Pallas kernels for 2%

profile of v5, /device:TPU:1, one launch (start us, length us, event | category | flops | bytes accessed | tf_op | source)
XLA Modules:
  0.0 68.5 jit_solution(512552691870560168)
XLA Ops:
  0.6 1.4 %shard_map.58 = (f32[32,128]{1,0:T(8,128)S(1)}, f32[8,32,128]{2,1,0:T(8,128)S(1)}, f32[8,32,128]{2,1,0:T(8,128)S(1)}, f32[3,8,32,128]{3,2,1,0:T(8,128)S(1)}) custom-call(f32[8,32,128]{2,1,0:T(8,128)} %u_ref.1, f32[8,32,128]{2,1,0:T(8,128)} %f_ref.1, f32[3,8,32,128]{3,2,1,0:T(8,128)} %p_ref.1), custom_call_target="tpu_custom_call" | custom-call | tf_op jit(solution)/shard_map/pallas_call | solution.py:451
  2.0 5.5 %collective-permute-start = (f32[32,128]{1,0:T(8,128)S(1)}, f32[32,128]{1,0:T(8,128)S(1)}, u32[]{:S(2)}, u32[]{:S(2)}) collective-permute-start(f32[32,128]{1,0:T(8,128)S(1)} %get-tuple-element.26), channel_id=1, source_target_pairs={{0,1},{1,0},{2,3},{3,2},{4,5},{5,4},{6,7},{7,6},{8,9},{9,8},{10,11... | collective-permute-start | bytes 49160 | tf_op jit(solution)/shard_map/ppermute | solution.py:458
  7.5 1.1 %collective-permute-done.columns_ref = f32[32,128]{1,0:T(8,128)S(1)} collective-permute-done((f32[32,128]{1,0:T(8,128)S(1)}, f32[32,128]{1,0:T(8,128)S(1)}, u32[]{:S(2)}, u32[]{:S(2)}) %collective-permute-start) | collective-permute-done | bytes 16416 | tf_op jit(solution)/shard_map/ppermute | solution.py:458
  8.6 0.1 shard_map.59
  8.7 3.4 %collective-permute-start.1 = (f32[10,8,128]{2,1,0:T(8,128)S(1)}, f32[10,8,128]{2,1,0:T(8,128)S(1)}, u32[]{:S(2)}, u32[]{:S(2)}) collective-permute-start(f32[10,8,128]{2,1,0:T(8,128)S(1)} %get-tuple-element.27), channel_id=1, source_target_pairs={{0,2},{2,0},{4,6},{6,4},{8,10},{10,8},{12,14},{14,12},{1,3},{3,1},... | collective-permute-start | bytes 122888 | tf_op jit(solution)/shard_map/ppermute | solution.py:437
  12.1 4.9 %collective-permute-start.2 = (f32[10,8,128]{2,1,0:T(8,128)S(1)}, f32[10,8,128]{2,1,0:T(8,128)S(1)}, u32[]{:S(2)}, u32[]{:S(2)}) collective-permute-start(f32[10,8,128]{2,1,0:T(8,128)S(1)} %get-tuple-element.28), channel_id=1, source_target_pairs={{0,14},{2,4},{4,2},{6,8},{8,6},{10,12},{12,10},{14,0},{1,15},{3,5}... | collective-permute-start | bytes 122888 | tf_op jit(solution)/shard_map/ppermute | solution.py:436
  17.0 0.0 collective-permute-done.1.first_y_ref
  17.0 1.4 %collective-permute-done.2.second_y_ref = f32[10,8,128]{2,1,0:T(8,128)S(1)} collective-permute-done((f32[10,8,128]{2,1,0:T(8,128)S(1)}, f32[10,8,128]{2,1,0:T(8,128)S(1)}, u32[]{:S(2)}, u32[]{:S(2)}) %collective-permute-start.2) | collective-permute-done | bytes 40992 | tf_op jit(solution)/shard_map/ppermute | solution.py:436
  18.4 0.3 shard_map.60
  18.7 8.7 %collective-permute-start.3 = (f32[5,40,128]{2,1,0:T(8,128)S(1)}, f32[5,40,128]{2,1,0:T(8,128)S(1)}, u32[]{:S(2)}, u32[]{:S(2)}) collective-permute-start(f32[5,40,128]{2,1,0:T(8,128)S(1)} %get-tuple-element.31), channel_id=1, source_target_pairs={{0,16},{16,0},{32,48},{48,32},{64,80},{80,64},{96,112},{112,96},{1... | collective-permute-start | bytes 307208 | tf_op jit(solution)/shard_map/ppermute | solution.py:437
  27.4 1.9 %collective-permute-start.4 = (f32[5,40,128]{2,1,0:T(8,128)S(1)}, f32[5,40,128]{2,1,0:T(8,128)S(1)}, u32[]{:S(2)}, u32[]{:S(2)}) collective-permute-start(f32[5,40,128]{2,1,0:T(8,128)S(1)} %get-tuple-element.32), channel_id=1, source_target_pairs={{0,496},{16,32},{32,16},{48,64},{64,48},{80,96},{96,80},{112,128},... | collective-permute-start | bytes 307208 | tf_op jit(solution)/shard_map/ppermute | solution.py:436
  29.3 1.1 %shard_map.61 = (f32[3,8,40,128]{3,2,1,0:T(8,128)S(1)}, f32[8,40,128]{2,1,0:T(8,128)S(1)}, f32[8,40,128]{2,1,0:T(8,128)S(1)}, f32[3,8,40,128]{3,2,1,0:T(8,128)S(...) custom-call(f32[8,32,128]{2,1,0:T(8,128)S(1)} %get-tuple-element.23.u_ref, ...), custom_call_target="tpu_custom_call" | custom-call | flops 1000000 | bytes 1000000 | tf_op jit(solution)/shard_map/pallas_call | solution.py:474
  30.5 0.0 collective-permute-done.3.first_x_ref
  30.5 2.9 %collective-permute-done.4.second_x_ref = f32[5,40,128]{2,1,0:T(8,128)S(1)} collective-permute-done((f32[5,40,128]{2,1,0:T(8,128)S(1)}, f32[5,40,128]{2,1,0:T(8,128)S(1)}, u32[]{:S(2)}, u32[]{:S(2)}) %collective-permute-start.4) | collective-permute-done | bytes 102432 | tf_op jit(solution)/shard_map/ppermute | solution.py:436
  33.4 1.3 %shard_map.62 = (f32[8,32,128]{2,1,0:T(8,128)}, f32[3,8,32,128]{3,2,1,0:T(8,128)}, f32[8,128]{1,0:T(8,128)S(1)}) custom-call(f32[8,32,128]{2,1,0:T(8,128)S(1)} %get-tuple-element.23.u_ref, f32[8,32,128]{2,1,0:T(8,128)S(1)} %get-tuple-element.24.f_ref, f32[3,8,32,128]{3,2,1,0:T(8,128)S(1)} %get-tuple-element.25.p_ref, ...), custom_call_target="tpu_custom_call" | custom-call | tf_op jit(solution)/shard_map/pallas_call | solution.py:483
  34.7 12.9 %all_to_all.12 = f32[8,1,2]{2,1,0:T(1,128)S(1)} all-to-all(f32[8,1,2]{2,1,0:T(1,128)S(1)} %broadcast_in_dim.4), channel_id=1, replica_groups=mesh['xl'=2,'z'=8,'core'=2,'y'=8,'xh'=2] {'xl','core','xh'}, dimensions={0} | all-to-all | bytes 128 | tf_op jit(solution)/shard_map/all_to_all | solution.py:445
  47.7 20.2 %all_to_all.13 = f32[64,1,2]{2,1,0:T(1,128)S(1)} all-to-all(f32[64,1,2]{2,1,0:T(1,128)S(1)} %broadcast_in_dim.5), channel_id=1, replica_groups=mesh['xl'=2,'z'=8,'core'=2,'y'=8,'xh'=2] {'z','y'}, dimensions={0} | all-to-all | bytes 1024 | tf_op jit(solution)/shard_map/all_to_all | solution.py:445
  67.9 0.1 reduce_sum.19
  68.0 0.5 multiply_sqrt_fusion
  (4 shorter events, 0.1 us)
Async XLA Ops:
  2.0 6.6 %collective-permute-start = (f32[32,128]{1,0:T(8,128)S(1)}, f32[32,128]{1,0:T(8,128)S(1)}, u32[]{:S(2)}, u32[]{:S(2)}) collective-permute-start(f32[32,128]{1,0:T(8,128)S(1)} %get-tuple-element.26), channel_id=1, source_target_pairs={{0,1},{1,0},{2,3},{3,2},{4,5},{5,4},{6,7},{7,6},{8,9},{9,8},{10,11... | collective-permute-start | bytes 49160 | tf_op jit(solution)/shard_map/ppermute | solution.py:458
  8.7 8.3 %collective-permute-start.1 = (f32[10,8,128]{2,1,0:T(8,128)S(1)}, f32[10,8,128]{2,1,0:T(8,128)S(1)}, u32[]{:S(2)}, u32[]{:S(2)}) collective-permute-start(f32[10,8,128]{2,1,0:T(8,128)S(1)} %get-tuple-element.27), channel_id=1, source_target_pairs={{0,2},{2,0},{4,6},{6,4},{8,10},{10,8},{12,14},{14,12},{1,3},{3,1},... | collective-permute-start | bytes 122888 | tf_op jit(solution)/shard_map/ppermute | solution.py:437
  12.1 6.3 %collective-permute-start.2 = (f32[10,8,128]{2,1,0:T(8,128)S(1)}, f32[10,8,128]{2,1,0:T(8,128)S(1)}, u32[]{:S(2)}, u32[]{:S(2)}) collective-permute-start(f32[10,8,128]{2,1,0:T(8,128)S(1)} %get-tuple-element.28), channel_id=1, source_target_pairs={{0,14},{2,4},{4,2},{6,8},{8,6},{10,12},{12,10},{14,0},{1,15},{3,5}... | collective-permute-start | bytes 122888 | tf_op jit(solution)/shard_map/ppermute | solution.py:436
  18.7 11.7 %collective-permute-start.3 = (f32[5,40,128]{2,1,0:T(8,128)S(1)}, f32[5,40,128]{2,1,0:T(8,128)S(1)}, u32[]{:S(2)}, u32[]{:S(2)}) collective-permute-start(f32[5,40,128]{2,1,0:T(8,128)S(1)} %get-tuple-element.31), channel_id=1, source_target_pairs={{0,16},{16,0},{32,48},{48,32},{64,80},{80,64},{96,112},{112,96},{1... | collective-permute-start | bytes 307208 | tf_op jit(solution)/shard_map/ppermute | solution.py:437
  27.4 6.0 %collective-permute-start.4 = (f32[5,40,128]{2,1,0:T(8,128)S(1)}, f32[5,40,128]{2,1,0:T(8,128)S(1)}, u32[]{:S(2)}, u32[]{:S(2)}) collective-permute-start(f32[5,40,128]{2,1,0:T(8,128)S(1)} %get-tuple-element.32), channel_id=1, source_target_pairs={{0,496},{16,32},{32,16},{48,64},{64,48},{80,96},{96,80},{112,128},... | collective-permute-start | bytes 307208 | tf_op jit(solution)/shard_map/ppermute | solution.py:436

commit v6 on v5

--- a/solution.py
+++ b/solution.py
@@ -228,7 +228,7 @@
 
 
 def x_faces(
-    u_ref, f_ref, p_ref, columns_ref, first_y_ref, second_y_ref,
+    u_ref, f_ref, p_ref, columns_ref, second_y_ref, first_y_ref,
     halo_ref, columns_out, first_ref, second_ref, below_s, above_s,
 ):
     even = is_even(GY)
@@ -336,7 +336,7 @@
 
 
 def late(
-    u_ref, f_ref, p_ref, halo_ref, columns_ref, first_x_ref, second_x_ref,
+    u_ref, f_ref, p_ref, halo_ref, columns_ref, second_x_ref, first_x_ref,
     dual_ref, bar_ref, primal_ref, dual_end, primal_end, gathered_ref, early_sums,
     u_out, p_out, sums_out,
 ):
@@ -466,7 +466,7 @@
         6,
         (shape(5, OWN, 8, LANES), shape(ALL_ROWS, LANES), message, message),
         [pltpu.VMEM((10, 8, LANES), jnp.float32)] * 2,
-    )(u, f, p, columns, first_y, second_y)
+    )(u, f, p, columns, second_y, first_y)
     first, second = trade(first, second, GX)
 
     planes = shape(OWN, ALL_ROWS, LANES)
@@ -484,7 +484,7 @@
         late,
         14,
         (shape(OWN, ROWS, LANES), shape(3, OWN, ROWS, LANES), shape(8, LANES)),
-    )(u, f, p, halo, columns, first, second, *done)
+    )(u, f, p, halo, columns, second, first, *done)
     cells = OWN * lax.axis_size(GX) * ROWS * lax.axis_size(GY) * LANES * lax.axis_size(GZ)
     return denoised, dual, jnp.sqrt(settle(sums) / float(cells))
 

time: 68.8 us -> 64.5 us (0.938)
  blocking collectives: 33.1 us -> 28 us
  starting transfers between devices: 24.4 us -> 26.6 us
  waiting for transfers between devices: 5.39 us -> 3.93 us
    ppermute x2, starting transfers between devices: 6.79 us -> 12.4 us  [trade(): second = lax.ppermute(second, axes, outer)]
    all_to_all x2, blocking collectives: 33.1 us -> 28 us  [settle(): lax.all_to_all(spread, axes, 0, 0, tiled=True)]
    ppermute x2, waiting for transfers between devices: 4.27 us -> 0.01 us  [trade(): second = lax.ppermute(second, axes, outer)]
    ppermute x2, starting transfers between devices: 12.1 us -> 8.68 us  [trade(): first = lax.ppermute(first, axes, [(i, i ^ 1) for i in range(count)])]
    ppermute x2, waiting for transfers between devices: 0.01 us -> 2.81 us  [trade(): first = lax.ppermute(first, axes, [(i, i ^ 1) for i in range(count)])]
  transfers between devices with their start and end apart: 5 -> 5, of which waited for: 3 -> 2; matrix products, arithmetic and copies ran while one was open for 0% -> 0% of each run, Pallas kernels for 2% -> 2%
where the time goes in v6:
time: 64.5 us; the launch traced here: 64.2 us
  blocking collectives  28 us (43%)
  starting transfers between devices  26.6 us (41%)
  Pallas kernels  4.25 us (7%)
  waiting for transfers between devices  3.93 us (6%)
  between operations  0.72 us (1%)
    all_to_all x2, blocking collectives, settle(): lax.all_to_all(spread, axes, 0, 0, tiled=True)  28 us
    ppermute x2, starting transfers between devices, trade(): second = lax.ppermute(second, axes, outer)  12.4 us
    ppermute x2, starting transfers between devices, trade(): first = lax.ppermute(first, axes, [(i, i ^ 1) for i in range(count)])  8.68 us
    ppermute x1, starting transfers between devices, on_device(): columns = lax.ppermute(columns, GZ, [(0, 1), (1, 0)])  5.48 us
    ppermute x2, waiting for transfers between devices, trade(): first = lax.ppermute(first, axes, [(i, i ^ 1) for i in range(count)])  2.81 us
    pallas_call x1, Pallas kernels, on_device(): call(load, 3, (shape(ROWS, LANES), shape(*u.shape), shape(*f.shape), shap...  1.4 us
    pallas_call x1, Pallas kernels, on_device(): call(late, 14, (shape(OWN, ROWS, LANES), shape(3, OWN, ROWS, LANES), shap...  1.31 us
  transfers between devices with their start and end apart: 5, of which 2 were waited for; matrix products, arithmetic and copies ran while one was open for 0% of the time, Pallas kernels for 2%

profile of v6, /device:TPU:1, one launch (start us, length us, event | category | flops | bytes accessed | tf_op | source)
XLA Modules:
  0.0 64.2 jit_solution(4261443898679627738)
XLA Ops:
  0.6 1.4 %shard_map.58 = (f32[32,128]{1,0:T(8,128)S(1)}, f32[8,32,128]{2,1,0:T(8,128)S(1)}, f32[8,32,128]{2,1,0:T(8,128)S(1)}, f32[3,8,32,128]{3,2,1,0:T(8,128)S(1)}) custom-call(f32[8,32,128]{2,1,0:T(8,128)} %u_ref.1, f32[8,32,128]{2,1,0:T(8,128)} %f_ref.1, f32[3,8,32,128]{3,2,1,0:T(8,128)} %p_ref.1), custom_call_target="tpu_custom_call" | custom-call | tf_op jit(solution)/shard_map/pallas_call | solution.py:451
  2.0 5.5 %collective-permute-start = (f32[32,128]{1,0:T(8,128)S(1)}, f32[32,128]{1,0:T(8,128)S(1)}, u32[]{:S(2)}, u32[]{:S(2)}) collective-permute-start(f32[32,128]{1,0:T(8,128)S(1)} %get-tuple-element.26), channel_id=1, source_target_pairs={{0,1},{1,0},{2,3},{3,2},{4,5},{5,4},{6,7},{7,6},{8,9},{9,8},{10,11... | collective-permute-start | bytes 49160 | tf_op jit(solution)/shard_map/ppermute | solution.py:458
  7.5 1.1 %collective-permute-done.columns_ref = f32[32,128]{1,0:T(8,128)S(1)} collective-permute-done((f32[32,128]{1,0:T(8,128)S(1)}, f32[32,128]{1,0:T(8,128)S(1)}, u32[]{:S(2)}, u32[]{:S(2)}) %collective-permute-start) | collective-permute-done | bytes 16416 | tf_op jit(solution)/shard_map/ppermute | solution.py:458
  8.6 0.1 shard_map.59
  8.7 5.3 %collective-permute-start.1 = (f32[10,8,128]{2,1,0:T(8,128)S(1)}, f32[10,8,128]{2,1,0:T(8,128)S(1)}, u32[]{:S(2)}, u32[]{:S(2)}) collective-permute-start(f32[10,8,128]{2,1,0:T(8,128)S(1)} %get-tuple-element.27), channel_id=1, source_target_pairs={{0,14},{2,4},{4,2},{6,8},{8,6},{10,12},{12,10},{14,0},{1,15},{3,5}... | collective-permute-start | bytes 122888 | tf_op jit(solution)/shard_map/ppermute | solution.py:436
  14.0 1.9 %collective-permute-start.2 = (f32[10,8,128]{2,1,0:T(8,128)S(1)}, f32[10,8,128]{2,1,0:T(8,128)S(1)}, u32[]{:S(2)}, u32[]{:S(2)}) collective-permute-start(f32[10,8,128]{2,1,0:T(8,128)S(1)} %get-tuple-element.28), channel_id=1, source_target_pairs={{0,2},{2,0},{4,6},{6,4},{8,10},{10,8},{12,14},{14,12},{1,3},{3,1},... | collective-permute-start | bytes 122888 | tf_op jit(solution)/shard_map/ppermute | solution.py:437
  16.0 0.0 collective-permute-done.1.second_y_ref
  16.0 2.8 %collective-permute-done.2.first_y_ref = f32[10,8,128]{2,1,0:T(8,128)S(1)} collective-permute-done((f32[10,8,128]{2,1,0:T(8,128)S(1)}, f32[10,8,128]{2,1,0:T(8,128)S(1)}, u32[]{:S(2)}, u32[]{:S(2)}) %collective-permute-start.2) | collective-permute-done | bytes 40992 | tf_op jit(solution)/shard_map/ppermute | solution.py:437
  18.8 0.3 shard_map.60
  19.1 7.1 %collective-permute-start.3 = (f32[5,40,128]{2,1,0:T(8,128)S(1)}, f32[5,40,128]{2,1,0:T(8,128)S(1)}, u32[]{:S(2)}, u32[]{:S(2)}) collective-permute-start(f32[5,40,128]{2,1,0:T(8,128)S(1)} %get-tuple-element.31), channel_id=1, source_target_pairs={{0,496},{16,32},{32,16},{48,64},{64,48},{80,96},{96,80},{112,128},... | collective-permute-start | bytes 307208 | tf_op jit(solution)/shard_map/ppermute | solution.py:436
  26.3 6.8 %collective-permute-start.4 = (f32[5,40,128]{2,1,0:T(8,128)S(1)}, f32[5,40,128]{2,1,0:T(8,128)S(1)}, u32[]{:S(2)}, u32[]{:S(2)}) collective-permute-start(f32[5,40,128]{2,1,0:T(8,128)S(1)} %get-tuple-element.32), channel_id=1, source_target_pairs={{0,16},{16,0},{32,48},{48,32},{64,80},{80,64},{96,112},{112,96},{1... | collective-permute-start | bytes 307208 | tf_op jit(solution)/shard_map/ppermute | solution.py:437
  33.0 1.1 %shard_map.61 = (f32[3,8,40,128]{3,2,1,0:T(8,128)S(1)}, f32[8,40,128]{2,1,0:T(8,128)S(1)}, f32[8,40,128]{2,1,0:T(8,128)S(1)}, f32[3,8,40,128]{3,2,1,0:T(8,128)S(...) custom-call(f32[8,32,128]{2,1,0:T(8,128)S(1)} %get-tuple-element.23.u_ref, ...), custom_call_target="tpu_custom_call" | custom-call | flops 1000000 | bytes 1000000 | tf_op jit(solution)/shard_map/pallas_call | solution.py:474
  34.2 0.0 collective-permute-done.3.second_x_ref
  34.2 0.0 collective-permute-done.4.first_x_ref
  34.2 1.3 %shard_map.62 = (f32[8,32,128]{2,1,0:T(8,128)}, f32[3,8,32,128]{3,2,1,0:T(8,128)}, f32[8,128]{1,0:T(8,128)S(1)}) custom-call(f32[8,32,128]{2,1,0:T(8,128)S(1)} %get-tuple-element.23.u_ref, f32[8,32,128]{2,1,0:T(8,128)S(1)} %get-tuple-element.24.f_ref, f32[3,8,32,128]{3,2,1,0:T(8,128)S(1)} %get-tuple-element.25.p_ref, ...), custom_call_target="tpu_custom_call" | custom-call | tf_op jit(solution)/shard_map/pallas_call | solution.py:483
  35.5 8.5 %all_to_all.12 = f32[8,1,2]{2,1,0:T(1,128)S(1)} all-to-all(f32[8,1,2]{2,1,0:T(1,128)S(1)} %broadcast_in_dim.4), channel_id=1, replica_groups=mesh['xl'=2,'z'=8,'core'=2,'y'=8,'xh'=2] {'xl','core','xh'}, dimensions={0} | all-to-all | bytes 128 | tf_op jit(solution)/shard_map/all_to_all | solution.py:445
  44.1 19.5 %all_to_all.13 = f32[64,1,2]{2,1,0:T(1,128)S(1)} all-to-all(f32[64,1,2]{2,1,0:T(1,128)S(1)} %broadcast_in_dim.5), channel_id=1, replica_groups=mesh['xl'=2,'z'=8,'core'=2,'y'=8,'xh'=2] {'z','y'}, dimensions={0} | all-to-all | bytes 1024 | tf_op jit(solution)/shard_map/all_to_all | solution.py:445
  63.6 0.1 reduce_sum.19
  63.7 0.5 multiply_sqrt_fusion
  (4 shorter events, 0.1 us)
Async XLA Ops:
  2.0 6.6 %collective-permute-start = (f32[32,128]{1,0:T(8,128)S(1)}, f32[32,128]{1,0:T(8,128)S(1)}, u32[]{:S(2)}, u32[]{:S(2)}) collective-permute-start(f32[32,128]{1,0:T(8,128)S(1)} %get-tuple-element.26), channel_id=1, source_target_pairs={{0,1},{1,0},{2,3},{3,2},{4,5},{5,4},{6,7},{7,6},{8,9},{9,8},{10,11... | collective-permute-start | bytes 49160 | tf_op jit(solution)/shard_map/ppermute | solution.py:458
  8.7 7.3 %collective-permute-start.1 = (f32[10,8,128]{2,1,0:T(8,128)S(1)}, f32[10,8,128]{2,1,0:T(8,128)S(1)}, u32[]{:S(2)}, u32[]{:S(2)}) collective-permute-start(f32[10,8,128]{2,1,0:T(8,128)S(1)} %get-tuple-element.27), channel_id=1, source_target_pairs={{0,14},{2,4},{4,2},{6,8},{8,6},{10,12},{12,10},{14,0},{1,15},{3,5}... | collective-permute-start | bytes 122888 | tf_op jit(solution)/shard_map/ppermute | solution.py:436
  14.0 4.7 %collective-permute-start.2 = (f32[10,8,128]{2,1,0:T(8,128)S(1)}, f32[10,8,128]{2,1,0:T(8,128)S(1)}, u32[]{:S(2)}, u32[]{:S(2)}) collective-permute-start(f32[10,8,128]{2,1,0:T(8,128)S(1)} %get-tuple-element.28), channel_id=1, source_target_pairs={{0,2},{2,0},{4,6},{6,4},{8,10},{10,8},{12,14},{14,12},{1,3},{3,1},... | collective-permute-start | bytes 122888 | tf_op jit(solution)/shard_map/ppermute | solution.py:437
  19.1 15.0 %collective-permute-start.3 = (f32[5,40,128]{2,1,0:T(8,128)S(1)}, f32[5,40,128]{2,1,0:T(8,128)S(1)}, u32[]{:S(2)}, u32[]{:S(2)}) collective-permute-start(f32[5,40,128]{2,1,0:T(8,128)S(1)} %get-tuple-element.31), channel_id=1, source_target_pairs={{0,496},{16,32},{32,16},{48,64},{64,48},{80,96},{96,80},{112,128},... | collective-permute-start | bytes 307208 | tf_op jit(solution)/shard_map/ppermute | solution.py:436
  26.3 7.9 %collective-permute-start.4 = (f32[5,40,128]{2,1,0:T(8,128)S(1)}, f32[5,40,128]{2,1,0:T(8,128)S(1)}, u32[]{:S(2)}, u32[]{:S(2)}) collective-permute-start(f32[5,40,128]{2,1,0:T(8,128)S(1)} %get-tuple-element.32), channel_id=1, source_target_pairs={{0,16},{16,0},{32,48},{48,32},{64,80},{80,64},{96,112},{112,96},{1... | collective-permute-start | bytes 307208 | tf_op jit(solution)/shard_map/ppermute | solution.py:437

commit v7 on v6

--- a/solution.py
+++ b/solution.py
@@ -60,20 +60,16 @@
 
 
 def load(u_ref, f_ref, p_ref, out_ref, u_vmem, f_vmem, p_vmem, sem):
-    copies = [
-        pltpu.make_async_copy(source, target, sem.at[k])
-        for k, (source, target) in enumerate(
-            ((u_ref, u_vmem), (f_ref, f_vmem), (p_ref, p_vmem))
-        )
-    ]
+    sources = fields(u_ref, p_ref, f_ref)
+    targets = fields(u_vmem, p_vmem, f_vmem)
+    copies = [pltpu.make_async_copy(a, b, sem.at[k]) for k, (a, b) in enumerate(zip(sources, targets))]
     for copy in copies:
         copy.start()
-    for copy in copies:
-        copy.wait()
     first = 1 - lax.axis_index(GZ)
     pair = lanes_of(ROWS) >> 1
     columns = jnp.zeros((ROWS, LANES), jnp.float32)
-    for g, field in enumerate(fields(u_vmem, p_vmem, f_vmem)):
+    for g, (copy, field) in enumerate(zip(copies, targets)):
+        copy.wait()
         for x in range(OWN):
             lane = g * GROUP + lane_of(x)
             moved = pltpu.roll(field[x], lane + 2 * first, 1)
@@ -96,7 +92,7 @@
     up += [f_ref[:, ROWS - 1, :], columns_ref[ROWS - 8 :, :]]
     down = {0: u_ref[:, 0, :], 1: u_ref[:, 1, :], 8: f_ref[:, 0, :], 9: columns_ref[:8, :]}
     down |= {2 + d: p_ref[d, :, 0, :] for d in range(3)}
-    even = is_even(GY)
+    even = is_even(GY) == (lax.axis_index("core") == 0)
     for k, tile in enumerate(up):
         first_ref[k], second_ref[k] = sort_out(even, tile, down.get(k, tile))
 
@@ -231,7 +227,7 @@
     u_ref, f_ref, p_ref, columns_ref, second_y_ref, first_y_ref,
     halo_ref, columns_out, first_ref, second_ref, below_s, above_s,
 ):
-    even = is_even(GY)
+    even = is_even(GY) == (lax.axis_index("core") == 0)
     for k in range(10):
         above_s[k], below_s[k] = sort_out(even, first_y_ref[k], second_y_ref[k])
     for field in range(5):
@@ -430,6 +426,21 @@
     )
 
 
+def trade_y(first, second):
+    count = lax.axis_size(GY)
+    inner = [i ^ 1 for i in range(count)]
+    outer = [(i + 1 if i % 2 else i - 1) % count for i in range(count)]
+
+    def pairs(on_first, on_second):
+        return [(i, j) for i, j in enumerate(on_first)] + [
+            (count + i, count + j) for i, j in enumerate(on_second)
+        ]
+
+    second = lax.ppermute(second, ("core", GY), pairs(outer, inner))
+    first = lax.ppermute(first, ("core", GY), pairs(inner, outer))
+    return first, second
+
+
 def trade(first, second, axes):
     count = lax.axis_size(axes)
     outer = [(i, (i + 1 if i % 2 else i - 1) % count) for i in range(count)]
@@ -438,11 +449,17 @@
     return first, second
 
 
-def settle(values):
-    for axes in (("xl", "core", "xh"), ("z", "y")):
+STAGES = ((("xl", "core", "y", "xh"), ((0 * 2 + 1) * 8 + 4) * 2 + 1), (("z",), 5))
+
+
+def settle(rows):
+    values = rows[:1, :2]
+    for axes, member in STAGES:
         count = lax.axis_size(axes)
-        spread = jnp.broadcast_to(values[:1, :2], (count, 2))
-        values = jnp.sum(lax.all_to_all(spread, axes, 0, 0, tiled=True), axis=0, keepdims=True)
+        order = [member] + [i for i in range(count) if i != member]
+        spread = jnp.broadcast_to(values, (count, 2))
+        spread = lax.all_to_all(spread, axes, 0, 0, tiled=True, axis_index_groups=[order])
+        values = jnp.sum(spread, axis=0, keepdims=True)
     return values[0, :2]
 
 
@@ -452,13 +469,13 @@
         load,
         3,
         (shape(ROWS, LANES), shape(*u.shape), shape(*f.shape), shape(*p.shape)),
-        [pltpu.SemaphoreType.DMA((3,))],
+        [pltpu.SemaphoreType.DMA((5,))],
         [pl.BlockSpec(memory_space=pltpu.HBM)] * 3,
     )(*inputs)
     columns = lax.ppermute(columns, GZ, [(0, 1), (1, 0)])
 
     message = shape(10, 8, LANES)
-    first_y, second_y = trade(*call(y_faces, 4, (message, message))(u, f, p, columns), GY)
+    first_y, second_y = trade_y(*call(y_faces, 4, (message, message))(u, f, p, columns))
 
     message = shape(5, ALL_ROWS, LANES)
     halo, columns, first, second = call(

time: 64.5 us -> 57.5 us (0.89)
  blocking collectives: 28 us -> 20.9 us
  waiting for transfers between devices: 3.93 us -> 2.49 us
  starting transfers between devices: 26.6 us -> 27.7 us
    ppermute x0 -> x2, starting transfers between devices: none -> 8.29 us  [the longest x1 4.87 us: trade_y(): first = lax.ppermute(first, ('core', GY), pairs(inner, outer))]
    all_to_all x2, blocking collectives: 28 us -> 20.9 us  [settle(): lax.all_to_all(spread, axes, 0, 0, tiled=True, axis_index_groups=[order])]
    ppermute x2 -> x1, starting transfers between devices: 12.4 us -> 7.52 us  [trade(): second = lax.ppermute(second, axes, outer)]
    ppermute x2 -> x1, waiting for transfers between devices: 2.81 us -> 0.01 us  [trade(): first = lax.ppermute(first, axes, [(i, i ^ 1) for i in range(count)])]
    ppermute x2 -> x1, starting transfers between devices: 8.68 us -> 6.37 us  [trade(): first = lax.ppermute(first, axes, [(i, i ^ 1) for i in range(count)])]
    ppermute x0 -> x2, waiting for transfers between devices: none -> 1.37 us  [the longest x1 1.37 us: trade_y(): first = lax.ppermute(first, ('core', GY), pairs(inner, outer))]
where the time goes in v7:
time: 57.5 us; the launch traced here: 56.7 us
  starting transfers between devices  27.7 us (48%)
  blocking collectives  20.9 us (36%)
  Pallas kernels  4.31 us (7%)
  waiting for transfers between devices  2.49 us (4%)
  between operations  0.72 us (1%)
  other arithmetic  0.63 us (1%)
    all_to_all x2, blocking collectives, settle(): lax.all_to_all(spread, axes, 0, 0, tiled=True, axis_index_groups=[order])  20.9 us
    ppermute x1, starting transfers between devices, trade(): second = lax.ppermute(second, axes, outer)  7.52 us
    ppermute x1, starting transfers between devices, trade(): first = lax.ppermute(first, axes, [(i, i ^ 1) for i in range(count)])  6.37 us
    ppermute x1, starting transfers between devices, on_device(): columns = lax.ppermute(columns, GZ, [(0, 1), (1, 0)])  5.48 us
    ppermute x1, starting transfers between devices, trade_y(): first = lax.ppermute(first, ('core', GY), pairs(inner, outer))  4.87 us
    ppermute x1, starting transfers between devices, trade_y(): second = lax.ppermute(second, ('core', GY), pairs(outer, inner))  3.42 us
    pallas_call x1, Pallas kernels, on_device(): call(load, 3, (shape(ROWS, LANES), shape(*u.shape), shape(*f.shape), shap...  1.46 us
    ppermute x1, waiting for transfers between devices, trade_y(): first = lax.ppermute(first, ('core', GY), pairs(inner, outer))  1.37 us
  transfers between devices with their start and end apart: 5, of which 2 were waited for; matrix products, arithmetic and copies ran while one was open for 0% of the time, Pallas kernels for 2%

profile of v7, /device:TPU:1, one launch (start us, length us, event | category | flops | bytes accessed | tf_op | source)
XLA Modules:
  0.0 56.7 jit_solution(876277681241186801)
XLA Ops:
  0.6 1.5 %shard_map.58 = (f32[32,128]{1,0:T(8,128)S(1)}, f32[8,32,128]{2,1,0:T(8,128)S(1)}, f32[8,32,128]{2,1,0:T(8,128)S(1)}, f32[3,8,32,128]{3,2,1,0:T(8,128)S(1)}) custom-call(f32[8,32,128]{2,1,0:T(8,128)} %u_ref.1, f32[8,32,128]{2,1,0:T(8,128)} %f_ref.1, f32[3,8,32,128]{3,2,1,0:T(8,128)} %p_ref.1), custom_call_target="tpu_custom_call" | custom-call | tf_op jit(solution)/shard_map/pallas_call | solution.py:468
  2.1 5.5 %collective-permute-start = (f32[32,128]{1,0:T(8,128)S(1)}, f32[32,128]{1,0:T(8,128)S(1)}, u32[]{:S(2)}, u32[]{:S(2)}) collective-permute-start(f32[32,128]{1,0:T(8,128)S(1)} %get-tuple-element.26), channel_id=1, source_target_pairs={{0,1},{1,0},{2,3},{3,2},{4,5},{5,4},{6,7},{7,6},{8,9},{9,8},{10,11... | collective-permute-start | bytes 49160 | tf_op jit(solution)/shard_map/ppermute | solution.py:475
  7.6 1.1 %collective-permute-done.columns_ref = f32[32,128]{1,0:T(8,128)S(1)} collective-permute-done((f32[32,128]{1,0:T(8,128)S(1)}, f32[32,128]{1,0:T(8,128)S(1)}, u32[]{:S(2)}, u32[]{:S(2)}) %collective-permute-start) | collective-permute-done | bytes 16416 | tf_op jit(solution)/shard_map/ppermute | solution.py:475
  8.7 0.1 shard_map.59
  8.8 3.4 %collective-permute-start.1 = (f32[10,8,128]{2,1,0:T(8,128)S(1)}, f32[10,8,128]{2,1,0:T(8,128)S(1)}, u32[]{:S(2)}, u32[]{:S(2)}) collective-permute-start(f32[10,8,128]{2,1,0:T(8,128)S(1)} %get-tuple-element.27), channel_id=1, source_target_pairs={{0,14},{2,4},{4,2},{6,8},{8,6},{10,12},{12,10},{14,0},{16,18},{18,... | collective-permute-start | bytes 122888 | tf_op jit(solution)/shard_map/ppermute | solution.py:439
  12.2 4.9 %collective-permute-start.2 = (f32[10,8,128]{2,1,0:T(8,128)S(1)}, f32[10,8,128]{2,1,0:T(8,128)S(1)}, u32[]{:S(2)}, u32[]{:S(2)}) collective-permute-start(f32[10,8,128]{2,1,0:T(8,128)S(1)} %get-tuple-element.28), channel_id=1, source_target_pairs={{0,2},{2,0},{4,6},{6,4},{8,10},{10,8},{12,14},{14,12},{16,30},{18,... | collective-permute-start | bytes 122888 | tf_op jit(solution)/shard_map/ppermute | solution.py:440
  17.1 0.0 collective-permute-done.1.second_y_ref
  17.1 1.4 %collective-permute-done.2.first_y_ref = f32[10,8,128]{2,1,0:T(8,128)S(1)} collective-permute-done((f32[10,8,128]{2,1,0:T(8,128)S(1)}, f32[10,8,128]{2,1,0:T(8,128)S(1)}, u32[]{:S(2)}, u32[]{:S(2)}) %collective-permute-start.2) | collective-permute-done | bytes 40992 | tf_op jit(solution)/shard_map/ppermute | solution.py:440
  18.4 0.4 shard_map.60
  18.8 7.5 %collective-permute-start.3 = (f32[5,40,128]{2,1,0:T(8,128)S(1)}, f32[5,40,128]{2,1,0:T(8,128)S(1)}, u32[]{:S(2)}, u32[]{:S(2)}) collective-permute-start(f32[5,40,128]{2,1,0:T(8,128)S(1)} %get-tuple-element.31), channel_id=1, source_target_pairs={{0,496},{16,32},{32,16},{48,64},{64,48},{80,96},{96,80},{112,128},... | collective-permute-start | bytes 307208 | tf_op jit(solution)/shard_map/ppermute | solution.py:447
  26.3 6.4 %collective-permute-start.4 = (f32[5,40,128]{2,1,0:T(8,128)S(1)}, f32[5,40,128]{2,1,0:T(8,128)S(1)}, u32[]{:S(2)}, u32[]{:S(2)}) collective-permute-start(f32[5,40,128]{2,1,0:T(8,128)S(1)} %get-tuple-element.32), channel_id=1, source_target_pairs={{0,16},{16,0},{32,48},{48,32},{64,80},{80,64},{96,112},{112,96},{1... | collective-permute-start | bytes 307208 | tf_op jit(solution)/shard_map/ppermute | solution.py:448
  32.7 1.1 %shard_map.61 = (f32[3,8,40,128]{3,2,1,0:T(8,128)S(1)}, f32[8,40,128]{2,1,0:T(8,128)S(1)}, f32[8,40,128]{2,1,0:T(8,128)S(1)}, f32[3,8,40,128]{3,2,1,0:T(8,128)S(...) custom-call(f32[8,32,128]{2,1,0:T(8,128)S(1)} %get-tuple-element.23.u_ref, ...), custom_call_target="tpu_custom_call" | custom-call | flops 1000000 | bytes 1000000 | tf_op jit(solution)/shard_map/pallas_call | solution.py:491
  33.8 0.0 collective-permute-done.3.second_x_ref
  33.9 0.0 collective-permute-done.4.first_x_ref
  33.9 1.3 %shard_map.62 = (f32[8,32,128]{2,1,0:T(8,128)}, f32[3,8,32,128]{3,2,1,0:T(8,128)}, f32[8,128]{1,0:T(8,128)S(1)}) custom-call(f32[8,32,128]{2,1,0:T(8,128)S(1)} %get-tuple-element.23.u_ref, f32[8,32,128]{2,1,0:T(8,128)S(1)} %get-tuple-element.24.f_ref, f32[3,8,32,128]{3,2,1,0:T(8,128)S(1)} %get-tuple-element.25.p_ref, ...), custom_call_target="tpu_custom_call" | custom-call | tf_op jit(solution)/shard_map/pallas_call | solution.py:500
  35.2 12.6 %all_to_all.12 = f32[64,1,2]{2,1,0:T(1,128)S(1)} all-to-all(f32[64,1,2]{2,1,0:T(1,128)S(1)} %broadcast_in_dim.4), channel_id=1, replica_groups={{25,0,1,2,3,4,5,6,7,8,9,10,11,12,13,14,15,16,17,18,19,20,21,22,23,24,26..., dimensions={0} | all-to-all | bytes 1024 | tf_op jit(solution)/shard_map/all_to_all | solution.py:461
  47.8 0.1 reduce_sum.18
  47.9 8.3 %all_to_all.13 = f32[8,1,2]{2,1,0:T(1,128)S(1)} all-to-all(f32[8,1,2]{2,1,0:T(1,128)S(1)} %broadcast_in_dim.5), channel_id=1, replica_groups={{160,0,32,64,96,128,192,224},{161,1,33,65,97,129,193,225},{162,2,34,66,..., dimensions={0} | all-to-all | bytes 128 | tf_op jit(solution)/shard_map/all_to_all | solution.py:461
  56.2 0.5 multiply_sqrt_fusion
  (4 shorter events, 0.1 us)
Async XLA Ops:
  2.1 6.6 %collective-permute-start = (f32[32,128]{1,0:T(8,128)S(1)}, f32[32,128]{1,0:T(8,128)S(1)}, u32[]{:S(2)}, u32[]{:S(2)}) collective-permute-start(f32[32,128]{1,0:T(8,128)S(1)} %get-tuple-element.26), channel_id=1, source_target_pairs={{0,1},{1,0},{2,3},{3,2},{4,5},{5,4},{6,7},{7,6},{8,9},{9,8},{10,11... | collective-permute-start | bytes 49160 | tf_op jit(solution)/shard_map/ppermute | solution.py:475
  8.8 8.3 %collective-permute-start.1 = (f32[10,8,128]{2,1,0:T(8,128)S(1)}, f32[10,8,128]{2,1,0:T(8,128)S(1)}, u32[]{:S(2)}, u32[]{:S(2)}) collective-permute-start(f32[10,8,128]{2,1,0:T(8,128)S(1)} %get-tuple-element.27), channel_id=1, source_target_pairs={{0,14},{2,4},{4,2},{6,8},{8,6},{10,12},{12,10},{14,0},{16,18},{18,... | collective-permute-start | bytes 122888 | tf_op jit(solution)/shard_map/ppermute | solution.py:439
  12.2 6.3 %collective-permute-start.2 = (f32[10,8,128]{2,1,0:T(8,128)S(1)}, f32[10,8,128]{2,1,0:T(8,128)S(1)}, u32[]{:S(2)}, u32[]{:S(2)}) collective-permute-start(f32[10,8,128]{2,1,0:T(8,128)S(1)} %get-tuple-element.28), channel_id=1, source_target_pairs={{0,2},{2,0},{4,6},{6,4},{8,10},{10,8},{12,14},{14,12},{16,30},{18,... | collective-permute-start | bytes 122888 | tf_op jit(solution)/shard_map/ppermute | solution.py:440
  18.8 15.0 %collective-permute-start.3 = (f32[5,40,128]{2,1,0:T(8,128)S(1)}, f32[5,40,128]{2,1,0:T(8,128)S(1)}, u32[]{:S(2)}, u32[]{:S(2)}) collective-permute-start(f32[5,40,128]{2,1,0:T(8,128)S(1)} %get-tuple-element.31), channel_id=1, source_target_pairs={{0,496},{16,32},{32,16},{48,64},{64,48},{80,96},{96,80},{112,128},... | collective-permute-start | bytes 307208 | tf_op jit(solution)/shard_map/ppermute | solution.py:447
  26.3 7.5 %collective-permute-start.4 = (f32[5,40,128]{2,1,0:T(8,128)S(1)}, f32[5,40,128]{2,1,0:T(8,128)S(1)}, u32[]{:S(2)}, u32[]{:S(2)}) collective-permute-start(f32[5,40,128]{2,1,0:T(8,128)S(1)} %get-tuple-element.32), channel_id=1, source_target_pairs={{0,16},{16,0},{32,48},{48,32},{64,80},{80,64},{96,112},{112,96},{1... | collective-permute-start | bytes 307208 | tf_op jit(solution)/shard_map/ppermute | solution.py:448

commit v8 on v6

--- a/solution.py
+++ b/solution.py
@@ -60,20 +60,16 @@
 
 
 def load(u_ref, f_ref, p_ref, out_ref, u_vmem, f_vmem, p_vmem, sem):
-    copies = [
-        pltpu.make_async_copy(source, target, sem.at[k])
-        for k, (source, target) in enumerate(
-            ((u_ref, u_vmem), (f_ref, f_vmem), (p_ref, p_vmem))
-        )
-    ]
+    arrays = ((u_ref, u_vmem), (p_ref, p_vmem), (f_ref, f_vmem))
+    copies = [pltpu.make_async_copy(a, b, sem.at[k]) for k, (a, b) in enumerate(arrays)]
     for copy in copies:
         copy.start()
-    for copy in copies:
-        copy.wait()
     first = 1 - lax.axis_index(GZ)
     pair = lanes_of(ROWS) >> 1
     columns = jnp.zeros((ROWS, LANES), jnp.float32)
     for g, field in enumerate(fields(u_vmem, p_vmem, f_vmem)):
+        if g in (0, 1, 4):
+            copies[(g + 1) // 2].wait()
         for x in range(OWN):
             lane = g * GROUP + lane_of(x)
             moved = pltpu.roll(field[x], lane + 2 * first, 1)
@@ -247,7 +243,7 @@
     here = Local()
     plane, dual = plane_of(u_ref, f_ref, p_ref, halo_ref)
     c_u, c_p, c_f = split(columns_out[...])
-    c_moved, c_dual = here.dual_columns(c_p, c_u, gather(lambda x: plane(0, x), range(OWN)))
+    c_moved, c_dual = here.dual_columns(c_p, c_u, gather(lambda x: plane(0, x), (0, 6, 7)))
 
     top = OWN - 1
     u, p = plane(0, top), dual(top)
@@ -438,11 +434,17 @@
     return first, second
 
 
-def settle(values):
-    for axes in (("xl", "core", "xh"), ("z", "y")):
+STAGES = ((("core", "y"), 12), (("xl", "z", "xh"), (0 * 8 + 5) * 2 + 1))
+
+
+def settle(rows):
+    values = rows[:1, :2]
+    for axes, member in STAGES:
         count = lax.axis_size(axes)
-        spread = jnp.broadcast_to(values[:1, :2], (count, 2))
-        values = jnp.sum(lax.all_to_all(spread, axes, 0, 0, tiled=True), axis=0, keepdims=True)
+        order = [member] + [i for i in range(count) if i != member]
+        spread = jnp.broadcast_to(values, (count, 2))
+        spread = lax.all_to_all(spread, axes, 0, 0, tiled=True, axis_index_groups=[order])
+        values = jnp.sum(spread, axis=0, keepdims=True)
     return values[0, :2]
 
 

time: 64.5 us -> 57 us (0.88)
  blocking collectives: 28 us -> 20.1 us
    all_to_all x2, blocking collectives: 28 us -> 20.1 us  [settle(): lax.all_to_all(spread, axes, 0, 0, tiled=True, axis_index_groups=[order])]
where the time goes in v8:
time: 57 us; the launch traced here: 56.1 us
  starting transfers between devices  26.6 us (47%)
  blocking collectives  20.1 us (35%)
  Pallas kernels  4.16 us (7%)
  waiting for transfers between devices  3.93 us (7%)
  between operations  0.73 us (1%)
  other arithmetic  0.61 us (1%)
    all_to_all x2, blocking collectives, settle(): lax.all_to_all(spread, axes, 0, 0, tiled=True, axis_index_groups=[order])  20.1 us
    ppermute x2, starting transfers between devices, trade(): second = lax.ppermute(second, axes, outer)  12.5 us
    ppermute x2, starting transfers between devices, trade(): first = lax.ppermute(first, axes, [(i, i ^ 1) for i in range(count)])  8.68 us
    ppermute x1, starting transfers between devices, on_device(): columns = lax.ppermute(columns, GZ, [(0, 1), (1, 0)])  5.48 us
    ppermute x2, waiting for transfers between devices, trade(): first = lax.ppermute(first, axes, [(i, i ^ 1) for i in range(count)])  2.81 us
    pallas_call x1, Pallas kernels, on_device(): call(load, 3, (shape(ROWS, LANES), shape(*u.shape), shape(*f.shape), shap...  1.36 us
    pallas_call x1, Pallas kernels, on_device(): call(late, 14, (shape(OWN, ROWS, LANES), shape(3, OWN, ROWS, LANES), shap...  1.31 us
  transfers between devices with their start and end apart: 5, of which 2 were waited for; matrix products, arithmetic and copies ran while one was open for 0% of the time, Pallas kernels for 2%

profile of v8, /device:TPU:1, one launch (start us, length us, event | category | flops | bytes accessed | tf_op | source)
XLA Modules:
  0.0 56.1 jit_solution(5213911657437999025)
XLA Ops:
  0.6 1.4 %shard_map.58 = (f32[32,128]{1,0:T(8,128)S(1)}, f32[8,32,128]{2,1,0:T(8,128)S(1)}, f32[8,32,128]{2,1,0:T(8,128)S(1)}, f32[3,8,32,128]{3,2,1,0:T(8,128)S(1)}) custom-call(f32[8,32,128]{2,1,0:T(8,128)} %u_ref.1, f32[8,32,128]{2,1,0:T(8,128)} %f_ref.1, f32[3,8,32,128]{3,2,1,0:T(8,128)} %p_ref.1), custom_call_target="tpu_custom_call" | custom-call | tf_op jit(solution)/shard_map/pallas_call | solution.py:453
  2.0 5.5 %collective-permute-start = (f32[32,128]{1,0:T(8,128)S(1)}, f32[32,128]{1,0:T(8,128)S(1)}, u32[]{:S(2)}, u32[]{:S(2)}) collective-permute-start(f32[32,128]{1,0:T(8,128)S(1)} %get-tuple-element.26), channel_id=1, source_target_pairs={{0,1},{1,0},{2,3},{3,2},{4,5},{5,4},{6,7},{7,6},{8,9},{9,8},{10,11... | collective-permute-start | bytes 49160 | tf_op jit(solution)/shard_map/ppermute | solution.py:460
  7.5 1.1 %collective-permute-done.columns_ref = f32[32,128]{1,0:T(8,128)S(1)} collective-permute-done((f32[32,128]{1,0:T(8,128)S(1)}, f32[32,128]{1,0:T(8,128)S(1)}, u32[]{:S(2)}, u32[]{:S(2)}) %collective-permute-start) | collective-permute-done | bytes 16416 | tf_op jit(solution)/shard_map/ppermute | solution.py:460
  8.6 0.1 shard_map.59
  8.7 5.3 %collective-permute-start.1 = (f32[10,8,128]{2,1,0:T(8,128)S(1)}, f32[10,8,128]{2,1,0:T(8,128)S(1)}, u32[]{:S(2)}, u32[]{:S(2)}) collective-permute-start(f32[10,8,128]{2,1,0:T(8,128)S(1)} %get-tuple-element.27), channel_id=1, source_target_pairs={{0,14},{2,4},{4,2},{6,8},{8,6},{10,12},{12,10},{14,0},{1,15},{3,5}... | collective-permute-start | bytes 122888 | tf_op jit(solution)/shard_map/ppermute | solution.py:432
  14.0 1.9 %collective-permute-start.2 = (f32[10,8,128]{2,1,0:T(8,128)S(1)}, f32[10,8,128]{2,1,0:T(8,128)S(1)}, u32[]{:S(2)}, u32[]{:S(2)}) collective-permute-start(f32[10,8,128]{2,1,0:T(8,128)S(1)} %get-tuple-element.28), channel_id=1, source_target_pairs={{0,2},{2,0},{4,6},{6,4},{8,10},{10,8},{12,14},{14,12},{1,3},{3,1},... | collective-permute-start | bytes 122888 | tf_op jit(solution)/shard_map/ppermute | solution.py:433
  15.9 0.0 collective-permute-done.1.second_y_ref
  15.9 2.8 %collective-permute-done.2.first_y_ref = f32[10,8,128]{2,1,0:T(8,128)S(1)} collective-permute-done((f32[10,8,128]{2,1,0:T(8,128)S(1)}, f32[10,8,128]{2,1,0:T(8,128)S(1)}, u32[]{:S(2)}, u32[]{:S(2)}) %collective-permute-start.2) | collective-permute-done | bytes 40992 | tf_op jit(solution)/shard_map/ppermute | solution.py:433
  18.7 0.3 shard_map.60
  19.0 7.1 %collective-permute-start.3 = (f32[5,40,128]{2,1,0:T(8,128)S(1)}, f32[5,40,128]{2,1,0:T(8,128)S(1)}, u32[]{:S(2)}, u32[]{:S(2)}) collective-permute-start(f32[5,40,128]{2,1,0:T(8,128)S(1)} %get-tuple-element.31), channel_id=1, source_target_pairs={{0,496},{16,32},{32,16},{48,64},{64,48},{80,96},{96,80},{112,128},... | collective-permute-start | bytes 307208 | tf_op jit(solution)/shard_map/ppermute | solution.py:432
  26.2 6.8 %collective-permute-start.4 = (f32[5,40,128]{2,1,0:T(8,128)S(1)}, f32[5,40,128]{2,1,0:T(8,128)S(1)}, u32[]{:S(2)}, u32[]{:S(2)}) collective-permute-start(f32[5,40,128]{2,1,0:T(8,128)S(1)} %get-tuple-element.32), channel_id=1, source_target_pairs={{0,16},{16,0},{32,48},{48,32},{64,80},{80,64},{96,112},{112,96},{1... | collective-permute-start | bytes 307208 | tf_op jit(solution)/shard_map/ppermute | solution.py:433
  33.0 1.1 %shard_map.61 = (f32[3,8,40,128]{3,2,1,0:T(8,128)S(1)}, f32[8,40,128]{2,1,0:T(8,128)S(1)}, f32[8,40,128]{2,1,0:T(8,128)S(1)}, f32[3,8,40,128]{3,2,1,0:T(8,128)S(...) custom-call(f32[8,32,128]{2,1,0:T(8,128)S(1)} %get-tuple-element.23.u_ref, ...), custom_call_target="tpu_custom_call" | custom-call | flops 1000000 | bytes 1000000 | tf_op jit(solution)/shard_map/pallas_call | solution.py:476
  34.1 0.0 collective-permute-done.3.second_x_ref
  34.1 0.0 collective-permute-done.4.first_x_ref
  34.1 1.3 %shard_map.62 = (f32[8,32,128]{2,1,0:T(8,128)}, f32[3,8,32,128]{3,2,1,0:T(8,128)}, f32[8,128]{1,0:T(8,128)S(1)}) custom-call(f32[8,32,128]{2,1,0:T(8,128)S(1)} %get-tuple-element.23.u_ref, f32[8,32,128]{2,1,0:T(8,128)S(1)} %get-tuple-element.24.f_ref, f32[3,8,32,128]{3,2,1,0:T(8,128)S(1)} %get-tuple-element.25.p_ref, ...), custom_call_target="tpu_custom_call" | custom-call | tf_op jit(solution)/shard_map/pallas_call | solution.py:485
  35.4 8.5 %all_to_all.12 = f32[16,1,2]{2,1,0:T(1,128)S(1)} all-to-all(f32[16,1,2]{2,1,0:T(1,128)S(1)} %broadcast_in_dim.4), channel_id=1, replica_groups={{24,0,2,4,6,8,10,12,14,16,18,20,22,26,28,30},{25,1,3,5,7,9,11,13,15,17,..., dimensions={0} | all-to-all | bytes 256 | tf_op jit(solution)/shard_map/all_to_all | solution.py:446
  44.0 11.5 %all_to_all.13 = f32[32,1,2]{2,1,0:T(1,128)S(1)} all-to-all(f32[32,1,2]{2,1,0:T(1,128)S(1)} %broadcast_in_dim.5), channel_id=1, replica_groups={{161,0,1,32,33,64,65,96,97,128,129,160,192,193,224,225,256,257,288,289,..., dimensions={0} | all-to-all | bytes 512 | tf_op jit(solution)/shard_map/all_to_all | solution.py:446
  55.6 0.1 reduce_sum.19
  55.6 0.5 multiply_sqrt_fusion
  (4 shorter events, 0.1 us)
Async XLA Ops:
  2.0 6.6 %collective-permute-start = (f32[32,128]{1,0:T(8,128)S(1)}, f32[32,128]{1,0:T(8,128)S(1)}, u32[]{:S(2)}, u32[]{:S(2)}) collective-permute-start(f32[32,128]{1,0:T(8,128)S(1)} %get-tuple-element.26), channel_id=1, source_target_pairs={{0,1},{1,0},{2,3},{3,2},{4,5},{5,4},{6,7},{7,6},{8,9},{9,8},{10,11... | collective-permute-start | bytes 49160 | tf_op jit(solution)/shard_map/ppermute | solution.py:460
  8.7 7.3 %collective-permute-start.1 = (f32[10,8,128]{2,1,0:T(8,128)S(1)}, f32[10,8,128]{2,1,0:T(8,128)S(1)}, u32[]{:S(2)}, u32[]{:S(2)}) collective-permute-start(f32[10,8,128]{2,1,0:T(8,128)S(1)} %get-tuple-element.27), channel_id=1, source_target_pairs={{0,14},{2,4},{4,2},{6,8},{8,6},{10,12},{12,10},{14,0},{1,15},{3,5}... | collective-permute-start | bytes 122888 | tf_op jit(solution)/shard_map/ppermute | solution.py:432
  14.0 4.7 %collective-permute-start.2 = (f32[10,8,128]{2,1,0:T(8,128)S(1)}, f32[10,8,128]{2,1,0:T(8,128)S(1)}, u32[]{:S(2)}, u32[]{:S(2)}) collective-permute-start(f32[10,8,128]{2,1,0:T(8,128)S(1)} %get-tuple-element.28), channel_id=1, source_target_pairs={{0,2},{2,0},{4,6},{6,4},{8,10},{10,8},{12,14},{14,12},{1,3},{3,1},... | collective-permute-start | bytes 122888 | tf_op jit(solution)/shard_map/ppermute | solution.py:433
  19.0 15.1 %collective-permute-start.3 = (f32[5,40,128]{2,1,0:T(8,128)S(1)}, f32[5,40,128]{2,1,0:T(8,128)S(1)}, u32[]{:S(2)}, u32[]{:S(2)}) collective-permute-start(f32[5,40,128]{2,1,0:T(8,128)S(1)} %get-tuple-element.31), channel_id=1, source_target_pairs={{0,496},{16,32},{32,16},{48,64},{64,48},{80,96},{96,80},{112,128},... | collective-permute-start | bytes 307208 | tf_op jit(solution)/shard_map/ppermute | solution.py:432
  26.2 7.9 %collective-permute-start.4 = (f32[5,40,128]{2,1,0:T(8,128)S(1)}, f32[5,40,128]{2,1,0:T(8,128)S(1)}, u32[]{:S(2)}, u32[]{:S(2)}) collective-permute-start(f32[5,40,128]{2,1,0:T(8,128)S(1)} %get-tuple-element.32), channel_id=1, source_target_pairs={{0,16},{16,0},{32,48},{48,32},{64,80},{80,64},{96,112},{112,96},{1... | collective-permute-start | bytes 307208 | tf_op jit(solution)/shard_map/ppermute | solution.py:433

commit v9 on v8

--- a/solution.py
+++ b/solution.py
@@ -21,6 +21,7 @@
 GROUP = 24
 
 VMEM = pl.BlockSpec(memory_space=pltpu.VMEM)
+HBM = pl.BlockSpec(memory_space=pltpu.HBM)
 
 
 def lanes_of(rows):
@@ -224,7 +225,7 @@
 
 
 def x_faces(
-    u_ref, f_ref, p_ref, columns_ref, second_y_ref, first_y_ref,
+    u_ref, f_ref, p_ref, columns_ref, first_y_ref, second_y_ref,
     halo_ref, columns_out, first_ref, second_ref, below_s, above_s,
 ):
     even = is_even(GY)
@@ -334,8 +335,16 @@
 def late(
     u_ref, f_ref, p_ref, halo_ref, columns_ref, second_x_ref, first_x_ref,
     dual_ref, bar_ref, primal_ref, dual_end, primal_end, gathered_ref, early_sums,
-    u_out, p_out, sums_out,
+    u_out, p_out, sums_out, u_s, p_s, sem,
 ):
+    copies = []
+
+    def write(source, target):
+        copies.append(pltpu.make_async_copy(source, target, sem.at[len(copies)]))
+        copies[-1].start()
+
+    write(dual_end.at[:, 1:6, :ROWS], p_out.at[:, 1:6])
+    write(primal_end.at[2:6], u_out.at[2:6])
     here = Local()
     plane, dual = plane_of(u_ref, f_ref, p_ref, halo_ref)
     even = is_even(GX)
@@ -390,36 +399,39 @@
         gathered = into_columns(gathered, bars[x], x)
     _, c_end = here.dual_columns(c_dual, c_bar, gathered)
     ends = {x: [dual_end[d, x] for d in range(3)] for x in range(1, 6)}
-    for x in (-1, 0, 6, 7):
+    for x in (6, 7, -1, 0):
         ends[x] = here.dual_plane(duals[x], bars[x], bars[x + 1], c_bar, x)
         if x >= 0:
             sums[1] += change_of(ends[x], duals[x]) * (1.0 / STEP_DUAL)
-    for x in range(OWN):
-        if 2 <= x <= 5:
-            u_out[x] = primal_end[x]
-        else:
-            divergence = ends[x][0] - ends[x - 1][0] + here.across(ends[x], c_end[2], x)
-            now = updated(primals[x], plane(4, x), divergence)
-            sums[1] += change_of([now], [primals[x]]) * (1.0 / STEP_PRIMAL)
-            u_out[x] = now[:ROWS]
-        for d in range(3):
-            p_out[d, x] = ends[x][d][:ROWS]
+            for d in range(3):
+                p_s[d, x] = ends[x][d][:ROWS]
+    write(p_s.at[:, 6:8], p_out.at[:, 6:8])
+    write(p_s.at[:, 0:1], p_out.at[:, 0:1])
+    for x in (6, 7, 0, 1):
+        divergence = ends[x][0] - ends[x - 1][0] + here.across(ends[x], c_end[2], x)
+        now = updated(primals[x], plane(4, x), divergence)
+        sums[1] += change_of([now], [primals[x]]) * (1.0 / STEP_PRIMAL)
+        u_s[x] = now[:ROWS]
+    write(u_s.at[6:8], u_out.at[6:8])
+    write(u_s.at[0:2], u_out.at[0:2])
     out_lane = lanes_of(8)
     sums_out[...] = jnp.where(
         out_lane == 0, jnp.sum(sums[0]), jnp.where(out_lane == 1, jnp.sum(sums[1]), 0.0)
     )
+    for copy in copies:
+        copy.wait()
 
 
 def shape(*dims):
     return jax.ShapeDtypeStruct(dims, jnp.float32)
 
 
-def call(kernel, count, outs, scratch=(), specs=None, work=0):
+def call(kernel, count, outs, scratch=(), specs=None, out_specs=None, work=0):
     return pl.pallas_call(
         kernel,
         out_shape=outs,
         in_specs=specs or [VMEM] * count,
-        out_specs=jax.tree.map(lambda _: VMEM, outs),
+        out_specs=out_specs or jax.tree.map(lambda _: VMEM, outs),
         scratch_shapes=list(scratch),
         compiler_params=pltpu.CompilerParams(vmem_limit_bytes=4 * 2**20),
         cost_estimate=pl.CostEstimate(flops=work, bytes_accessed=work, transcendentals=0),
@@ -455,7 +467,7 @@
         3,
         (shape(ROWS, LANES), shape(*u.shape), shape(*f.shape), shape(*p.shape)),
         [pltpu.SemaphoreType.DMA((3,))],
-        [pl.BlockSpec(memory_space=pltpu.HBM)] * 3,
+        [HBM] * 3,
     )(*inputs)
     columns = lax.ppermute(columns, GZ, [(0, 1), (1, 0)])
 
@@ -468,7 +480,7 @@
         6,
         (shape(5, OWN, 8, LANES), shape(ALL_ROWS, LANES), message, message),
         [pltpu.VMEM((10, 8, LANES), jnp.float32)] * 2,
-    )(u, f, p, columns, second_y, first_y)
+    )(u, f, p, columns, first_y, second_y)
     first, second = trade(first, second, GX)
 
     planes = shape(OWN, ALL_ROWS, LANES)
@@ -486,6 +498,12 @@
         late,
         14,
         (shape(OWN, ROWS, LANES), shape(3, OWN, ROWS, LANES), shape(8, LANES)),
+        [
+            pltpu.VMEM((OWN, ROWS, LANES), jnp.float32),
+            pltpu.VMEM((3, OWN, ROWS, LANES), jnp.float32),
+            pltpu.SemaphoreType.DMA((6,)),
+        ],
+        out_specs=(HBM, HBM, VMEM),
     )(u, f, p, halo, columns, second, first, *done)
     cells = OWN * lax.axis_size(GX) * ROWS * lax.axis_size(GY) * LANES * lax.axis_size(GZ)
     return denoised, dual, jnp.sqrt(settle(sums) / float(cells))

time: 57 us -> 56.8 us (level)
  waiting for transfers between devices: 3.93 us -> 2.49 us
  starting transfers between devices: 26.6 us -> 27.7 us
    ppermute x2, waiting for transfers between devices: 2.81 us -> 0.01 us  [trade(): first = lax.ppermute(first, axes, [(i, i ^ 1) for i in range(count)])]
    ppermute x2, starting transfers between devices: 8.68 us -> 10.5 us  [trade(): first = lax.ppermute(first, axes, [(i, i ^ 1) for i in range(count)])]
    ppermute x2, waiting for transfers between devices: 0.01 us -> 1.37 us  [trade(): second = lax.ppermute(second, axes, outer)]
    ppermute x2, starting transfers between devices: 12.5 us -> 11.7 us  [trade(): second = lax.ppermute(second, axes, outer)]
where the time goes in v9:
time: 56.8 us; the launch traced here: 55.9 us
  starting transfers between devices  27.7 us (49%)
  blocking collectives  20.3 us (36%)
  Pallas kernels  4.05 us (7%)
  waiting for transfers between devices  2.49 us (4%)
  between operations  0.75 us (1%)
  other arithmetic  0.61 us (1%)
    all_to_all x2, blocking collectives, settle(): lax.all_to_all(spread, axes, 0, 0, tiled=True, axis_index_groups=[order])  20.3 us
    ppermute x2, starting transfers between devices, trade(): second = lax.ppermute(second, axes, outer)  11.7 us
    ppermute x2, starting transfers between devices, trade(): first = lax.ppermute(first, axes, [(i, i ^ 1) for i in range(count)])  10.5 us
    ppermute x1, starting transfers between devices, on_device(): columns = lax.ppermute(columns, GZ, [(0, 1), (1, 0)])  5.48 us
    ppermute x2, waiting for transfers between devices, trade(): second = lax.ppermute(second, axes, outer)  1.37 us
    pallas_call x1, Pallas kernels, on_device(): call(load, 3, (shape(ROWS, LANES), shape(*u.shape), shape(*f.shape), shap...  1.36 us
    pallas_call x1, Pallas kernels, on_device(): call(late, 14, (shape(OWN, ROWS, LANES), shape(3, OWN, ROWS, LANES), shap...  1.21 us
  transfers between devices with their start and end apart: 5, of which 2 were waited for; matrix products, arithmetic and copies ran while one was open for 0% of the time, Pallas kernels for 2%

profile of v9, /device:TPU:1, one launch (start us, length us, event | category | flops | bytes accessed | tf_op | source)
XLA Modules:
  0.0 55.9 jit_solution(16988122448576428668)
XLA Ops:
  0.6 1.4 %shard_map.58 = (f32[32,128]{1,0:T(8,128)S(1)}, f32[8,32,128]{2,1,0:T(8,128)S(1)}, f32[8,32,128]{2,1,0:T(8,128)S(1)}, f32[3,8,32,128]{3,2,1,0:T(8,128)S(1)}) custom-call(f32[8,32,128]{2,1,0:T(8,128)} %u_ref.1, f32[8,32,128]{2,1,0:T(8,128)} %f_ref.1, f32[3,8,32,128]{3,2,1,0:T(8,128)} %p_ref.1), custom_call_target="tpu_custom_call" | custom-call | tf_op jit(solution)/shard_map/pallas_call | solution.py:465
  2.0 5.5 %collective-permute-start = (f32[32,128]{1,0:T(8,128)S(1)}, f32[32,128]{1,0:T(8,128)S(1)}, u32[]{:S(2)}, u32[]{:S(2)}) collective-permute-start(f32[32,128]{1,0:T(8,128)S(1)} %get-tuple-element.26), channel_id=1, source_target_pairs={{0,1},{1,0},{2,3},{3,2},{4,5},{5,4},{6,7},{7,6},{8,9},{9,8},{10,11... | collective-permute-start | bytes 49160 | tf_op jit(solution)/shard_map/ppermute | solution.py:472
  7.5 1.1 %collective-permute-done.columns_ref = f32[32,128]{1,0:T(8,128)S(1)} collective-permute-done((f32[32,128]{1,0:T(8,128)S(1)}, f32[32,128]{1,0:T(8,128)S(1)}, u32[]{:S(2)}, u32[]{:S(2)}) %collective-permute-start) | collective-permute-done | bytes 16416 | tf_op jit(solution)/shard_map/ppermute | solution.py:472
  8.6 0.1 shard_map.59
  8.7 3.4 %collective-permute-start.1 = (f32[10,8,128]{2,1,0:T(8,128)S(1)}, f32[10,8,128]{2,1,0:T(8,128)S(1)}, u32[]{:S(2)}, u32[]{:S(2)}) collective-permute-start(f32[10,8,128]{2,1,0:T(8,128)S(1)} %get-tuple-element.27), channel_id=1, source_target_pairs={{0,2},{2,0},{4,6},{6,4},{8,10},{10,8},{12,14},{14,12},{1,3},{3,1},... | collective-permute-start | bytes 122888 | tf_op jit(solution)/shard_map/ppermute | solution.py:445
  12.1 4.9 %collective-permute-start.2 = (f32[10,8,128]{2,1,0:T(8,128)S(1)}, f32[10,8,128]{2,1,0:T(8,128)S(1)}, u32[]{:S(2)}, u32[]{:S(2)}) collective-permute-start(f32[10,8,128]{2,1,0:T(8,128)S(1)} %get-tuple-element.28), channel_id=1, source_target_pairs={{0,14},{2,4},{4,2},{6,8},{8,6},{10,12},{12,10},{14,0},{1,15},{3,5}... | collective-permute-start | bytes 122888 | tf_op jit(solution)/shard_map/ppermute | solution.py:444
  17.0 0.0 collective-permute-done.1.first_y_ref
  17.0 1.4 %collective-permute-done.2.second_y_ref = f32[10,8,128]{2,1,0:T(8,128)S(1)} collective-permute-done((f32[10,8,128]{2,1,0:T(8,128)S(1)}, f32[10,8,128]{2,1,0:T(8,128)S(1)}, u32[]{:S(2)}, u32[]{:S(2)}) %collective-permute-start.2) | collective-permute-done | bytes 40992 | tf_op jit(solution)/shard_map/ppermute | solution.py:444
  18.4 0.3 shard_map.60
  18.7 6.9 %collective-permute-start.3 = (f32[5,40,128]{2,1,0:T(8,128)S(1)}, f32[5,40,128]{2,1,0:T(8,128)S(1)}, u32[]{:S(2)}, u32[]{:S(2)}) collective-permute-start(f32[5,40,128]{2,1,0:T(8,128)S(1)} %get-tuple-element.31), channel_id=1, source_target_pairs={{0,496},{16,32},{32,16},{48,64},{64,48},{80,96},{96,80},{112,128},... | collective-permute-start | bytes 307208 | tf_op jit(solution)/shard_map/ppermute | solution.py:444
  25.5 7.0 %collective-permute-start.4 = (f32[5,40,128]{2,1,0:T(8,128)S(1)}, f32[5,40,128]{2,1,0:T(8,128)S(1)}, u32[]{:S(2)}, u32[]{:S(2)}) collective-permute-start(f32[5,40,128]{2,1,0:T(8,128)S(1)} %get-tuple-element.32), channel_id=1, source_target_pairs={{0,16},{16,0},{32,48},{48,32},{64,80},{80,64},{96,112},{112,96},{1... | collective-permute-start | bytes 307208 | tf_op jit(solution)/shard_map/ppermute | solution.py:445
  32.6 1.1 %shard_map.61 = (f32[3,8,40,128]{3,2,1,0:T(8,128)S(1)}, f32[8,40,128]{2,1,0:T(8,128)S(1)}, f32[8,40,128]{2,1,0:T(8,128)S(1)}, f32[3,8,40,128]{3,2,1,0:T(8,128)S(...) custom-call(f32[8,32,128]{2,1,0:T(8,128)S(1)} %get-tuple-element.23.u_ref, ...), custom_call_target="tpu_custom_call" | custom-call | flops 1000000 | bytes 1000000 | tf_op jit(solution)/shard_map/pallas_call | solution.py:488
  33.7 0.0 collective-permute-done.3.second_x_ref
  33.7 0.0 collective-permute-done.4.first_x_ref
  33.7 1.2 %shard_map.62 = (f32[8,32,128]{2,1,0:T(8,128)}, f32[3,8,32,128]{3,2,1,0:T(8,128)}, f32[8,128]{1,0:T(8,128)S(1)}) custom-call(f32[8,32,128]{2,1,0:T(8,128)S(1)} %get-tuple-element.23.u_ref, f32[8,32,128]{2,1,0:T(8,128)S(1)} %get-tuple-element.24.f_ref, f32[3,8,32,128]{3,2,1,0:T(8,128)S(1)} %get-tuple-element.25.p_ref, ...), custom_call_target="tpu_custom_call" | custom-call | tf_op jit(solution)/shard_map/pallas_call | solution.py:497
  35.0 8.8 %all_to_all.12 = f32[16,1,2]{2,1,0:T(1,128)S(1)} all-to-all(f32[16,1,2]{2,1,0:T(1,128)S(1)} %broadcast_in_dim.4), channel_id=1, replica_groups={{24,0,2,4,6,8,10,12,14,16,18,20,22,26,28,30},{25,1,3,5,7,9,11,13,15,17,..., dimensions={0} | all-to-all | bytes 256 | tf_op jit(solution)/shard_map/all_to_all | solution.py:458
  43.8 11.5 %all_to_all.13 = f32[32,1,2]{2,1,0:T(1,128)S(1)} all-to-all(f32[32,1,2]{2,1,0:T(1,128)S(1)} %broadcast_in_dim.5), channel_id=1, replica_groups={{161,0,1,32,33,64,65,96,97,128,129,160,192,193,224,225,256,257,288,289,..., dimensions={0} | all-to-all | bytes 512 | tf_op jit(solution)/shard_map/all_to_all | solution.py:458
  55.4 0.1 reduce_sum.19
  55.4 0.5 multiply_sqrt_fusion
  (4 shorter events, 0.1 us)
Async XLA Ops:
  2.0 6.6 %collective-permute-start = (f32[32,128]{1,0:T(8,128)S(1)}, f32[32,128]{1,0:T(8,128)S(1)}, u32[]{:S(2)}, u32[]{:S(2)}) collective-permute-start(f32[32,128]{1,0:T(8,128)S(1)} %get-tuple-element.26), channel_id=1, source_target_pairs={{0,1},{1,0},{2,3},{3,2},{4,5},{5,4},{6,7},{7,6},{8,9},{9,8},{10,11... | collective-permute-start | bytes 49160 | tf_op jit(solution)/shard_map/ppermute | solution.py:472
  8.7 8.3 %collective-permute-start.1 = (f32[10,8,128]{2,1,0:T(8,128)S(1)}, f32[10,8,128]{2,1,0:T(8,128)S(1)}, u32[]{:S(2)}, u32[]{:S(2)}) collective-permute-start(f32[10,8,128]{2,1,0:T(8,128)S(1)} %get-tuple-element.27), channel_id=1, source_target_pairs={{0,2},{2,0},{4,6},{6,4},{8,10},{10,8},{12,14},{14,12},{1,3},{3,1},... | collective-permute-start | bytes 122888 | tf_op jit(solution)/shard_map/ppermute | solution.py:445
  12.1 6.3 %collective-permute-start.2 = (f32[10,8,128]{2,1,0:T(8,128)S(1)}, f32[10,8,128]{2,1,0:T(8,128)S(1)}, u32[]{:S(2)}, u32[]{:S(2)}) collective-permute-start(f32[10,8,128]{2,1,0:T(8,128)S(1)} %get-tuple-element.28), channel_id=1, source_target_pairs={{0,14},{2,4},{4,2},{6,8},{8,6},{10,12},{12,10},{14,0},{1,15},{3,5}... | collective-permute-start | bytes 122888 | tf_op jit(solution)/shard_map/ppermute | solution.py:444
  18.7 15.1 %collective-permute-start.3 = (f32[5,40,128]{2,1,0:T(8,128)S(1)}, f32[5,40,128]{2,1,0:T(8,128)S(1)}, u32[]{:S(2)}, u32[]{:S(2)}) collective-permute-start(f32[5,40,128]{2,1,0:T(8,128)S(1)} %get-tuple-element.31), channel_id=1, source_target_pairs={{0,496},{16,32},{32,16},{48,64},{64,48},{80,96},{96,80},{112,128},... | collective-permute-start | bytes 307208 | tf_op jit(solution)/shard_map/ppermute | solution.py:444
  25.5 8.2 %collective-permute-start.4 = (f32[5,40,128]{2,1,0:T(8,128)S(1)}, f32[5,40,128]{2,1,0:T(8,128)S(1)}, u32[]{:S(2)}, u32[]{:S(2)}) collective-permute-start(f32[5,40,128]{2,1,0:T(8,128)S(1)} %get-tuple-element.32), channel_id=1, source_target_pairs={{0,16},{16,0},{32,48},{48,32},{64,80},{80,64},{96,112},{112,96},{1... | collective-permute-start | bytes 307208 | tf_op jit(solution)/shard_map/ppermute | solution.py:445

commit v10 on v8

--- a/solution.py
+++ b/solution.py
@@ -404,10 +404,9 @@
             u_out[x] = now[:ROWS]
         for d in range(3):
             p_out[d, x] = ends[x][d][:ROWS]
-    out_lane = lanes_of(8)
-    sums_out[...] = jnp.where(
-        out_lane == 0, jnp.sum(sums[0]), jnp.where(out_lane == 1, jnp.sum(sums[1]), 0.0)
-    )
+    for k in range(2):
+        total = jnp.sum(sums[k], axis=0, keepdims=True)
+        sums_out[:, k * LANES : (k + 1) * LANES] = jnp.broadcast_to(total, (8, LANES))
 
 
 def shape(*dims):
@@ -438,14 +437,14 @@
 
 
 def settle(rows):
-    values = rows[:1, :2]
+    values = rows[:1]
     for axes, member in STAGES:
         count = lax.axis_size(axes)
         order = [member] + [i for i in range(count) if i != member]
-        spread = jnp.broadcast_to(values, (count, 2))
+        spread = jnp.broadcast_to(values, (count, 2 * LANES))
         spread = lax.all_to_all(spread, axes, 0, 0, tiled=True, axis_index_groups=[order])
         values = jnp.sum(spread, axis=0, keepdims=True)
-    return values[0, :2]
+    return jnp.sum(values.reshape(2, LANES), axis=1)
 
 
 def on_device(f, u, p):
@@ -485,7 +484,7 @@
     denoised, dual, sums = call(
         late,
         14,
-        (shape(OWN, ROWS, LANES), shape(3, OWN, ROWS, LANES), shape(8, LANES)),
+        (shape(OWN, ROWS, LANES), shape(3, OWN, ROWS, LANES), shape(8, 2 * LANES)),
     )(u, f, p, halo, columns, second, first, *done)
     cells = OWN * lax.axis_size(GX) * ROWS * lax.axis_size(GY) * LANES * lax.axis_size(GZ)
     return denoised, dual, jnp.sqrt(settle(sums) / float(cells))

time: 57 us -> 57.4 us (level)
  blocking collectives: 20.1 us -> 20.9 us
    all_to_all x2, blocking collectives: 20.1 us -> 20.9 us  [settle(): lax.all_to_all(spread, axes, 0, 0, tiled=True, axis_index_groups=[order])]
where the time goes in v10:
time: 57.4 us; the launch traced here: 57.1 us
  starting transfers between devices  26.6 us (46%)
  blocking collectives  20.9 us (36%)
  Pallas kernels  4.11 us (7%)
  waiting for transfers between devices  3.93 us (7%)
  other arithmetic  0.73 us (1%)
  between operations  0.73 us (1%)
    all_to_all x2, blocking collectives, settle(): lax.all_to_all(spread, axes, 0, 0, tiled=True, axis_index_groups=[order])  20.9 us
    ppermute x2, starting transfers between devices, trade(): second = lax.ppermute(second, axes, outer)  12.5 us
    ppermute x2, starting transfers between devices, trade(): first = lax.ppermute(first, axes, [(i, i ^ 1) for i in range(count)])  8.68 us
    ppermute x1, starting transfers between devices, on_device(): columns = lax.ppermute(columns, GZ, [(0, 1), (1, 0)])  5.48 us
    ppermute x2, waiting for transfers between devices, trade(): first = lax.ppermute(first, axes, [(i, i ^ 1) for i in range(count)])  2.81 us
    pallas_call x1, Pallas kernels, on_device(): call(load, 3, (shape(ROWS, LANES), shape(*u.shape), shape(*f.shape), shap...  1.36 us
    pallas_call x1, Pallas kernels, on_device(): call(late, 14, (shape(OWN, ROWS, LANES), shape(3, OWN, ROWS, LANES), shap...  1.26 us
  transfers between devices with their start and end apart: 5, of which 2 were waited for; matrix products, arithmetic and copies ran while one was open for 0% of the time, Pallas kernels for 2%

profile of v10, /device:TPU:1, one launch (start us, length us, event | category | flops | bytes accessed | tf_op | source)
XLA Modules:
  0.0 57.1 jit_solution(14771085621836273237)
XLA Ops:
  0.6 1.4 %shard_map.58 = (f32[32,128]{1,0:T(8,128)S(1)}, f32[8,32,128]{2,1,0:T(8,128)S(1)}, f32[8,32,128]{2,1,0:T(8,128)S(1)}, f32[3,8,32,128]{3,2,1,0:T(8,128)S(1)}) custom-call(f32[8,32,128]{2,1,0:T(8,128)} %u_ref.1, f32[8,32,128]{2,1,0:T(8,128)} %f_ref.1, f32[3,8,32,128]{3,2,1,0:T(8,128)} %p_ref.1), custom_call_target="tpu_custom_call" | custom-call | tf_op jit(solution)/shard_map/pallas_call | solution.py:452
  2.0 5.5 %collective-permute-start = (f32[32,128]{1,0:T(8,128)S(1)}, f32[32,128]{1,0:T(8,128)S(1)}, u32[]{:S(2)}, u32[]{:S(2)}) collective-permute-start(f32[32,128]{1,0:T(8,128)S(1)} %get-tuple-element.26), channel_id=1, source_target_pairs={{0,1},{1,0},{2,3},{3,2},{4,5},{5,4},{6,7},{7,6},{8,9},{9,8},{10,11... | collective-permute-start | bytes 49160 | tf_op jit(solution)/shard_map/ppermute | solution.py:459
  7.5 1.1 %collective-permute-done.columns_ref = f32[32,128]{1,0:T(8,128)S(1)} collective-permute-done((f32[32,128]{1,0:T(8,128)S(1)}, f32[32,128]{1,0:T(8,128)S(1)}, u32[]{:S(2)}, u32[]{:S(2)}) %collective-permute-start) | collective-permute-done | bytes 16416 | tf_op jit(solution)/shard_map/ppermute | solution.py:459
  8.6 0.1 shard_map.59
  8.7 5.3 %collective-permute-start.1 = (f32[10,8,128]{2,1,0:T(8,128)S(1)}, f32[10,8,128]{2,1,0:T(8,128)S(1)}, u32[]{:S(2)}, u32[]{:S(2)}) collective-permute-start(f32[10,8,128]{2,1,0:T(8,128)S(1)} %get-tuple-element.27), channel_id=1, source_target_pairs={{0,14},{2,4},{4,2},{6,8},{8,6},{10,12},{12,10},{14,0},{1,15},{3,5}... | collective-permute-start | bytes 122888 | tf_op jit(solution)/shard_map/ppermute | solution.py:431
  14.0 1.9 %collective-permute-start.2 = (f32[10,8,128]{2,1,0:T(8,128)S(1)}, f32[10,8,128]{2,1,0:T(8,128)S(1)}, u32[]{:S(2)}, u32[]{:S(2)}) collective-permute-start(f32[10,8,128]{2,1,0:T(8,128)S(1)} %get-tuple-element.28), channel_id=1, source_target_pairs={{0,2},{2,0},{4,6},{6,4},{8,10},{10,8},{12,14},{14,12},{1,3},{3,1},... | collective-permute-start | bytes 122888 | tf_op jit(solution)/shard_map/ppermute | solution.py:432
  15.9 0.0 collective-permute-done.1.second_y_ref
  15.9 2.8 %collective-permute-done.2.first_y_ref = f32[10,8,128]{2,1,0:T(8,128)S(1)} collective-permute-done((f32[10,8,128]{2,1,0:T(8,128)S(1)}, f32[10,8,128]{2,1,0:T(8,128)S(1)}, u32[]{:S(2)}, u32[]{:S(2)}) %collective-permute-start.2) | collective-permute-done | bytes 40992 | tf_op jit(solution)/shard_map/ppermute | solution.py:432
  18.7 0.3 shard_map.60
  19.0 7.1 %collective-permute-start.3 = (f32[5,40,128]{2,1,0:T(8,128)S(1)}, f32[5,40,128]{2,1,0:T(8,128)S(1)}, u32[]{:S(2)}, u32[]{:S(2)}) collective-permute-start(f32[5,40,128]{2,1,0:T(8,128)S(1)} %get-tuple-element.31), channel_id=1, source_target_pairs={{0,496},{16,32},{32,16},{48,64},{64,48},{80,96},{96,80},{112,128},... | collective-permute-start | bytes 307208 | tf_op jit(solution)/shard_map/ppermute | solution.py:431
  26.2 6.8 %collective-permute-start.4 = (f32[5,40,128]{2,1,0:T(8,128)S(1)}, f32[5,40,128]{2,1,0:T(8,128)S(1)}, u32[]{:S(2)}, u32[]{:S(2)}) collective-permute-start(f32[5,40,128]{2,1,0:T(8,128)S(1)} %get-tuple-element.32), channel_id=1, source_target_pairs={{0,16},{16,0},{32,48},{48,32},{64,80},{80,64},{96,112},{112,96},{1... | collective-permute-start | bytes 307208 | tf_op jit(solution)/shard_map/ppermute | solution.py:432
  33.0 1.1 %shard_map.61 = (f32[3,8,40,128]{3,2,1,0:T(8,128)S(1)}, f32[8,40,128]{2,1,0:T(8,128)S(1)}, f32[8,40,128]{2,1,0:T(8,128)S(1)}, f32[3,8,40,128]{3,2,1,0:T(8,128)S(...) custom-call(f32[8,32,128]{2,1,0:T(8,128)S(1)} %get-tuple-element.23.u_ref, ...), custom_call_target="tpu_custom_call" | custom-call | flops 1000000 | bytes 1000000 | tf_op jit(solution)/shard_map/pallas_call | solution.py:475
  34.1 0.0 collective-permute-done.3.second_x_ref
  34.1 0.0 collective-permute-done.4.first_x_ref
  34.1 1.3 %shard_map.62 = (f32[8,32,128]{2,1,0:T(8,128)}, f32[3,8,32,128]{3,2,1,0:T(8,128)}, f32[8,256]{1,0:T(8,128)S(1)}) custom-call(f32[8,32,128]{2,1,0:T(8,128)S(1)} %get-tuple-element.23.u_ref, f32[8,32,128]{2,1,0:T(8,128)S(1)} %get-tuple-element.24.f_ref, f32[3,8,32,128]{3,2,1,0:T(8,128)S(1)} %get-tuple-element.25.p_ref, ...), custom_call_target="tpu_custom_call" | custom-call | tf_op jit(solution)/shard_map/pallas_call | solution.py:484
  35.4 8.9 %all_to_all.12 = f32[16,1,256]{2,1,0:T(1,128)S(1)} all-to-all(f32[16,1,256]{2,1,0:T(1,128)S(1)} %broadcast_in_dim.4), channel_id=1, replica_groups={{24,0,2,4,6,8,10,12,14,16,18,20,22,26,28,30},{25,1,3,5,7,9,11,13,15,17,..., dimensions={0} | all-to-all | bytes 32768 | tf_op jit(solution)/shard_map/all_to_all | solution.py:445
  44.3 12.0 %all_to_all.13 = f32[32,1,256]{2,1,0:T(1,128)S(1)} all-to-all(f32[32,1,256]{2,1,0:T(1,128)S(1)} %broadcast_in_dim.5), channel_id=1, replica_groups={{161,0,1,32,33,64,65,96,97,128,129,160,192,193,224,225,256,257,288,289,..., dimensions={0} | all-to-all | bytes 65536 | tf_op jit(solution)/shard_map/all_to_all | solution.py:445
  56.4 0.1 reduce_sum.28
  56.4 0.1 bitcast_reduce_fusion
  56.5 0.5 multiply_sqrt_fusion
  (4 shorter events, 0.1 us)
Async XLA Ops:
  2.0 6.6 %collective-permute-start = (f32[32,128]{1,0:T(8,128)S(1)}, f32[32,128]{1,0:T(8,128)S(1)}, u32[]{:S(2)}, u32[]{:S(2)}) collective-permute-start(f32[32,128]{1,0:T(8,128)S(1)} %get-tuple-element.26), channel_id=1, source_target_pairs={{0,1},{1,0},{2,3},{3,2},{4,5},{5,4},{6,7},{7,6},{8,9},{9,8},{10,11... | collective-permute-start | bytes 49160 | tf_op jit(solution)/shard_map/ppermute | solution.py:459
  8.7 7.3 %collective-permute-start.1 = (f32[10,8,128]{2,1,0:T(8,128)S(1)}, f32[10,8,128]{2,1,0:T(8,128)S(1)}, u32[]{:S(2)}, u32[]{:S(2)}) collective-permute-start(f32[10,8,128]{2,1,0:T(8,128)S(1)} %get-tuple-element.27), channel_id=1, source_target_pairs={{0,14},{2,4},{4,2},{6,8},{8,6},{10,12},{12,10},{14,0},{1,15},{3,5}... | collective-permute-start | bytes 122888 | tf_op jit(solution)/shard_map/ppermute | solution.py:431
  14.0 4.7 %collective-permute-start.2 = (f32[10,8,128]{2,1,0:T(8,128)S(1)}, f32[10,8,128]{2,1,0:T(8,128)S(1)}, u32[]{:S(2)}, u32[]{:S(2)}) collective-permute-start(f32[10,8,128]{2,1,0:T(8,128)S(1)} %get-tuple-element.28), channel_id=1, source_target_pairs={{0,2},{2,0},{4,6},{6,4},{8,10},{10,8},{12,14},{14,12},{1,3},{3,1},... | collective-permute-start | bytes 122888 | tf_op jit(solution)/shard_map/ppermute | solution.py:432
  19.0 15.1 %collective-permute-start.3 = (f32[5,40,128]{2,1,0:T(8,128)S(1)}, f32[5,40,128]{2,1,0:T(8,128)S(1)}, u32[]{:S(2)}, u32[]{:S(2)}) collective-permute-start(f32[5,40,128]{2,1,0:T(8,128)S(1)} %get-tuple-element.31), channel_id=1, source_target_pairs={{0,496},{16,32},{32,16},{48,64},{64,48},{80,96},{96,80},{112,128},... | collective-permute-start | bytes 307208 | tf_op jit(solution)/shard_map/ppermute | solution.py:431
  26.2 7.9 %collective-permute-start.4 = (f32[5,40,128]{2,1,0:T(8,128)S(1)}, f32[5,40,128]{2,1,0:T(8,128)S(1)}, u32[]{:S(2)}, u32[]{:S(2)}) collective-permute-start(f32[5,40,128]{2,1,0:T(8,128)S(1)} %get-tuple-element.32), channel_id=1, source_target_pairs={{0,16},{16,0},{32,48},{48,32},{64,80},{80,64},{96,112},{112,96},{1... | collective-permute-start | bytes 307208 | tf_op jit(solution)/shard_map/ppermute | solution.py:432

commit v11 on v8

--- a/solution.py
+++ b/solution.py
@@ -223,19 +223,23 @@
     return into
 
 
+def lay_out(first_ref, second_ref, halo_ref, below_s, above_s, planes):
+    even = is_even(GY)
+    for k in range(10):
+        above_s[k], below_s[k] = sort_out(even, first_ref[k], second_ref[k])
+    for field in range(5):
+        for x in planes:
+            halo_ref[field, x] = jnp.zeros((8, LANES), jnp.float32)
+            for row, from_below, tile in HALO_ROWS[field]:
+                source = below_s if from_below else above_s
+                halo_ref[field, x, row : row + 1, :] = source[tile, x : x + 1, :]
+
+
 def x_faces(
     u_ref, f_ref, p_ref, columns_ref, second_y_ref, first_y_ref,
     halo_ref, columns_out, first_ref, second_ref, below_s, above_s,
 ):
-    even = is_even(GY)
-    for k in range(10):
-        above_s[k], below_s[k] = sort_out(even, first_y_ref[k], second_y_ref[k])
-    for field in range(5):
-        for x in range(OWN):
-            halo_ref[field, x] = jnp.zeros((8, LANES), jnp.float32)
-            for row, from_below, tile in HALO_ROWS[field]:
-                source = below_s if from_below else above_s
-                halo_ref[field, x, row : row + 1, :] = source[tile, x : x + 1, :]
+    lay_out(first_y_ref, second_y_ref, halo_ref, below_s, above_s, (0, 1, 6, 7))
     row = rows_of(8)
     columns_out[:ROWS, :] = columns_ref[...]
     columns_out[ROWS:, :] = jnp.where(row >= 6, below_s[9], jnp.where(row < 2, above_s[9], 0.0))
@@ -279,9 +283,11 @@
 
 
 def early(
-    u_ref, f_ref, p_ref, halo_ref, columns_ref,
+    u_ref, f_ref, p_ref, columns_ref, first_y_ref, second_y_ref,
     dual_out, bar_out, primal_out, dual_end, primal_end, gathered_out, sums_out,
+    halo_ref, below_s, above_s,
 ):
+    lay_out(first_y_ref, second_y_ref, halo_ref, below_s, above_s, range(OWN))
     here = Local()
     plane, dual = plane_of(u_ref, f_ref, p_ref, halo_ref)
     c_u, c_p, c_f = split(columns_ref[...])
@@ -475,13 +481,15 @@
     triple = shape(3, OWN, ALL_ROWS, LANES)
     done = call(
         early,
-        5,
+        6,
         (
             triple, planes, planes, triple, shape(OWN, ROWS, LANES),
             shape(3, ALL_ROWS, LANES), shape(2, 8, LANES),
         ),
+        [pltpu.VMEM((5, OWN, 8, LANES), jnp.float32)]
+        + [pltpu.VMEM((10, 8, LANES), jnp.float32)] * 2,
         work=10**6,
-    )(u, f, p, halo, columns)
+    )(u, f, p, columns, first_y, second_y)
     denoised, dual, sums = call(
         late,
         14,

time: 57 us -> 57 us (level)
  no operation moved by 1% of the time
where the time goes in v11:
time: 57 us; the launch traced here: 56.1 us
  starting transfers between devices  26.6 us (47%)
  blocking collectives  20.1 us (35%)
  Pallas kernels  4.16 us (7%)
  waiting for transfers between devices  3.93 us (7%)
  between operations  0.73 us (1%)
  other arithmetic  0.61 us (1%)
    all_to_all x2, blocking collectives, settle(): lax.all_to_all(spread, axes, 0, 0, tiled=True, axis_index_groups=[order])  20.1 us
    ppermute x2, starting transfers between devices, trade(): second = lax.ppermute(second, axes, outer)  12.5 us
    ppermute x2, starting transfers between devices, trade(): first = lax.ppermute(first, axes, [(i, i ^ 1) for i in range(count)])  8.68 us
    ppermute x1, starting transfers between devices, on_device(): columns = lax.ppermute(columns, GZ, [(0, 1), (1, 0)])  5.48 us
    ppermute x2, waiting for transfers between devices, trade(): first = lax.ppermute(first, axes, [(i, i ^ 1) for i in range(count)])  2.81 us
    pallas_call x1, Pallas kernels, on_device(): call(load, 3, (shape(ROWS, LANES), shape(*u.shape), shape(*f.shape), shap...  1.36 us
    pallas_call x1, Pallas kernels, on_device(): call(late, 14, (shape(OWN, ROWS, LANES), shape(3, OWN, ROWS, LANES), shap...  1.31 us
  transfers between devices with their start and end apart: 5, of which 2 were waited for; matrix products, arithmetic and copies ran while one was open for 0% of the time, Pallas kernels for 2%

profile of v11, /device:TPU:1, one launch (start us, length us, event | category | flops | bytes accessed | tf_op | source)
XLA Modules:
  0.0 56.1 jit_solution(8441257818100366039)
XLA Ops:
  0.6 1.4 %shard_map.58 = (f32[32,128]{1,0:T(8,128)S(1)}, f32[8,32,128]{2,1,0:T(8,128)S(1)}, f32[8,32,128]{2,1,0:T(8,128)S(1)}, f32[3,8,32,128]{3,2,1,0:T(8,128)S(1)}) custom-call(f32[8,32,128]{2,1,0:T(8,128)} %u_ref.1, f32[8,32,128]{2,1,0:T(8,128)} %f_ref.1, f32[3,8,32,128]{3,2,1,0:T(8,128)} %p_ref.1), custom_call_target="tpu_custom_call" | custom-call | tf_op jit(solution)/shard_map/pallas_call | solution.py:459
  2.0 5.5 %collective-permute-start = (f32[32,128]{1,0:T(8,128)S(1)}, f32[32,128]{1,0:T(8,128)S(1)}, u32[]{:S(2)}, u32[]{:S(2)}) collective-permute-start(f32[32,128]{1,0:T(8,128)S(1)} %get-tuple-element.26), channel_id=1, source_target_pairs={{0,1},{1,0},{2,3},{3,2},{4,5},{5,4},{6,7},{7,6},{8,9},{9,8},{10,11... | collective-permute-start | bytes 49160 | tf_op jit(solution)/shard_map/ppermute | solution.py:466
  7.5 1.1 %collective-permute-done.columns_ref = f32[32,128]{1,0:T(8,128)S(1)} collective-permute-done((f32[32,128]{1,0:T(8,128)S(1)}, f32[32,128]{1,0:T(8,128)S(1)}, u32[]{:S(2)}, u32[]{:S(2)}) %collective-permute-start) | collective-permute-done | bytes 16416 | tf_op jit(solution)/shard_map/ppermute | solution.py:466
  8.6 0.1 shard_map.59
  8.7 5.3 %collective-permute-start.1 = (f32[10,8,128]{2,1,0:T(8,128)S(1)}, f32[10,8,128]{2,1,0:T(8,128)S(1)}, u32[]{:S(2)}, u32[]{:S(2)}) collective-permute-start(f32[10,8,128]{2,1,0:T(8,128)S(1)} %get-tuple-element.27), channel_id=1, source_target_pairs={{0,14},{2,4},{4,2},{6,8},{8,6},{10,12},{12,10},{14,0},{1,15},{3,5}... | collective-permute-start | bytes 122888 | tf_op jit(solution)/shard_map/ppermute | solution.py:438
  14.0 1.9 %collective-permute-start.2 = (f32[10,8,128]{2,1,0:T(8,128)S(1)}, f32[10,8,128]{2,1,0:T(8,128)S(1)}, u32[]{:S(2)}, u32[]{:S(2)}) collective-permute-start(f32[10,8,128]{2,1,0:T(8,128)S(1)} %get-tuple-element.28), channel_id=1, source_target_pairs={{0,2},{2,0},{4,6},{6,4},{8,10},{10,8},{12,14},{14,12},{1,3},{3,1},... | collective-permute-start | bytes 122888 | tf_op jit(solution)/shard_map/ppermute | solution.py:439
  15.9 0.0 collective-permute-done.1.second_y_ref
  15.9 2.8 %collective-permute-done.2.first_y_ref = f32[10,8,128]{2,1,0:T(8,128)S(1)} collective-permute-done((f32[10,8,128]{2,1,0:T(8,128)S(1)}, f32[10,8,128]{2,1,0:T(8,128)S(1)}, u32[]{:S(2)}, u32[]{:S(2)}) %collective-permute-start.2) | collective-permute-done | bytes 40992 | tf_op jit(solution)/shard_map/ppermute | solution.py:439
  18.7 0.3 shard_map.60
  19.0 7.1 %collective-permute-start.3 = (f32[5,40,128]{2,1,0:T(8,128)S(1)}, f32[5,40,128]{2,1,0:T(8,128)S(1)}, u32[]{:S(2)}, u32[]{:S(2)}) collective-permute-start(f32[5,40,128]{2,1,0:T(8,128)S(1)} %get-tuple-element.31), channel_id=1, source_target_pairs={{0,496},{16,32},{32,16},{48,64},{64,48},{80,96},{96,80},{112,128},... | collective-permute-start | bytes 307208 | tf_op jit(solution)/shard_map/ppermute | solution.py:438
  26.2 6.8 %collective-permute-start.4 = (f32[5,40,128]{2,1,0:T(8,128)S(1)}, f32[5,40,128]{2,1,0:T(8,128)S(1)}, u32[]{:S(2)}, u32[]{:S(2)}) collective-permute-start(f32[5,40,128]{2,1,0:T(8,128)S(1)} %get-tuple-element.32), channel_id=1, source_target_pairs={{0,16},{16,0},{32,48},{48,32},{64,80},{80,64},{96,112},{112,96},{1... | collective-permute-start | bytes 307208 | tf_op jit(solution)/shard_map/ppermute | solution.py:439
  32.9 1.1 %shard_map.61 = (f32[3,8,40,128]{3,2,1,0:T(8,128)S(1)}, f32[8,40,128]{2,1,0:T(8,128)S(1)}, f32[8,40,128]{2,1,0:T(8,128)S(1)}, f32[3,8,40,128]{3,2,1,0:T(8,128)S(...) custom-call(f32[8,32,128]{2,1,0:T(8,128)S(1)} %get-tuple-element.23.u_ref, ...), custom_call_target="tpu_custom_call" | custom-call | flops 1000000 | bytes 1000000 | tf_op jit(solution)/shard_map/pallas_call | solution.py:482
  34.1 0.0 collective-permute-done.3.second_x_ref
  34.1 0.0 collective-permute-done.4.first_x_ref
  34.1 1.3 %shard_map.62 = (f32[8,32,128]{2,1,0:T(8,128)}, f32[3,8,32,128]{3,2,1,0:T(8,128)}, f32[8,128]{1,0:T(8,128)S(1)}) custom-call(f32[8,32,128]{2,1,0:T(8,128)S(1)} %get-tuple-element.23.u_ref, f32[8,32,128]{2,1,0:T(8,128)S(1)} %get-tuple-element.24.f_ref, f32[3,8,32,128]{3,2,1,0:T(8,128)S(1)} %get-tuple-element.25.p_ref, ...), custom_call_target="tpu_custom_call" | custom-call | tf_op jit(solution)/shard_map/pallas_call | solution.py:493
  35.4 8.5 %all_to_all.12 = f32[16,1,2]{2,1,0:T(1,128)S(1)} all-to-all(f32[16,1,2]{2,1,0:T(1,128)S(1)} %broadcast_in_dim.4), channel_id=1, replica_groups={{24,0,2,4,6,8,10,12,14,16,18,20,22,26,28,30},{25,1,3,5,7,9,11,13,15,17,..., dimensions={0} | all-to-all | bytes 256 | tf_op jit(solution)/shard_map/all_to_all | solution.py:452
  44.0 11.5 %all_to_all.13 = f32[32,1,2]{2,1,0:T(1,128)S(1)} all-to-all(f32[32,1,2]{2,1,0:T(1,128)S(1)} %broadcast_in_dim.5), channel_id=1, replica_groups={{161,0,1,32,33,64,65,96,97,128,129,160,192,193,224,225,256,257,288,289,..., dimensions={0} | all-to-all | bytes 512 | tf_op jit(solution)/shard_map/all_to_all | solution.py:452
  55.6 0.1 reduce_sum.19
  55.6 0.5 multiply_sqrt_fusion
  (4 shorter events, 0.1 us)
Async XLA Ops:
  2.0 6.6 %collective-permute-start = (f32[32,128]{1,0:T(8,128)S(1)}, f32[32,128]{1,0:T(8,128)S(1)}, u32[]{:S(2)}, u32[]{:S(2)}) collective-permute-start(f32[32,128]{1,0:T(8,128)S(1)} %get-tuple-element.26), channel_id=1, source_target_pairs={{0,1},{1,0},{2,3},{3,2},{4,5},{5,4},{6,7},{7,6},{8,9},{9,8},{10,11... | collective-permute-start | bytes 49160 | tf_op jit(solution)/shard_map/ppermute | solution.py:466
  8.7 7.3 %collective-permute-start.1 = (f32[10,8,128]{2,1,0:T(8,128)S(1)}, f32[10,8,128]{2,1,0:T(8,128)S(1)}, u32[]{:S(2)}, u32[]{:S(2)}) collective-permute-start(f32[10,8,128]{2,1,0:T(8,128)S(1)} %get-tuple-element.27), channel_id=1, source_target_pairs={{0,14},{2,4},{4,2},{6,8},{8,6},{10,12},{12,10},{14,0},{1,15},{3,5}... | collective-permute-start | bytes 122888 | tf_op jit(solution)/shard_map/ppermute | solution.py:438
  14.0 4.7 %collective-permute-start.2 = (f32[10,8,128]{2,1,0:T(8,128)S(1)}, f32[10,8,128]{2,1,0:T(8,128)S(1)}, u32[]{:S(2)}, u32[]{:S(2)}) collective-permute-start(f32[10,8,128]{2,1,0:T(8,128)S(1)} %get-tuple-element.28), channel_id=1, source_target_pairs={{0,2},{2,0},{4,6},{6,4},{8,10},{10,8},{12,14},{14,12},{1,3},{3,1},... | collective-permute-start | bytes 122888 | tf_op jit(solution)/shard_map/ppermute | solution.py:439
  19.0 15.1 %collective-permute-start.3 = (f32[5,40,128]{2,1,0:T(8,128)S(1)}, f32[5,40,128]{2,1,0:T(8,128)S(1)}, u32[]{:S(2)}, u32[]{:S(2)}) collective-permute-start(f32[5,40,128]{2,1,0:T(8,128)S(1)} %get-tuple-element.31), channel_id=1, source_target_pairs={{0,496},{16,32},{32,16},{48,64},{64,48},{80,96},{96,80},{112,128},... | collective-permute-start | bytes 307208 | tf_op jit(solution)/shard_map/ppermute | solution.py:438
  26.2 7.9 %collective-permute-start.4 = (f32[5,40,128]{2,1,0:T(8,128)S(1)}, f32[5,40,128]{2,1,0:T(8,128)S(1)}, u32[]{:S(2)}, u32[]{:S(2)}) collective-permute-start(f32[5,40,128]{2,1,0:T(8,128)S(1)} %get-tuple-element.32), channel_id=1, source_target_pairs={{0,16},{16,0},{32,48},{48,32},{64,80},{80,64},{96,112},{112,96},{1... | collective-permute-start | bytes 307208 | tf_op jit(solution)/shard_map/ppermute | solution.py:439
